TPU v7x, 32 devices: a whole 2x2x4 slice. The times are simulated.
32 devices in a mesh: gx: 4 (over y, core), gy: 4 (over z), gz: 2 (over x).
Axes of the slice: x: 2, y: 2, z: 4, core: 2. Of those that a mesh axis runs over, the one named last changes fastest.
Arguments:
- panels: bfloat16 [4, 4, 16, 32, 1024], P(None, None, 'gz', 'gy', 'gx'), may hold values from -6 to 6
- eof_basis: bfloat16 [4, 16, 10], replicated, may hold values from -1.5 to 1.5
- control: float32 [4, 10, 32, 1024], P(None, None, 'gy', ('gx', 'gz')), may hold values from -6 to 6
- coefficients: float32 [4, 32, 1024], P(None, 'gy', ('gx', 'gz')), may hold values from -0.5 to 1.6, as said below
Outputs:
- covariance_image: float32 [4, 10, 32, 1024], P(None, None, 'gy', ('gx', 'gz'))
Inputs may be any that keep to these rules, and one draw needn't show every extreme that they name: `coefficients`: kxx and kyy lie in 0.2 to 1, kxy = c sqrt(kxx kyy) with c in -0.5 to 0.5, and the inverse cell area lies in 0.6 to 1.6.
All inputs are finite; a program needn't handle non-finite values.
Results may differ from a plain program's by a relative error of at most 0.00085.
Values may be sent and summed in bfloat16 or wider, within the bound.
No kernel may reach another device: no remote copies, remote signals or barrier semaphores. Data moves between devices by JAX's collectives and lax.ppermute only.
A program may use at most 64 MiB of HBM per device.

v0:
```python
import jax
import jax.numpy as jnp
from jax import lax
from jax.sharding import PartitionSpec as P

STEPS = 6


time_step = 0.09


def padded_2(cells, sides, width, closed):
    for axis, dim in sides:
        count = lax.axis_size(axis)
        ends = count if closed else count - 1
        head = lax.slice_in_dim(cells, 0, width, axis=dim)
        tail = lax.slice_in_dim(cells, cells.shape[dim] - width, cells.shape[dim], axis=dim)
        cells = jnp.concatenate(
            [
                lax.ppermute(tail, axis, [(i, (i + 1) % count) for i in range(ends)]),
                cells,
                lax.ppermute(head, axis, [((i + 1) % count, i) for i in range(ends)]),
            ],
            axis=dim,
        )
    return cells


def divergence(padded, coeffs):
    east_diff = padded[:, :-1, 1:] - padded[:, :-1, :-1]
    north_diff = padded[:, 1:, :-1] - padded[:, :-1, :-1]
    flux_east = coeffs[0, :-1, :-1] * east_diff + coeffs[1, :-1, :-1] * north_diff
    flux_north = coeffs[1, :-1, :-1] * east_diff + coeffs[2, :-1, :-1] * north_diff
    return (
        flux_east[:, 1:, 1:]
        - flux_east[:, 1:, :-1]
        + (flux_north[:, 1:, 1:] - flux_north[:, :-1, 1:])
    )


def forward_section(padded, coeffs):
    return padded[:, 1:-1, 1:-1] + time_step * coeffs[3, 1:-1, 1:-1] * divergence(padded, coeffs)


def adjoint_section(padded, coeffs):
    return padded[:, 1:-1, 1:-1] + time_step * divergence(coeffs[3] * padded, coeffs)


def extend(values, width):
    zonal_wide = padded_2(values, ((("gx", "gz"), 2),), width, True)
    return padded_2(zonal_wide, (("gy", 1),), width, False)


def diffuse(values, coeff_wide, halo_depth, section_fn):
    for outer_turn in range(STEPS // halo_depth):
        padded = extend(values, halo_depth)
        padded = section_fn(padded, coeff_wide)
        values = padded
    return values


def per_device(panels, eof_basis, control, coefficients):
    halo_depth = 1
    coeff_wide = extend(coefficients, halo_depth)
    members = panels.shape[0]
    fields, eof_count, row_count, col_count = control.shape
    flat_control = control.reshape(fields * eof_count, row_count, col_count)
    adjointed = diffuse(flat_control, coeff_wide, halo_depth, adjoint_section)
    projected = jnp.einsum(
        "mflyx,fle->mfeyx",
        lax.all_to_all(panels, "gz", split_axis=4, concat_axis=2, tiled=True),
        eof_basis,
        preferred_element_type=jnp.float32,
    )
    weights = adjointed.reshape(fields, eof_count, row_count, col_count)
    scores = jnp.sum(projected * weights[None], axis=(1, 2))
    combined = jnp.sum(projected * scores[:, None, None], axis=0) / (members - 1)
    result = diffuse(
        combined.reshape(fields * eof_count, row_count, col_count),
        coeff_wide,
        halo_depth,
        forward_section,
    )
    return result.reshape(fields, eof_count, row_count, col_count)


def solution(mesh):
    in_specs = (
        P(None, None, "gz", "gy", "gx"),
        P(),
        P(None, None, "gy", ("gx", "gz")),
        P(None, "gy", ("gx", "gz")),
    )
    out_specs = P(None, None, "gy", ("gx", "gz"))
    return jax.shard_map(
        per_device, mesh=mesh, in_specs=in_specs, out_specs=out_specs, check_vma=False
    )
```

profile of v0, /device:TPU:10, one launch (start us, length us, event | category | flops | bytes accessed | tf_op | source)
XLA Modules:
  0.0 283.1 jit_solution(17416321862199547483)
XLA Ops:
  0.9 2.0 collective-permute-start.1
  4.1 2.0 collective-permute-start.5
  7.0 3.5 %collective-permute-start.2 = (f32[4,1,130]{2,1,0:T(1,128)S(1)}, f32[4,1,130]{2,1,0:T(1,128)S(1)}, u32[]{:S(2)}, u32[]{:S(2)}) collective-permute-start(f32[4,1,130]{2,1,0:T(1,128)S(1)} %get-tuple-element.81), channel_id=1, source_target_pairs={{0,2},{2,4},{4,6},{1,3},{3,5},{5,7},{8,10},{10,12},{12,14},{9,11},... | collective-permute-start | bytes 6248 | tf_op jit(solution)/shard_map/ppermute | solution.py:20
  10.5 2.4 collective-permute-start.3
  14.2 3.5 %collective-permute-start.6 = (f32[40,1,130]{2,1,0:T(1,128)S(1)}, f32[40,1,130]{2,1,0:T(1,128)S(1)}, u32[]{:S(2)}, u32[]{:S(2)}) collective-permute-start(f32[40,1,130]{2,1,0:T(1,128)S(1)} %get-tuple-element.51), channel_id=1, source_target_pairs={{0,2},{2,4},{4,6},{1,3},{3,5},{5,7},{8,10},{10,12},{12,14},{9,11},... | collective-permute-start | bytes 62408 | tf_op jit(solution)/shard_map/ppermute | solution.py:20
  17.7 2.4 collective-permute-start.7
  21.6 2.0 collective-permute-done.7
  26.6 2.0 collective-permute-start.9
  28.6 5.1 %collective-permute-done.8 = f32[40,8,1]{2,1,0:T(8,128)S(1)} collective-permute-done((f32[40,8,1]{2,1,0:T(8,128)S(1)}, f32[40,8,1]{2,1,0:T(8,128)S(1)}, u32[]{:S(2)}, u32[]{:S(2)}) %collective-permute-start.8) | collective-permute-done | bytes 1312 | tf_op jit(solution)/shard_map/ppermute | solution.py:20
  35.1 3.5 %collective-permute-start.10 = (f32[40,1,130]{2,1,0:T(1,128)S(1)}, f32[40,1,130]{2,1,0:T(1,128)S(1)}, u32[]{:S(2)}, u32[]{:S(2)}) collective-permute-start(f32[40,1,130]{2,1,0:T(1,128)S(1)} %get-tuple-element.49), channel_id=1, source_target_pairs={{0,2},{2,4},{4,6},{1,3},{3,5},{5,7},{8,10},{10,12},{12,14},{9,11},... | collective-permute-start | bytes 62408 | tf_op jit(solution)/shard_map/ppermute | solution.py:20
  38.6 2.3 collective-permute-start.11
  41.3 3.2 %collective-permute-done.11 = f32[40,1,130]{2,1,0:T(1,128)S(1)} collective-permute-done((f32[40,1,130]{2,1,0:T(1,128)S(1)}, f32[40,1,130]{2,1,0:T(1,128)S(1)}, u32[]{:S(2)}, u32[]{:S(2)}) %collective-permute-start.11) | collective-permute-done | bytes 20832 | tf_op jit(solution)/shard_map/ppermute | solution.py:22
  47.6 5.1 %collective-permute-done.12 = f32[40,8,1]{2,1,0:T(8,128)S(1)} collective-permute-done((f32[40,8,1]{2,1,0:T(8,128)S(1)}, f32[40,8,1]{2,1,0:T(8,128)S(1)}, u32[]{:S(2)}, u32[]{:S(2)}) %collective-permute-start.12) | collective-permute-done | bytes 1312 | tf_op jit(solution)/shard_map/ppermute | solution.py:20
  53.8 1.9 collective-permute-start.14
  55.8 3.9 %collective-permute-start.15 = (f32[40,1,130]{2,1,0:T(1,128)S(1)}, f32[40,1,130]{2,1,0:T(1,128)S(1)}, u32[]{:S(2)}, u32[]{:S(2)}) collective-permute-start(f32[40,1,130]{2,1,0:T(1,128)S(1)} %get-tuple-element.48), channel_id=1, source_target_pairs={{2,0},{4,2},{6,4},{3,1},{5,3},{7,5},{10,8},{12,10},{14,12},{11,9},... | collective-permute-start | bytes 62408 | tf_op jit(solution)/shard_map/ppermute | solution.py:22
  59.7 1.9 collective-permute-done.15
  62.7 2.2 collective-permute-start.16
  65.5 4.9 %collective-permute-done.16 = f32[40,8,1]{2,1,0:T(8,128)S(1)} collective-permute-done((f32[40,8,1]{2,1,0:T(8,128)S(1)}, f32[40,8,1]{2,1,0:T(8,128)S(1)}, u32[]{:S(2)}, u32[]{:S(2)}) %collective-permute-start.16) | collective-permute-done | bytes 1312 | tf_op jit(solution)/shard_map/ppermute | solution.py:20
  70.5 2.2 collective-permute-done.17
  73.0 2.8 collective-permute-start.18
  75.9 3.0 %collective-permute-start.19 = (f32[40,1,130]{2,1,0:T(1,128)S(1)}, f32[40,1,130]{2,1,0:T(1,128)S(1)}, u32[]{:S(2)}, u32[]{:S(2)}) collective-permute-start(f32[40,1,130]{2,1,0:T(1,128)S(1)} %get-tuple-element.46), channel_id=1, source_target_pairs={{2,0},{4,2},{6,4},{3,1},{5,3},{7,5},{10,8},{12,10},{14,12},{11,9},... | collective-permute-start | bytes 62408 | tf_op jit(solution)/shard_map/ppermute | solution.py:22
  78.9 2.8 %collective-permute-done.19 = f32[40,1,130]{2,1,0:T(1,128)S(1)} collective-permute-done((f32[40,1,130]{2,1,0:T(1,128)S(1)}, f32[40,1,130]{2,1,0:T(1,128)S(1)}, u32[]{:S(2)}, u32[]{:S(2)}) %collective-permute-start.19) | collective-permute-done | bytes 20832 | tf_op jit(solution)/shard_map/ppermute | solution.py:22
  84.9 5.1 %collective-permute-done.20 = f32[40,8,1]{2,1,0:T(8,128)S(1)} collective-permute-done((f32[40,8,1]{2,1,0:T(8,128)S(1)}, f32[40,8,1]{2,1,0:T(8,128)S(1)}, u32[]{:S(2)}, u32[]{:S(2)}) %collective-permute-start.20) | collective-permute-done | bytes 1312 | tf_op jit(solution)/shard_map/ppermute | solution.py:20
  91.4 1.9 collective-permute-start.22
  93.4 3.9 %collective-permute-start.23 = (f32[40,1,130]{2,1,0:T(1,128)S(1)}, f32[40,1,130]{2,1,0:T(1,128)S(1)}, u32[]{:S(2)}, u32[]{:S(2)}) collective-permute-start(f32[40,1,130]{2,1,0:T(1,128)S(1)} %get-tuple-element.44), channel_id=1, source_target_pairs={{2,0},{4,2},{6,4},{3,1},{5,3},{7,5},{10,8},{12,10},{14,12},{11,9},... | collective-permute-start | bytes 62408 | tf_op jit(solution)/shard_map/ppermute | solution.py:22
  97.7 1.9 collective-permute-done.23
  102.9 5.0 %collective-permute-done.24 = f32[40,8,1]{2,1,0:T(8,128)S(1)} collective-permute-done((f32[40,8,1]{2,1,0:T(8,128)S(1)}, f32[40,8,1]{2,1,0:T(8,128)S(1)}, u32[]{:S(2)}, u32[]{:S(2)}) %collective-permute-start.24) | collective-permute-done | bytes 1312 | tf_op jit(solution)/shard_map/ppermute | solution.py:20
  109.8 1.9 collective-permute-start.26
  111.7 4.1 %collective-permute-start.27 = (f32[40,1,130]{2,1,0:T(1,128)S(1)}, f32[40,1,130]{2,1,0:T(1,128)S(1)}, u32[]{:S(2)}, u32[]{:S(2)}) collective-permute-start(f32[40,1,130]{2,1,0:T(1,128)S(1)} %get-tuple-element.42), channel_id=1, source_target_pairs={{2,0},{4,2},{6,4},{3,1},{5,3},{7,5},{10,8},{12,10},{14,12},{11,9},... | collective-permute-start | bytes 62408 | tf_op jit(solution)/shard_map/ppermute | solution.py:22
  115.8 11.8 %copy.19 = bf16[4,4,8,8,256]{3,2,1,0,4:T(8,128)(2,1)} copy(bf16[4,4,8,8,256]{4,3,2,1,0:T(8,128)(2,1)S(1)} %copy-done) | data formatting | bytes 1048576 | tf_op args[0]
  127.7 12.0 %reshape.15 = bf16[2,2,65536]{2,1,0:T(2,128)(2,1)} reshape(bf16[256,4,4,8,8]{4,3,2,1,0:T(8,128)(2,1)} %bitcast.28) | data formatting | bytes 1048576
  139.7 5.8 %all-to-all-start = ((bf16[2,2,65536]{2,1,0:T(2,128)(2,1)}), bf16[2,2,65536]{2,1,0:T(2,128)(2,1)S(1)}, u32[]{:S(2)}, u32[]{:S(2)}) async-start(bf16[2,2,65536]{2,1,0:T(2,128)(2,1)} %reshape.15), calls=%async_computation | async-start | bytes 1048576 | tf_op jit(solution)/shard_map/all_to_all | solution.py:71
  146.4 5.4 %all-to-all-done = bf16[2,2,65536]{2,1,0:T(2,128)(2,1)S(1)} async-done(((bf16[2,2,65536]{2,1,0:T(2,128)(2,1)}), bf16[2,2,65536]{2,1,0:T(2,128)(2,1)S(1)}, u32[]{:S(2)}, u32[]{:S(2)}) %all-to-all-start) | async-done | bytes 524320 | tf_op jit(solution)/shard_map/all_to_all | solution.py:71
  151.8 11.9 %reshape.16 = bf16[256,4,4,8,8]{4,3,2,1,0:T(8,128)(2,1)} reshape(bf16[2,2,65536]{2,1,0:T(2,128)(2,1)S(1)} %all-to-all-done) | data formatting | bytes 1048576
  163.7 9.4 %copy.20 = bf16[4,4,8,8,2,128]{5,2,4,3,0,1:T(8,128)(2,1)S(1)} copy(bf16[4,4,8,8,2,128]{3,2,1,0,5,4:T(8,128)(2,1)} %bitcast.27) | data formatting | bytes 1048576 | tf_op jit(solution)/shard_map/all_to_all | solution.py:71
  173.9 1.9 collective-permute-start.29
  175.8 4.9 %collective-permute-done.28 = f32[40,8,1]{2,1,0:T(8,128)S(1)} collective-permute-done((f32[40,8,1]{2,1,0:T(8,128)S(1)}, f32[40,8,1]{2,1,0:T(8,128)S(1)}, u32[]{:S(2)}, u32[]{:S(2)}) %collective-permute-start.28) | collective-permute-done | bytes 1312 | tf_op jit(solution)/shard_map/ppermute | solution.py:20
  181.9 2.5 collective-permute-start.30
  185.1 3.3 %collective-permute-start.31 = (f32[40,1,130]{2,1,0:T(1,128)S(1)}, f32[40,1,130]{2,1,0:T(1,128)S(1)}, u32[]{:S(2)}, u32[]{:S(2)}) collective-permute-start(f32[40,1,130]{2,1,0:T(1,128)S(1)} %get-tuple-element.39), channel_id=1, source_target_pairs={{2,0},{4,2},{6,4},{3,1},{5,3},{7,5},{10,8},{12,10},{14,12},{11,9},... | collective-permute-start | bytes 62408 | tf_op jit(solution)/shard_map/ppermute | solution.py:22
  188.8 2.4 collective-permute-done.31
  192.6 1.7 collective-permute-start.33
  194.3 5.0 %collective-permute-done.32 = f32[40,8,1]{2,1,0:T(8,128)S(1)} collective-permute-done((f32[40,8,1]{2,1,0:T(8,128)S(1)}, f32[40,8,1]{2,1,0:T(8,128)S(1)}, u32[]{:S(2)}, u32[]{:S(2)}) %collective-permute-start.32) | collective-permute-done | bytes 1312 | tf_op jit(solution)/shard_map/ppermute | solution.py:20
  200.2 2.7 collective-permute-start.34
  202.9 3.1 %collective-permute-start.35 = (f32[40,1,130]{2,1,0:T(1,128)S(1)}, f32[40,1,130]{2,1,0:T(1,128)S(1)}, u32[]{:S(2)}, u32[]{:S(2)}) collective-permute-start(f32[40,1,130]{2,1,0:T(1,128)S(1)} %get-tuple-element.37), channel_id=1, source_target_pairs={{2,0},{4,2},{6,4},{3,1},{5,3},{7,5},{10,8},{12,10},{14,12},{11,9},... | collective-permute-start | bytes 62408 | tf_op jit(solution)/shard_map/ppermute | solution.py:22
  206.4 2.5 collective-permute-done.35
  212.2 5.0 %collective-permute-done.36 = f32[40,8,1]{2,1,0:T(8,128)S(1)} collective-permute-done((f32[40,8,1]{2,1,0:T(8,128)S(1)}, f32[40,8,1]{2,1,0:T(8,128)S(1)}, u32[]{:S(2)}, u32[]{:S(2)}) %collective-permute-start.36) | collective-permute-done | bytes 1312 | tf_op jit(solution)/shard_map/ppermute | solution.py:20
  218.6 2.3 collective-permute-start.38
  220.9 3.6 %collective-permute-start.39 = (f32[40,1,130]{2,1,0:T(1,128)S(1)}, f32[40,1,130]{2,1,0:T(1,128)S(1)}, u32[]{:S(2)}, u32[]{:S(2)}) collective-permute-start(f32[40,1,130]{2,1,0:T(1,128)S(1)} %get-tuple-element.35), channel_id=1, source_target_pairs={{2,0},{4,2},{6,4},{3,1},{5,3},{7,5},{10,8},{12,10},{14,12},{11,9},... | collective-permute-start | bytes 62408 | tf_op jit(solution)/shard_map/ppermute | solution.py:22
  224.8 2.0 collective-permute-done.39
  227.5 1.7 collective-permute-start.40
  229.6 5.0 %collective-permute-done.40 = f32[40,8,1]{2,1,0:T(8,128)S(1)} collective-permute-done((f32[40,8,1]{2,1,0:T(8,128)S(1)}, f32[40,8,1]{2,1,0:T(8,128)S(1)}, u32[]{:S(2)}, u32[]{:S(2)}) %collective-permute-start.40) | collective-permute-done | bytes 1312 | tf_op jit(solution)/shard_map/ppermute | solution.py:20
  234.6 2.9 %collective-permute-done.41 = f32[40,8,1]{2,1,0:T(8,128)S(1)} collective-permute-done((f32[40,8,1]{2,1,0:T(8,128)S(1)}, f32[40,8,1]{2,1,0:T(8,128)S(1)}, u32[]{:S(2)}, u32[]{:S(2)}) %collective-permute-start.41) | collective-permute-done | bytes 1312 | tf_op jit(solution)/shard_map/ppermute | solution.py:22
  237.8 2.3 collective-permute-start.42
  240.1 3.6 %collective-permute-start.43 = (f32[40,1,130]{2,1,0:T(1,128)S(1)}, f32[40,1,130]{2,1,0:T(1,128)S(1)}, u32[]{:S(2)}, u32[]{:S(2)}) collective-permute-start(f32[40,1,130]{2,1,0:T(1,128)S(1)} %get-tuple-element.33), channel_id=1, source_target_pairs={{2,0},{4,2},{6,4},{3,1},{5,3},{7,5},{10,8},{12,10},{14,12},{11,9},... | collective-permute-start | bytes 62408 | tf_op jit(solution)/shard_map/ppermute | solution.py:22
  247.0 1.9 collective-permute-start.45
  248.8 5.1 %collective-permute-done.44 = f32[40,8,1]{2,1,0:T(8,128)S(1)} collective-permute-done((f32[40,8,1]{2,1,0:T(8,128)S(1)}, f32[40,8,1]{2,1,0:T(8,128)S(1)}, u32[]{:S(2)}, u32[]{:S(2)}) %collective-permute-start.44) | collective-permute-done | bytes 1312 | tf_op jit(solution)/shard_map/ppermute | solution.py:20
  255.3 2.5 collective-permute-start.46
  257.8 3.3 %collective-permute-start.47 = (f32[40,1,130]{2,1,0:T(1,128)S(1)}, f32[40,1,130]{2,1,0:T(1,128)S(1)}, u32[]{:S(2)}, u32[]{:S(2)}) collective-permute-start(f32[40,1,130]{2,1,0:T(1,128)S(1)} %get-tuple-element.31), channel_id=1, source_target_pairs={{2,0},{4,2},{6,4},{3,1},{5,3},{7,5},{10,8},{12,10},{14,12},{11,9},... | collective-permute-start | bytes 62408 | tf_op jit(solution)/shard_map/ppermute | solution.py:22
  261.8 2.0 collective-permute-done.47
  265.0 1.7 collective-permute-start.49
  266.6 5.1 %collective-permute-done.48 = f32[40,8,1]{2,1,0:T(8,128)S(1)} collective-permute-done((f32[40,8,1]{2,1,0:T(8,128)S(1)}, f32[40,8,1]{2,1,0:T(8,128)S(1)}, u32[]{:S(2)}, u32[]{:S(2)}) %collective-permute-start.48) | collective-permute-done | bytes 1312 | tf_op jit(solution)/shard_map/ppermute | solution.py:20
  273.2 2.8 collective-permute-start.50
  276.0 3.0 %collective-permute-start.51 = (f32[40,1,130]{2,1,0:T(1,128)S(1)}, f32[40,1,130]{2,1,0:T(1,128)S(1)}, u32[]{:S(2)}, u32[]{:S(2)}) collective-permute-start(f32[40,1,130]{2,1,0:T(1,128)S(1)} %get-tuple-element.29), channel_id=1, source_target_pairs={{2,0},{4,2},{6,4},{3,1},{5,3},{7,5},{10,8},{12,10},{14,12},{11,9},... | collective-permute-start | bytes 62408 | tf_op jit(solution)/shard_map/ppermute | solution.py:22
  279.4 2.5 collective-permute-done.51
  (119 shorter events, 49.1 us)
Async XLA Ops:
  0.9 5.2 %collective-permute-start = (f32[4,8,1]{2,1,0:T(8,128)S(1)}, f32[4,8,1]{2,1,0:T(8,128)S(1)}, u32[]{:S(2)}, u32[]{:S(2)}) collective-permute-start(f32[4,8,1]{2,1,0:T(8,128)S(1)} %get-tuple-element.82), channel_id=1, source_target_pairs={{0,1},{1,8},{8,9},{9,16},{16,17},{17,24},{24,25},{25,0},{2,3},{3,1... | collective-permute-start | bytes 392 | tf_op jit(solution)/shard_map/ppermute | solution.py:20
  0.9 5.2 %collective-permute-start.1 = (f32[4,8,1]{2,1,0:T(8,128)S(1)}, f32[4,8,1]{2,1,0:T(8,128)S(1)}, u32[]{:S(2)}, u32[]{:S(2)}) collective-permute-start(f32[4,8,1]{2,1,0:T(8,128)S(1)} %get-tuple-element.83), channel_id=1, source_target_pairs={{1,0},{8,1},{9,8},{16,9},{17,16},{24,17},{25,24},{0,25},{3,2},{10,... | collective-permute-start | bytes 392 | tf_op jit(solution)/shard_map/ppermute | solution.py:22
  4.0 8.8 %collective-permute-start.4 = (f32[40,8,1]{2,1,0:T(8,128)S(1)}, f32[40,8,1]{2,1,0:T(8,128)S(1)}, u32[]{:S(2)}, u32[]{:S(2)}) collective-permute-start(f32[40,8,1]{2,1,0:T(8,128)S(1)} %get-tuple-element.75), channel_id=1, source_target_pairs={{0,1},{1,8},{8,9},{9,16},{16,17},{17,24},{24,25},{25,0},{2,3},{3,1... | collective-permute-start | bytes 3848 | tf_op jit(solution)/shard_map/ppermute | solution.py:20
  4.1 8.8 %collective-permute-start.5 = (f32[40,8,1]{2,1,0:T(8,128)S(1)}, f32[40,8,1]{2,1,0:T(8,128)S(1)}, u32[]{:S(2)}, u32[]{:S(2)}) collective-permute-start(f32[40,8,1]{2,1,0:T(8,128)S(1)} %get-tuple-element.76), channel_id=1, source_target_pairs={{1,0},{8,1},{9,8},{16,9},{17,16},{24,17},{25,24},{0,25},{3,2},{10,... | collective-permute-start | bytes 3848 | tf_op jit(solution)/shard_map/ppermute | solution.py:22
  7.0 13.1 %collective-permute-start.2 = (f32[4,1,130]{2,1,0:T(1,128)S(1)}, f32[4,1,130]{2,1,0:T(1,128)S(1)}, u32[]{:S(2)}, u32[]{:S(2)}) collective-permute-start(f32[4,1,130]{2,1,0:T(1,128)S(1)} %get-tuple-element.81), channel_id=1, source_target_pairs={{0,2},{2,4},{4,6},{1,3},{3,5},{5,7},{8,10},{10,12},{12,14},{9,11},... | collective-permute-start | bytes 6248 | tf_op jit(solution)/shard_map/ppermute | solution.py:20
  10.5 10.4 %collective-permute-start.3 = (f32[4,1,130]{2,1,0:T(1,128)S(1)}, f32[4,1,130]{2,1,0:T(1,128)S(1)}, u32[]{:S(2)}, u32[]{:S(2)}) collective-permute-start(f32[4,1,130]{2,1,0:T(1,128)S(1)} %get-tuple-element.80), channel_id=1, source_target_pairs={{2,0},{4,2},{6,4},{3,1},{5,3},{7,5},{10,8},{12,10},{14,12},{11,9},... | collective-permute-start | bytes 6248 | tf_op jit(solution)/shard_map/ppermute | solution.py:22
  14.2 7.5 %collective-permute-start.6 = (f32[40,1,130]{2,1,0:T(1,128)S(1)}, f32[40,1,130]{2,1,0:T(1,128)S(1)}, u32[]{:S(2)}, u32[]{:S(2)}) collective-permute-start(f32[40,1,130]{2,1,0:T(1,128)S(1)} %get-tuple-element.51), channel_id=1, source_target_pairs={{0,2},{2,4},{4,6},{1,3},{3,5},{5,7},{8,10},{10,12},{12,14},{9,11},... | collective-permute-start | bytes 62408 | tf_op jit(solution)/shard_map/ppermute | solution.py:20
  17.7 5.9 %collective-permute-start.7 = (f32[40,1,130]{2,1,0:T(1,128)S(1)}, f32[40,1,130]{2,1,0:T(1,128)S(1)}, u32[]{:S(2)}, u32[]{:S(2)}) collective-permute-start(f32[40,1,130]{2,1,0:T(1,128)S(1)} %get-tuple-element.52), channel_id=1, source_target_pairs={{2,0},{4,2},{6,4},{3,1},{5,3},{7,5},{10,8},{12,10},{14,12},{11,9},... | collective-permute-start | bytes 62408 | tf_op jit(solution)/shard_map/ppermute | solution.py:22
  26.5 7.2 %collective-permute-start.8 = (f32[40,8,1]{2,1,0:T(8,128)S(1)}, f32[40,8,1]{2,1,0:T(8,128)S(1)}, u32[]{:S(2)}, u32[]{:S(2)}) collective-permute-start(f32[40,8,1]{2,1,0:T(8,128)S(1)} %get-tuple-element.73), channel_id=1, source_target_pairs={{0,1},{1,8},{8,9},{9,16},{16,17},{17,24},{24,25},{25,0},{2,3},{3,1... | collective-permute-start | bytes 3848 | tf_op jit(solution)/shard_map/ppermute | solution.py:20
  26.6 8.2 %collective-permute-start.9 = (f32[40,8,1]{2,1,0:T(8,128)S(1)}, f32[40,8,1]{2,1,0:T(8,128)S(1)}, u32[]{:S(2)}, u32[]{:S(2)}) collective-permute-start(f32[40,8,1]{2,1,0:T(8,128)S(1)} %get-tuple-element.74), channel_id=1, source_target_pairs={{1,0},{8,1},{9,8},{16,9},{17,16},{24,17},{25,24},{0,25},{3,2},{10,... | collective-permute-start | bytes 3848 | tf_op jit(solution)/shard_map/ppermute | solution.py:22
  35.1 6.2 %collective-permute-start.10 = (f32[40,1,130]{2,1,0:T(1,128)S(1)}, f32[40,1,130]{2,1,0:T(1,128)S(1)}, u32[]{:S(2)}, u32[]{:S(2)}) collective-permute-start(f32[40,1,130]{2,1,0:T(1,128)S(1)} %get-tuple-element.49), channel_id=1, source_target_pairs={{0,2},{2,4},{4,6},{1,3},{3,5},{5,7},{8,10},{10,12},{12,14},{9,11},... | collective-permute-start | bytes 62408 | tf_op jit(solution)/shard_map/ppermute | solution.py:20
  38.6 5.9 %collective-permute-start.11 = (f32[40,1,130]{2,1,0:T(1,128)S(1)}, f32[40,1,130]{2,1,0:T(1,128)S(1)}, u32[]{:S(2)}, u32[]{:S(2)}) collective-permute-start(f32[40,1,130]{2,1,0:T(1,128)S(1)} %get-tuple-element.50), channel_id=1, source_target_pairs={{2,0},{4,2},{6,4},{3,1},{5,3},{7,5},{10,8},{12,10},{14,12},{11,9},... | collective-permute-start | bytes 62408 | tf_op jit(solution)/shard_map/ppermute | solution.py:22
  45.5 7.2 %collective-permute-start.12 = (f32[40,8,1]{2,1,0:T(8,128)S(1)}, f32[40,8,1]{2,1,0:T(8,128)S(1)}, u32[]{:S(2)}, u32[]{:S(2)}) collective-permute-start(f32[40,8,1]{2,1,0:T(8,128)S(1)} %get-tuple-element.71), channel_id=1, source_target_pairs={{0,1},{1,8},{8,9},{9,16},{16,17},{17,24},{24,25},{25,0},{2,3},{3,1... | collective-permute-start | bytes 3848 | tf_op jit(solution)/shard_map/ppermute | solution.py:20
  46.3 7.2 %collective-permute-start.13 = (f32[40,8,1]{2,1,0:T(8,128)S(1)}, f32[40,8,1]{2,1,0:T(8,128)S(1)}, u32[]{:S(2)}, u32[]{:S(2)}) collective-permute-start(f32[40,8,1]{2,1,0:T(8,128)S(1)} %get-tuple-element.72), channel_id=1, source_target_pairs={{1,0},{8,1},{9,8},{16,9},{17,16},{24,17},{25,24},{0,25},{3,2},{10,... | collective-permute-start | bytes 3848 | tf_op jit(solution)/shard_map/ppermute | solution.py:22
  53.8 5.9 %collective-permute-start.14 = (f32[40,1,130]{2,1,0:T(1,128)S(1)}, f32[40,1,130]{2,1,0:T(1,128)S(1)}, u32[]{:S(2)}, u32[]{:S(2)}) collective-permute-start(f32[40,1,130]{2,1,0:T(1,128)S(1)} %get-tuple-element.47), channel_id=1, source_target_pairs={{0,2},{2,4},{4,6},{1,3},{3,5},{5,7},{8,10},{10,12},{12,14},{9,11},... | collective-permute-start | bytes 62408 | tf_op jit(solution)/shard_map/ppermute | solution.py:20
  55.8 5.9 %collective-permute-start.15 = (f32[40,1,130]{2,1,0:T(1,128)S(1)}, f32[40,1,130]{2,1,0:T(1,128)S(1)}, u32[]{:S(2)}, u32[]{:S(2)}) collective-permute-start(f32[40,1,130]{2,1,0:T(1,128)S(1)} %get-tuple-element.48), channel_id=1, source_target_pairs={{2,0},{4,2},{6,4},{3,1},{5,3},{7,5},{10,8},{12,10},{14,12},{11,9},... | collective-permute-start | bytes 62408 | tf_op jit(solution)/shard_map/ppermute | solution.py:22
  62.4 53.5 %copy-start = (bf16[4,4,8,8,256]{4,3,2,1,0:T(8,128)(2,1)S(1)}, bf16[4,4,8,8,256]{4,3,2,1,0:T(8,128)(2,1)}, u32[]{:S(2)}) copy-start(bf16[4,4,8,8,256]{4,3,2,1,0:T(8,128)(2,1)} %param.4) | copy-start | bytes 1572868
  62.7 7.8 %collective-permute-start.16 = (f32[40,8,1]{2,1,0:T(8,128)S(1)}, f32[40,8,1]{2,1,0:T(8,128)S(1)}, u32[]{:S(2)}, u32[]{:S(2)}) collective-permute-start(f32[40,8,1]{2,1,0:T(8,128)S(1)} %get-tuple-element.69), channel_id=1, source_target_pairs={{0,1},{1,8},{8,9},{9,16},{16,17},{17,24},{24,25},{25,0},{2,3},{3,1... | collective-permute-start | bytes 3848 | tf_op jit(solution)/shard_map/ppermute | solution.py:20
  64.9 7.8 %collective-permute-start.17 = (f32[40,8,1]{2,1,0:T(8,128)S(1)}, f32[40,8,1]{2,1,0:T(8,128)S(1)}, u32[]{:S(2)}, u32[]{:S(2)}) collective-permute-start(f32[40,8,1]{2,1,0:T(8,128)S(1)} %get-tuple-element.70), channel_id=1, source_target_pairs={{1,0},{8,1},{9,8},{16,9},{17,16},{24,17},{25,24},{0,25},{3,2},{10,... | collective-permute-start | bytes 3848 | tf_op jit(solution)/shard_map/ppermute | solution.py:22
  73.0 5.9 %collective-permute-start.18 = (f32[40,1,130]{2,1,0:T(1,128)S(1)}, f32[40,1,130]{2,1,0:T(1,128)S(1)}, u32[]{:S(2)}, u32[]{:S(2)}) collective-permute-start(f32[40,1,130]{2,1,0:T(1,128)S(1)} %get-tuple-element.45), channel_id=1, source_target_pairs={{0,2},{2,4},{4,6},{1,3},{3,5},{5,7},{8,10},{10,12},{12,14},{9,11},... | collective-permute-start | bytes 62408 | tf_op jit(solution)/shard_map/ppermute | solution.py:20
  75.9 5.9 %collective-permute-start.19 = (f32[40,1,130]{2,1,0:T(1,128)S(1)}, f32[40,1,130]{2,1,0:T(1,128)S(1)}, u32[]{:S(2)}, u32[]{:S(2)}) collective-permute-start(f32[40,1,130]{2,1,0:T(1,128)S(1)} %get-tuple-element.46), channel_id=1, source_target_pairs={{2,0},{4,2},{6,4},{3,1},{5,3},{7,5},{10,8},{12,10},{14,12},{11,9},... | collective-permute-start | bytes 62408 | tf_op jit(solution)/shard_map/ppermute | solution.py:22
  82.8 7.2 %collective-permute-start.20 = (f32[40,8,1]{2,1,0:T(8,128)S(1)}, f32[40,8,1]{2,1,0:T(8,128)S(1)}, u32[]{:S(2)}, u32[]{:S(2)}) collective-permute-start(f32[40,8,1]{2,1,0:T(8,128)S(1)} %get-tuple-element.67), channel_id=1, source_target_pairs={{0,1},{1,8},{8,9},{9,16},{16,17},{17,24},{24,25},{25,0},{2,3},{3,1... | collective-permute-start | bytes 3848 | tf_op jit(solution)/shard_map/ppermute | solution.py:20
  83.5 7.6 %collective-permute-start.21 = (f32[40,8,1]{2,1,0:T(8,128)S(1)}, f32[40,8,1]{2,1,0:T(8,128)S(1)}, u32[]{:S(2)}, u32[]{:S(2)}) collective-permute-start(f32[40,8,1]{2,1,0:T(8,128)S(1)} %get-tuple-element.68), channel_id=1, source_target_pairs={{1,0},{8,1},{9,8},{16,9},{17,16},{24,17},{25,24},{0,25},{3,2},{10,... | collective-permute-start | bytes 3848 | tf_op jit(solution)/shard_map/ppermute | solution.py:22
  91.4 6.3 %collective-permute-start.22 = (f32[40,1,130]{2,1,0:T(1,128)S(1)}, f32[40,1,130]{2,1,0:T(1,128)S(1)}, u32[]{:S(2)}, u32[]{:S(2)}) collective-permute-start(f32[40,1,130]{2,1,0:T(1,128)S(1)} %get-tuple-element.43), channel_id=1, source_target_pairs={{0,2},{2,4},{4,6},{1,3},{3,5},{5,7},{8,10},{10,12},{12,14},{9,11},... | collective-permute-start | bytes 62408 | tf_op jit(solution)/shard_map/ppermute | solution.py:20
  93.4 6.3 %collective-permute-start.23 = (f32[40,1,130]{2,1,0:T(1,128)S(1)}, f32[40,1,130]{2,1,0:T(1,128)S(1)}, u32[]{:S(2)}, u32[]{:S(2)}) collective-permute-start(f32[40,1,130]{2,1,0:T(1,128)S(1)} %get-tuple-element.44), channel_id=1, source_target_pairs={{2,0},{4,2},{6,4},{3,1},{5,3},{7,5},{10,8},{12,10},{14,12},{11,9},... | collective-permute-start | bytes 62408 | tf_op jit(solution)/shard_map/ppermute | solution.py:22
  100.7 7.2 %collective-permute-start.24 = (f32[40,8,1]{2,1,0:T(8,128)S(1)}, f32[40,8,1]{2,1,0:T(8,128)S(1)}, u32[]{:S(2)}, u32[]{:S(2)}) collective-permute-start(f32[40,8,1]{2,1,0:T(8,128)S(1)} %get-tuple-element.65), channel_id=1, source_target_pairs={{0,1},{1,8},{8,9},{9,16},{16,17},{17,24},{24,25},{25,0},{2,3},{3,1... | collective-permute-start | bytes 3848 | tf_op jit(solution)/shard_map/ppermute | solution.py:20
  101.6 7.9 %collective-permute-start.25 = (f32[40,8,1]{2,1,0:T(8,128)S(1)}, f32[40,8,1]{2,1,0:T(8,128)S(1)}, u32[]{:S(2)}, u32[]{:S(2)}) collective-permute-start(f32[40,8,1]{2,1,0:T(8,128)S(1)} %get-tuple-element.66), channel_id=1, source_target_pairs={{1,0},{8,1},{9,8},{16,9},{17,16},{24,17},{25,24},{0,25},{3,2},{10,... | collective-permute-start | bytes 3848 | tf_op jit(solution)/shard_map/ppermute | solution.py:22
  109.8 35.7 %collective-permute-start.26 = (f32[40,1,130]{2,1,0:T(1,128)S(1)}, f32[40,1,130]{2,1,0:T(1,128)S(1)}, u32[]{:S(2)}, u32[]{:S(2)}) collective-permute-start(f32[40,1,130]{2,1,0:T(1,128)S(1)} %get-tuple-element.41), channel_id=1, source_target_pairs={{0,2},{2,4},{4,6},{1,3},{3,5},{5,7},{8,10},{10,12},{12,14},{9,11},... | collective-permute-start | bytes 62408 | tf_op jit(solution)/shard_map/ppermute | solution.py:20
  111.7 33.7 %collective-permute-start.27 = (f32[40,1,130]{2,1,0:T(1,128)S(1)}, f32[40,1,130]{2,1,0:T(1,128)S(1)}, u32[]{:S(2)}, u32[]{:S(2)}) collective-permute-start(f32[40,1,130]{2,1,0:T(1,128)S(1)} %get-tuple-element.42), channel_id=1, source_target_pairs={{2,0},{4,2},{6,4},{3,1},{5,3},{7,5},{10,8},{12,10},{14,12},{11,9},... | collective-permute-start | bytes 62408 | tf_op jit(solution)/shard_map/ppermute | solution.py:22
  139.7 12.1 %all-to-all-start = ((bf16[2,2,65536]{2,1,0:T(2,128)(2,1)}), bf16[2,2,65536]{2,1,0:T(2,128)(2,1)S(1)}, u32[]{:S(2)}, u32[]{:S(2)}) async-start(bf16[2,2,65536]{2,1,0:T(2,128)(2,1)} %reshape.15), calls=%async_computation | async-start | bytes 1048576 | tf_op jit(solution)/shard_map/all_to_all | solution.py:71
  146.4 26.7 %copy-start.1 = (bf16[4,16,10]{1,0,2:T(4,128)(2,1)S(1)}, bf16[4,16,10]{1,0,2:T(4,128)(2,1)}, u32[]{:S(2)}) copy-start(bf16[4,16,10]{1,0,2:T(4,128)(2,1)} %param.5) | copy-start | bytes 3844
  173.8 7.0 %collective-permute-start.28 = (f32[40,8,1]{2,1,0:T(8,128)S(1)}, f32[40,8,1]{2,1,0:T(8,128)S(1)}, u32[]{:S(2)}, u32[]{:S(2)}) collective-permute-start(f32[40,8,1]{2,1,0:T(8,128)S(1)} %get-tuple-element.63), channel_id=1, source_target_pairs={{0,1},{1,8},{8,9},{9,16},{16,17},{17,24},{24,25},{25,0},{2,3},{3,1... | collective-permute-start | bytes 3848 | tf_op jit(solution)/shard_map/ppermute | solution.py:20
  173.9 7.7 %collective-permute-start.29 = (f32[40,8,1]{2,1,0:T(8,128)S(1)}, f32[40,8,1]{2,1,0:T(8,128)S(1)}, u32[]{:S(2)}, u32[]{:S(2)}) collective-permute-start(f32[40,8,1]{2,1,0:T(8,128)S(1)} %get-tuple-element.64), channel_id=1, source_target_pairs={{1,0},{8,1},{9,8},{16,9},{17,16},{24,17},{25,24},{0,25},{3,2},{10,... | collective-permute-start | bytes 3848 | tf_op jit(solution)/shard_map/ppermute | solution.py:22
  181.9 6.5 %collective-permute-start.30 = (f32[40,1,130]{2,1,0:T(1,128)S(1)}, f32[40,1,130]{2,1,0:T(1,128)S(1)}, u32[]{:S(2)}, u32[]{:S(2)}) collective-permute-start(f32[40,1,130]{2,1,0:T(1,128)S(1)} %get-tuple-element.40), channel_id=1, source_target_pairs={{0,2},{2,4},{4,6},{1,3},{3,5},{5,7},{8,10},{10,12},{12,14},{9,11},... | collective-permute-start | bytes 62408 | tf_op jit(solution)/shard_map/ppermute | solution.py:20
  185.1 6.0 %collective-permute-start.31 = (f32[40,1,130]{2,1,0:T(1,128)S(1)}, f32[40,1,130]{2,1,0:T(1,128)S(1)}, u32[]{:S(2)}, u32[]{:S(2)}) collective-permute-start(f32[40,1,130]{2,1,0:T(1,128)S(1)} %get-tuple-element.39), channel_id=1, source_target_pairs={{2,0},{4,2},{6,4},{3,1},{5,3},{7,5},{10,8},{12,10},{14,12},{11,9},... | collective-permute-start | bytes 62408 | tf_op jit(solution)/shard_map/ppermute | solution.py:22
  191.9 7.5 %collective-permute-start.32 = (f32[40,8,1]{2,1,0:T(8,128)S(1)}, f32[40,8,1]{2,1,0:T(8,128)S(1)}, u32[]{:S(2)}, u32[]{:S(2)}) collective-permute-start(f32[40,8,1]{2,1,0:T(8,128)S(1)} %get-tuple-element.61), channel_id=1, source_target_pairs={{0,1},{1,8},{8,9},{9,16},{16,17},{17,24},{24,25},{25,0},{2,3},{3,1... | collective-permute-start | bytes 3848 | tf_op jit(solution)/shard_map/ppermute | solution.py:20
  192.6 7.3 %collective-permute-start.33 = (f32[40,8,1]{2,1,0:T(8,128)S(1)}, f32[40,8,1]{2,1,0:T(8,128)S(1)}, u32[]{:S(2)}, u32[]{:S(2)}) collective-permute-start(f32[40,8,1]{2,1,0:T(8,128)S(1)} %get-tuple-element.62), channel_id=1, source_target_pairs={{1,0},{8,1},{9,8},{16,9},{17,16},{24,17},{25,24},{0,25},{3,2},{10,... | collective-permute-start | bytes 3848 | tf_op jit(solution)/shard_map/ppermute | solution.py:22
  200.2 5.9 %collective-permute-start.34 = (f32[40,1,130]{2,1,0:T(1,128)S(1)}, f32[40,1,130]{2,1,0:T(1,128)S(1)}, u32[]{:S(2)}, u32[]{:S(2)}) collective-permute-start(f32[40,1,130]{2,1,0:T(1,128)S(1)} %get-tuple-element.38), channel_id=1, source_target_pairs={{0,2},{2,4},{4,6},{1,3},{3,5},{5,7},{8,10},{10,12},{12,14},{9,11},... | collective-permute-start | bytes 62408 | tf_op jit(solution)/shard_map/ppermute | solution.py:20
  202.9 6.0 %collective-permute-start.35 = (f32[40,1,130]{2,1,0:T(1,128)S(1)}, f32[40,1,130]{2,1,0:T(1,128)S(1)}, u32[]{:S(2)}, u32[]{:S(2)}) collective-permute-start(f32[40,1,130]{2,1,0:T(1,128)S(1)} %get-tuple-element.37), channel_id=1, source_target_pairs={{2,0},{4,2},{6,4},{3,1},{5,3},{7,5},{10,8},{12,10},{14,12},{11,9},... | collective-permute-start | bytes 62408 | tf_op jit(solution)/shard_map/ppermute | solution.py:22
  209.7 7.5 %collective-permute-start.36 = (f32[40,8,1]{2,1,0:T(8,128)S(1)}, f32[40,8,1]{2,1,0:T(8,128)S(1)}, u32[]{:S(2)}, u32[]{:S(2)}) collective-permute-start(f32[40,8,1]{2,1,0:T(8,128)S(1)} %get-tuple-element.59), channel_id=1, source_target_pairs={{0,1},{1,8},{8,9},{9,16},{16,17},{17,24},{24,25},{25,0},{2,3},{3,1... | collective-permute-start | bytes 3848 | tf_op jit(solution)/shard_map/ppermute | solution.py:20
  210.7 7.5 %collective-permute-start.37 = (f32[40,8,1]{2,1,0:T(8,128)S(1)}, f32[40,8,1]{2,1,0:T(8,128)S(1)}, u32[]{:S(2)}, u32[]{:S(2)}) collective-permute-start(f32[40,8,1]{2,1,0:T(8,128)S(1)} %get-tuple-element.60), channel_id=1, source_target_pairs={{1,0},{8,1},{9,8},{16,9},{17,16},{24,17},{25,24},{0,25},{3,2},{10,... | collective-permute-start | bytes 3848 | tf_op jit(solution)/shard_map/ppermute | solution.py:22
  218.6 5.9 %collective-permute-start.38 = (f32[40,1,130]{2,1,0:T(1,128)S(1)}, f32[40,1,130]{2,1,0:T(1,128)S(1)}, u32[]{:S(2)}, u32[]{:S(2)}) collective-permute-start(f32[40,1,130]{2,1,0:T(1,128)S(1)} %get-tuple-element.36), channel_id=1, source_target_pairs={{0,2},{2,4},{4,6},{1,3},{3,5},{5,7},{8,10},{10,12},{12,14},{9,11},... | collective-permute-start | bytes 62408 | tf_op jit(solution)/shard_map/ppermute | solution.py:20
  220.9 5.9 %collective-permute-start.39 = (f32[40,1,130]{2,1,0:T(1,128)S(1)}, f32[40,1,130]{2,1,0:T(1,128)S(1)}, u32[]{:S(2)}, u32[]{:S(2)}) collective-permute-start(f32[40,1,130]{2,1,0:T(1,128)S(1)} %get-tuple-element.35), channel_id=1, source_target_pairs={{2,0},{4,2},{6,4},{3,1},{5,3},{7,5},{10,8},{12,10},{14,12},{11,9},... | collective-permute-start | bytes 62408 | tf_op jit(solution)/shard_map/ppermute | solution.py:22
  227.5 7.1 %collective-permute-start.40 = (f32[40,8,1]{2,1,0:T(8,128)S(1)}, f32[40,8,1]{2,1,0:T(8,128)S(1)}, u32[]{:S(2)}, u32[]{:S(2)}) collective-permute-start(f32[40,8,1]{2,1,0:T(8,128)S(1)} %get-tuple-element.57), channel_id=1, source_target_pairs={{0,1},{1,8},{8,9},{9,16},{16,17},{17,24},{24,25},{25,0},{2,3},{3,1... | collective-permute-start | bytes 3848 | tf_op jit(solution)/shard_map/ppermute | solution.py:20
  229.2 8.4 %collective-permute-start.41 = (f32[40,8,1]{2,1,0:T(8,128)S(1)}, f32[40,8,1]{2,1,0:T(8,128)S(1)}, u32[]{:S(2)}, u32[]{:S(2)}) collective-permute-start(f32[40,8,1]{2,1,0:T(8,128)S(1)} %get-tuple-element.58), channel_id=1, source_target_pairs={{1,0},{8,1},{9,8},{16,9},{17,16},{24,17},{25,24},{0,25},{3,2},{10,... | collective-permute-start | bytes 3848 | tf_op jit(solution)/shard_map/ppermute | solution.py:22
  237.8 6.2 %collective-permute-start.42 = (f32[40,1,130]{2,1,0:T(1,128)S(1)}, f32[40,1,130]{2,1,0:T(1,128)S(1)}, u32[]{:S(2)}, u32[]{:S(2)}) collective-permute-start(f32[40,1,130]{2,1,0:T(1,128)S(1)} %get-tuple-element.34), channel_id=1, source_target_pairs={{0,2},{2,4},{4,6},{1,3},{3,5},{5,7},{8,10},{10,12},{12,14},{9,11},... | collective-permute-start | bytes 62408 | tf_op jit(solution)/shard_map/ppermute | solution.py:20
  240.1 5.9 %collective-permute-start.43 = (f32[40,1,130]{2,1,0:T(1,128)S(1)}, f32[40,1,130]{2,1,0:T(1,128)S(1)}, u32[]{:S(2)}, u32[]{:S(2)}) collective-permute-start(f32[40,1,130]{2,1,0:T(1,128)S(1)} %get-tuple-element.33), channel_id=1, source_target_pairs={{2,0},{4,2},{6,4},{3,1},{5,3},{7,5},{10,8},{12,10},{14,12},{11,9},... | collective-permute-start | bytes 62408 | tf_op jit(solution)/shard_map/ppermute | solution.py:22
  246.7 7.2 %collective-permute-start.44 = (f32[40,8,1]{2,1,0:T(8,128)S(1)}, f32[40,8,1]{2,1,0:T(8,128)S(1)}, u32[]{:S(2)}, u32[]{:S(2)}) collective-permute-start(f32[40,8,1]{2,1,0:T(8,128)S(1)} %get-tuple-element.55), channel_id=1, source_target_pairs={{0,1},{1,8},{8,9},{9,16},{16,17},{17,24},{24,25},{25,0},{2,3},{3,1... | collective-permute-start | bytes 3848 | tf_op jit(solution)/shard_map/ppermute | solution.py:20
  247.0 8.0 %collective-permute-start.45 = (f32[40,8,1]{2,1,0:T(8,128)S(1)}, f32[40,8,1]{2,1,0:T(8,128)S(1)}, u32[]{:S(2)}, u32[]{:S(2)}) collective-permute-start(f32[40,8,1]{2,1,0:T(8,128)S(1)} %get-tuple-element.56), channel_id=1, source_target_pairs={{1,0},{8,1},{9,8},{16,9},{17,16},{24,17},{25,24},{0,25},{3,2},{10,... | collective-permute-start | bytes 3848 | tf_op jit(solution)/shard_map/ppermute | solution.py:22
  255.3 6.2 %collective-permute-start.46 = (f32[40,1,130]{2,1,0:T(1,128)S(1)}, f32[40,1,130]{2,1,0:T(1,128)S(1)}, u32[]{:S(2)}, u32[]{:S(2)}) collective-permute-start(f32[40,1,130]{2,1,0:T(1,128)S(1)} %get-tuple-element.32), channel_id=1, source_target_pairs={{0,2},{2,4},{4,6},{1,3},{3,5},{5,7},{8,10},{10,12},{12,14},{9,11},... | collective-permute-start | bytes 62408 | tf_op jit(solution)/shard_map/ppermute | solution.py:20
  257.8 6.0 %collective-permute-start.47 = (f32[40,1,130]{2,1,0:T(1,128)S(1)}, f32[40,1,130]{2,1,0:T(1,128)S(1)}, u32[]{:S(2)}, u32[]{:S(2)}) collective-permute-start(f32[40,1,130]{2,1,0:T(1,128)S(1)} %get-tuple-element.31), channel_id=1, source_target_pairs={{2,0},{4,2},{6,4},{3,1},{5,3},{7,5},{10,8},{12,10},{14,12},{11,9},... | collective-permute-start | bytes 62408 | tf_op jit(solution)/shard_map/ppermute | solution.py:22
  264.5 7.2 %collective-permute-start.48 = (f32[40,8,1]{2,1,0:T(8,128)S(1)}, f32[40,8,1]{2,1,0:T(8,128)S(1)}, u32[]{:S(2)}, u32[]{:S(2)}) collective-permute-start(f32[40,8,1]{2,1,0:T(8,128)S(1)} %get-tuple-element.53), channel_id=1, source_target_pairs={{0,1},{1,8},{8,9},{9,16},{16,17},{17,24},{24,25},{25,0},{2,3},{3,1... | collective-permute-start | bytes 3848 | tf_op jit(solution)/shard_map/ppermute | solution.py:20
  265.0 7.9 %collective-permute-start.49 = (f32[40,8,1]{2,1,0:T(8,128)S(1)}, f32[40,8,1]{2,1,0:T(8,128)S(1)}, u32[]{:S(2)}, u32[]{:S(2)}) collective-permute-start(f32[40,8,1]{2,1,0:T(8,128)S(1)} %get-tuple-element.54), channel_id=1, source_target_pairs={{1,0},{8,1},{9,8},{16,9},{17,16},{24,17},{25,24},{0,25},{3,2},{10,... | collective-permute-start | bytes 3848 | tf_op jit(solution)/shard_map/ppermute | solution.py:22
  273.2 5.9 %collective-permute-start.50 = (f32[40,1,130]{2,1,0:T(1,128)S(1)}, f32[40,1,130]{2,1,0:T(1,128)S(1)}, u32[]{:S(2)}, u32[]{:S(2)}) collective-permute-start(f32[40,1,130]{2,1,0:T(1,128)S(1)} %get-tuple-element.30), channel_id=1, source_target_pairs={{0,2},{2,4},{4,6},{1,3},{3,5},{5,7},{8,10},{10,12},{12,14},{9,11},... | collective-permute-start | bytes 62408 | tf_op jit(solution)/shard_map/ppermute | solution.py:20
  276.0 5.9 %collective-permute-start.51 = (f32[40,1,130]{2,1,0:T(1,128)S(1)}, f32[40,1,130]{2,1,0:T(1,128)S(1)}, u32[]{:S(2)}, u32[]{:S(2)}) collective-permute-start(f32[40,1,130]{2,1,0:T(1,128)S(1)} %get-tuple-element.29), channel_id=1, source_target_pairs={{2,0},{4,2},{6,4},{3,1},{5,3},{7,5},{10,8},{12,10},{14,12},{11,9},... | collective-permute-start | bytes 62408 | tf_op jit(solution)/shard_map/ppermute | solution.py:22
where the time goes:
time: 288 us; the launch traced here: 283 us
  starting transfers between devices  111 us (39%)
  waiting for transfers between devices  102 us (35%)
  local copies, waits for them, and re-layouts  48.3 us (17%)
  other arithmetic  21.6 us (8%)
    ppermute x26, starting transfers between devices, padded_2(): lax.ppermute(head, axis, [((i + 1) % count, i) for i in range(ends)])  61.6 us
    ppermute x26, waiting for transfers between devices, padded_2(): lax.ppermute(tail, axis, [(i, (i + 1) % count) for i in range(ends)])  57 us
    ppermute x26, starting transfers between devices, padded_2(): lax.ppermute(tail, axis, [(i, (i + 1) % count) for i in range(ends)])  43.2 us
    ppermute x26, waiting for transfers between devices, padded_2(): lax.ppermute(head, axis, [((i + 1) % count, i) for i in range(ends)])  39.4 us
    unnamed x7, local copies, waits for them, and re-layouts  35.8 us
    all_to_all x1, local copies, waits for them, and re-layouts, per_device(): lax.all_to_all(panels, 'gz', split_axis=4, concat_axis=2, tiled=True)  9.42 us
    all_to_all x1, starting transfers between devices, per_device(): lax.all_to_all(panels, 'gz', split_axis=4, concat_axis=2, tiled=True)  5.78 us
  transfers between devices with their start and end apart: 53, of which 38 were waited for; matrix products, arithmetic and copies ran while one was open for 11% of the time, Pallas kernels for 0%

commit v1 on v0

v1 whole, which is shorter than its diff:
```python
import functools

import jax
import jax.numpy as jnp
from jax import lax
from jax.experimental import pallas as pl
from jax.experimental.pallas import tpu as pltpu
from jax.sharding import PartitionSpec as P

STEPS = 6
LANES = 128
SUB = 8
RING = ("gx", "gz")

time_step = 0.09

WINDOW = SUB + 2 * STEPS
HALO = 2 * STEPS
SLOT = 32


def turn(cells, shift):
    return pltpu.roll(cells, shift % LANES, 1)


def swap_a(values, axes):
    count = lax.axis_size(axes)
    return lax.ppermute(values, axes, [(i, i ^ 1) for i in range(count)])


def swap_b(values, axes, closed):
    count = lax.axis_size(axes)
    pairs = [(i, i + 1) for i in range(1, count - 1, 2)]
    if closed:
        pairs.append((count - 1, 0))
    return lax.ppermute(values, axes, pairs + [(j, i) for i, j in pairs])


def place(w):
    return (w + 2) // SUB, (w + 2) % SUB


def lane_grid():
    return lax.broadcasted_iota(jnp.int32, (SUB, LANES), 1)


def diffuse(rows, coeff, adjoint):
    for step in range(STEPS):
        low, high = step, WINDOW - 1 - step
        moved = {}
        if adjoint:
            seen = {w: coeff(3, w) * rows[w] for w in range(low, high + 1)}
        else:
            seen = rows
        south = None
        for w in range(low, high):
            east_diff = turn(seen[w], -1) - seen[w]
            north_diff = seen[w + 1] - seen[w]
            cross = coeff(1, w)
            flux_north = cross * east_diff + coeff(2, w) * north_diff
            if w > low:
                flux_east = coeff(0, w) * east_diff + cross * north_diff
                div = flux_east - turn(flux_east, 1) + (flux_north - south)
                moved[w] = rows[w] + (div if adjoint else coeff(3, w) * div)
            south = flux_north
        rows = moved
    return rows


def tile_picker(own, from_a, from_b, odd):
    def tile(t, index):
        at = pl.ds(index * SUB, SUB)
        if t == 1:
            return own[at, :]
        first, second = (from_a, from_b) if t == 0 else (from_b, from_a)
        return jnp.where(odd, first[at, :], second[at, :])

    return tile


def row_picker(own, from_a, from_b, odd):
    def row(w, group):
        t, y = place(w)
        at = pl.ds(group * SUB * SUB + y, SUB, stride=SUB)
        if t == 1:
            return own[at, :]
        first, second = (from_a, from_b) if t == 0 else (from_b, from_a)
        return jnp.where(odd, first[at, :], second[at, :])

    return row


def pack_kernel(
    fields, eofs, members, place_ref, own, from_a, from_b, panel, *rest
):
    arrived, (out_a, out_b) = rest[:-2], rest[-2:]
    ring_odd, odd, me = place_ref[0] == 1, place_ref[1] == 1, place_ref[2]
    tile = tile_picker(own, from_a, from_b, odd)
    lane = lane_grid()
    pair = eofs // 2
    zero = jnp.zeros((SUB, LANES), jnp.float32)

    def put(at, west, east):
        out_a[at, :] = jnp.where(ring_odd, west, east)
        out_b[at, :] = jnp.where(ring_odd, east, west)

    for t in range(3):
        for j in range(pair):
            west, east = zero, zero
            for half in range(2):
                for f in range(fields):
                    cells = tile(t, f * eofs + half * pair + j)
                    start = f * SLOT + half * (SLOT // 2)
                    mask = (lane >= start) & (lane < start + HALO)
                    west = jnp.where(mask, turn(cells, start), west)
                    east = jnp.where(mask, turn(cells, start + HALO - LANES), east)
            put(pl.ds((t * pair + j) * SUB, SUB), west, east)
        west, east = zero, zero
        for k in range(4):
            cells = tile(t, fields * eofs + k)
            start = k * SLOT
            mask = (lane >= start) & (lane < start + HALO)
            west = jnp.where(mask, turn(cells, start), west)
            east = jnp.where(mask, turn(cells, start + HALO - LANES), east)
        put(pl.ds((3 * pair + t) * SUB, SUB), west, east)

    base = 3 * (pair + 1) * SUB
    depth = panel.shape[2] * SUB
    column = lax.broadcasted_iota(jnp.int32, (LANES, 2 * LANES), 0)
    target = lax.broadcasted_iota(jnp.int32, (LANES, 2 * LANES), 1)
    west_ok = (target < LANES) & (column < STEPS)
    east_ok = (target >= LANES) & (column >= LANES - STEPS)
    offset = jnp.where(
        west_ok,
        target - column,
        jnp.where(east_ok, target - LANES - column + LANES - STEPS, -1),
    )
    blocks = (panel,) + arrived
    count = len(blocks)
    for s, block in enumerate(blocks):
        total = jnp.zeros((depth, 2 * LANES), jnp.float32)
        for m in range(members):
            for f in range(fields):
                pick = (offset == f * SLOT + m * SUB).astype(jnp.bfloat16)
                total += jnp.dot(
                    block[m, f].reshape(depth, LANES), pick, preferred_element_type=jnp.float32
                )
        start = pl.multiple_of(base + lax.rem(me - s + count, count) * depth, SUB)
        put(pl.ds(start, depth), total[:, :LANES], total[:, LANES:])


def main_kernel(
    fields, eofs, members, place_ref, own, from_a, from_b, basis, panel, *rest
):
    arrived, (adj, proj, strip, coeff_main, coeff_strip, wide) = rest[:-6], rest[-6:]
    odd, me = place_ref[1] == 1, place_ref[2]
    tile = tile_picker(own, from_a, from_b, odd)
    row = row_picker(own, from_a, from_b, odd)
    lane = lane_grid()
    inner = lane & (SLOT - 1)
    shifted = (lane + STEPS) & (LANES - 1)
    zero = jnp.zeros((SUB, LANES), jnp.float32)

    blocks = (panel,) + arrived
    count = len(blocks)
    depth = panel.shape[2] * SUB
    for f in range(fields):
        total = None
        for s, block in enumerate(blocks):
            cells = jnp.concatenate(
                [block[m, f].reshape(depth, LANES) for m in range(members)], axis=1
            )
            part = jnp.dot(
                basis[lax.rem(me - s + count, count), f], cells, preferred_element_type=jnp.float32
            )
            total = part if total is None else total + part
        for m in range(members):
            proj[m, pl.ds(f * eofs * SUB, eofs * SUB), :] = total[:, m * LANES : (m + 1) * LANES]

    for k in range(4):
        for t in range(3):
            cells = tile(t, fields * eofs + k)
            if k < 3:
                cells = time_step * cells
            at = pl.ds(t * SUB, SUB)
            coeff_main[k, at, :] = cells
            west, east = zero, zero
            for f in range(fields):
                start = f * SLOT
                west = jnp.where(lane // SLOT == f, turn(cells, start + HALO), west)
                east = jnp.where(shifted // SLOT == f, turn(cells, start - STEPS - LANES + HALO), east)
            coeff_strip[0, k, at, :] = jnp.where((inner >= HALO) & (inner < 2 * HALO), west, 0.0)
            coeff_strip[1, k, at, :] = jnp.where((shifted & (SLOT - 1)) < HALO, east, 0.0)
        for w in range(WINDOW):
            wide[k, w] = jnp.broadcast_to(coeff_main[k, pl.ds(w + 2, 1), :], (SUB, LANES))

    def group(g, carry):
        rows = {w: row(w, g) for w in range(WINDOW)}
        rows = diffuse(rows, lambda k, w: wide[k, w], True)
        for y in range(SUB):
            adj[pl.ds(g * SUB * SUB + y, SUB, stride=SUB), :] = rows[y + STEPS]
        return carry

    lax.fori_loop(0, fields * eofs // SUB, group, 0)

    for t in range(3):
        for e in range(eofs):
            west, east = zero, zero
            for f in range(fields):
                cells = tile(t, f * eofs + e)
                west = jnp.where(lane // SLOT == f, turn(cells, f * SLOT + HALO), west)
                east = jnp.where(
                    shifted // SLOT == f, turn(cells, f * SLOT - STEPS - LANES + HALO), east
                )
            strip[t, pl.ds(e * SUB, SUB), :] = west
            strip[t, pl.ds((eofs + e) * SUB, SUB), :] = east
        strip[t, pl.ds(2 * eofs * SUB, 4 * SUB), :] = jnp.zeros((4 * SUB, LANES), jnp.float32)


def strip_coefficients(coeff_strip, wide_strip, eofs):
    sub = lax.broadcasted_iota(jnp.int32, (SUB, LANES), 0)
    for k in range(4):
        for w in range(WINDOW):
            west = jnp.broadcast_to(coeff_strip[0, k, pl.ds(w + 2, 1), :], (SUB, LANES))
            east = jnp.broadcast_to(coeff_strip[1, k, pl.ds(w + 2, 1), :], (SUB, LANES))
            wide_strip[k, w, pl.ds(0, SUB), :] = west
            wide_strip[k, w, pl.ds(SUB, SUB), :] = jnp.where(sub < eofs - SUB, west, east)
            wide_strip[k, w, pl.ds(2 * SUB, SUB), :] = east


def combine_kernel(
    fields, eofs, members, place_ref, got_a, got_b, basis, adj, proj, strip_own, coeff_own,
    combined, coeff_strip, strip, wide_strip, adj_strip, panel_in, proj_strip,
):
    ring_odd = place_ref[0] == 1
    lane = lane_grid()
    inner = lane & (SLOT - 1)
    pair = eofs // 2

    def got(at):
        first, second = got_a[at, :], got_b[at, :]
        return jnp.where(ring_odd, first, second), jnp.where(ring_odd, second, first)

    west_mask = inner < HALO
    east_mask = (inner >= STEPS) & (inner < STEPS + HALO)
    for t in range(3):
        for j in range(pair):
            west, east = got(pl.ds((t * pair + j) * SUB, SUB))
            for half in range(2):
                e = half * pair + j
                at = pl.ds(e * SUB, SUB)
                strip[t, at, :] = jnp.where(
                    west_mask, turn(west, -half * (SLOT // 2)), strip_own[t, at, :]
                )
                at = pl.ds((eofs + e) * SUB, SUB)
                strip[t, at, :] = jnp.where(
                    east_mask, turn(east, STEPS - half * (SLOT // 2)), strip_own[t, at, :]
                )
        at = pl.ds(2 * eofs * SUB, 4 * SUB)
        strip[t, at, :] = strip_own[t, at, :]
        west, east = got(pl.ds((3 * pair + t) * SUB, SUB))
        at = pl.ds(t * SUB, SUB)
        for k in range(4):
            for side, (cells, mask, shift) in enumerate(
                ((west, west_mask, 0), (east, east_mask, STEPS))
            ):
                mine = jnp.where(lane // SLOT == k, cells, 0.0)
                mine = mine + turn(mine, SLOT)
                mine = mine + turn(mine, 2 * SLOT)
                if shift:
                    mine = turn(mine, shift)
                if k < 3:
                    mine = time_step * mine
                coeff_strip[side, k, at, :] = jnp.where(mask, mine, coeff_own[side, k, at, :])
    strip_coefficients(coeff_strip, wide_strip, eofs)

    for g in range(3):
        rows = {}
        for w in range(WINDOW):
            t, y = place(w)
            rows[w] = strip[t, pl.ds(g * SUB * SUB + y, SUB, stride=SUB), :]
        rows = diffuse(rows, lambda k, w: wide_strip[k, w, pl.ds(g * SUB, SUB), :], True)
        for y in range(SUB):
            adj_strip[pl.ds(g * SUB * SUB + y, SUB, stride=SUB), :] = rows[y + STEPS]

    base = 3 * (pair + 1) * SUB
    levels = got_a.shape[0] - base
    west, east = got(pl.ds(base, levels))
    panel_in[...] = jnp.concatenate([west, east], axis=1).astype(jnp.bfloat16)
    count, depth = basis.shape[0], basis.shape[3]
    wide_lane = lax.broadcasted_iota(jnp.int32, (eofs * SUB, 2 * LANES), 1) & (LANES - 1)
    halo = jnp.zeros((eofs * SUB, 2 * LANES), jnp.float32)
    for f in range(fields):
        total = None
        for h in range(count):
            part = jnp.dot(
                basis[h, f], panel_in[pl.ds(h * depth, depth), :], preferred_element_type=jnp.float32
            )
            total = part if total is None else total + part
        halo = jnp.where(wide_lane // SLOT == f, total, halo)
    proj_strip[pl.ds(0, eofs * SUB), :] = halo[:, :LANES]
    proj_strip[pl.ds(eofs * SUB, eofs * SUB), :] = halo[:, LANES:]

    scores = [jnp.zeros((SUB, LANES), jnp.float32) for _ in range(members)]
    for f in range(fields):
        for e in range(eofs):
            at = pl.ds((f * eofs + e) * SUB, SUB)
            west = turn(adj_strip[pl.ds(e * SUB, SUB), :], -f * SLOT - HALO)
            east = turn(adj_strip[pl.ds((eofs + e) * SUB, SUB), :], LANES - STEPS - f * SLOT)
            cells = jnp.where(
                lane < STEPS, west, jnp.where(lane >= LANES - STEPS, east, adj[at, :])
            )
            for m in range(members):
                scores[m] = scores[m] + proj[m, at, :] * cells
    scores = [s / (members - 1) for s in scores]
    for i in range(fields * eofs):
        at = pl.ds(i * SUB, SUB)
        total = proj[0, at, :] * scores[0]
        for m in range(1, members):
            total = total + proj[m, at, :] * scores[m]
        combined[at, :] = total

    slot = inner // SUB
    packed = [jnp.zeros((SUB, LANES), jnp.float32) for _ in range(2 * eofs // 4)]
    for side in range(2):
        total = jnp.zeros((SUB, LANES), jnp.float32)
        for e in range(eofs):
            at = pl.ds((side * eofs + e) * SUB, SUB)
            cells = adj_strip[at, :]
            spread = turn(cells, -STEPS)
            for m in range(1, members):
                spread = jnp.where(slot == m, turn(cells, m * SUB - STEPS), spread)
            total = total + proj_strip[at, :] * spread
        total = total + turn(total, SLOT)
        total = (total + turn(total, 2 * SLOT)) / (members - 1)
        for e in range(eofs):
            i = side * eofs + e
            cells = proj_strip[pl.ds(i * SUB, SUB), :] * total
            cells = cells + turn(cells, -2 * SUB)
            cells = cells + turn(cells, -SUB)
            packed[i // 4] = jnp.where(slot == i % 4, turn(cells, (i % 4) * SUB), packed[i // 4])
    for j in range(len(packed)):
        combined[pl.ds((fields * eofs + j) * SUB, SUB), :] = packed[j]


def forward_kernel(
    fields, eofs, place_ref, own, from_a, from_b, coeff_main, coeff_strip,
    out, strip, strip_out, wide, wide_strip,
):
    odd = place_ref[1] == 1
    tile = tile_picker(own, from_a, from_b, odd)
    row = row_picker(own, from_a, from_b, odd)
    lane = lane_grid()
    inner = lane & (SLOT - 1)
    shifted = (lane + STEPS) & (LANES - 1)
    zero = jnp.zeros((SUB, LANES), jnp.float32)
    halo = (inner >= STEPS) & (inner < HALO)

    for k in range(4):
        for w in range(WINDOW):
            wide[k, w] = jnp.broadcast_to(coeff_main[k, pl.ds(w + 2, 1), :], (SUB, LANES))
    strip_coefficients(coeff_strip, wide_strip, eofs)

    for t in range(3):
        for e in range(eofs):
            west, east = zero, zero
            for f in range(fields):
                cells = tile(t, f * eofs + e)
                west = jnp.where(lane // SLOT == f, turn(cells, f * SLOT + HALO), west)
                east = jnp.where(
                    shifted // SLOT == f, turn(cells, f * SLOT - STEPS - LANES + HALO), east
                )
            for side, cells in enumerate((west, east)):
                i = side * eofs + e
                beyond = turn(tile(t, fields * eofs + i // 4), STEPS - (i % 4) * SUB)
                strip[t, pl.ds(i * SUB, SUB), :] = jnp.where(halo, beyond, cells)
        strip[t, pl.ds(2 * eofs * SUB, 4 * SUB), :] = jnp.zeros((4 * SUB, LANES), jnp.float32)

    for g in range(3):
        rows = {}
        for w in range(WINDOW):
            t, y = place(w)
            rows[w] = strip[t, pl.ds(g * SUB * SUB + y, SUB, stride=SUB), :]
        rows = diffuse(rows, lambda k, w: wide_strip[k, w, pl.ds(g * SUB, SUB), :], False)
        for y in range(SUB):
            strip_out[pl.ds(g * SUB * SUB + y, SUB, stride=SUB), :] = rows[y + STEPS]

    def group(g, carry):
        rows = {w: row(w, g) for w in range(WINDOW)}
        rows = diffuse(rows, lambda k, w: wide[k, w], False)
        for y in range(SUB):
            out[pl.ds(g * SUB * SUB + y, SUB, stride=SUB), :] = rows[y + STEPS]
        return carry

    lax.fori_loop(0, fields * eofs // SUB, group, 0)
    for f in range(fields):
        for e in range(eofs):
            at = pl.ds((f * eofs + e) * SUB, SUB)
            west = turn(strip_out[pl.ds(e * SUB, SUB), :], -f * SLOT - HALO)
            east = turn(strip_out[pl.ds((eofs + e) * SUB, SUB), :], LANES - STEPS - f * SLOT)
            out[at, :] = jnp.where(
                lane < STEPS, west, jnp.where(lane >= LANES - STEPS, east, out[at, :])
            )


def call(kernel, args, outs, scratch=(), flops=1_000_000):
    whole = pl.BlockSpec(memory_space=pltpu.VMEM)
    moved = sum(a.size * a.dtype.itemsize for a in list(args) + list(outs))
    return pl.pallas_call(
        kernel,
        in_specs=[pl.BlockSpec(memory_space=pltpu.SMEM)] + [whole] * (len(args) - 1),
        out_specs=[whole] * len(outs),
        out_shape=list(outs),
        scratch_shapes=list(scratch),
        compiler_params=pltpu.CompilerParams(vmem_limit_bytes=32 * 2**20),
        cost_estimate=pl.CostEstimate(flops=flops, bytes_accessed=moved, transcendentals=0),
    )(*args)


def per_device(panels, eof_basis, control, coefficients):
    members, fields, depth, row_count, _ = panels.shape
    _, eofs, _, col_count = control.shape
    count = lax.axis_size("gz")
    me = lax.axis_index("gz")
    ring = lax.axis_index("gx") * count + me
    where_am_i = jnp.stack([ring % 2, lax.axis_index("gy") % 2, me]).astype(jnp.int32)

    def columns(of):
        return lax.dynamic_slice_in_dim(panels, of * col_count, col_count, axis=4)

    arrived = [
        lax.ppermute(
            columns((me + s) % count), "gz", [(i, (i + s) % count) for i in range(count)]
        )
        for s in range(1, count)
    ]
    panel = columns(me)
    total_fields = fields * eofs
    own = jnp.concatenate(
        [
            control.reshape(total_fields * row_count, col_count),
            coefficients.reshape(4 * row_count, col_count),
        ]
    )
    from_a, from_b = swap_a(own, "gy"), swap_b(own, "gy", False)

    basis = eof_basis.transpose(0, 2, 1).reshape(fields, eofs, 1, count, depth, 1)
    basis = basis * jnp.eye(row_count, dtype=eof_basis.dtype)[:, None, None, :]
    basis = basis.transpose(3, 0, 1, 2, 4, 5).reshape(
        count, fields, eofs * row_count, depth * row_count
    )

    f32 = lambda *shape: jax.ShapeDtypeStruct(shape, jnp.float32)
    rows_sent = 3 * (eofs // 2 + 1) * row_count + count * depth * row_count
    sent_a, sent_b = call(
        functools.partial(pack_kernel, fields, eofs, members),
        [where_am_i, own, from_a, from_b, panel, *arrived],
        [f32(rows_sent, col_count)] * 2,
    )
    got_a, got_b = swap_a(sent_a, RING), swap_b(sent_b, RING, True)

    strip_rows = (2 * eofs + 4) * row_count
    adj, proj, strip, coeff_main, coeff_strip = call(
        functools.partial(main_kernel, fields, eofs, members),
        [where_am_i, own, from_a, from_b, basis, panel, *arrived],
        [
            f32(total_fields * row_count, col_count),
            f32(members, total_fields * row_count, col_count),
            f32(3, strip_rows, col_count),
            f32(4, 3 * row_count, col_count),
            f32(2, 4, 3 * row_count, col_count),
        ],
        [pltpu.VMEM((4, WINDOW, SUB, LANES), jnp.float32)],
        flops=20_000_000,
    )
    combined, coeff_strip = call(
        functools.partial(combine_kernel, fields, eofs, members),
        [where_am_i, got_a, got_b, basis, adj, proj, strip, coeff_strip],
        [
            f32(total_fields * row_count + 2 * eofs // 4 * row_count, col_count),
            f32(2, 4, 3 * row_count, col_count),
        ],
        [
            pltpu.VMEM((3, strip_rows, LANES), jnp.float32),
            pltpu.VMEM((4, WINDOW, 3 * SUB, LANES), jnp.float32),
            pltpu.VMEM((strip_rows, LANES), jnp.float32),
            pltpu.VMEM((count * depth * row_count, 2 * LANES), jnp.bfloat16),
            pltpu.VMEM((strip_rows, LANES), jnp.float32),
        ],
    )
    from_a, from_b = swap_a(combined, "gy"), swap_b(combined, "gy", False)
    (result,) = call(
        functools.partial(forward_kernel, fields, eofs),
        [where_am_i, combined, from_a, from_b, coeff_main, coeff_strip],
        [f32(total_fields * row_count, col_count)],
        [
            pltpu.VMEM((3, strip_rows, LANES), jnp.float32),
            pltpu.VMEM((strip_rows, LANES), jnp.float32),
            pltpu.VMEM((4, WINDOW, SUB, LANES), jnp.float32),
            pltpu.VMEM((4, WINDOW, 3 * SUB, LANES), jnp.float32),
        ],
    )
    return result.reshape(control.shape)


def solution(mesh):
    in_specs = (
        P(None, None, "gz", "gy", "gx"),
        P(),
        P(None, None, "gy", ("gx", "gz")),
        P(None, "gy", ("gx", "gz")),
    )
    out_specs = P(None, None, "gy", ("gx", "gz"))
    return jax.shard_map(
        per_device, mesh=mesh, in_specs=in_specs, out_specs=out_specs, check_vma=False
    )
```

time: 288 us -> 40.3 us (0.14)
  the two profiles are of different devices: /device:TPU:10 before, /device:TPU:16 now
where the time goes in v1:
time: 40.3 us; the launch traced here: 40 us
  Pallas kernels  16.2 us (40%)
  waiting for transfers between devices  11.9 us (30%)
  starting transfers between devices  8.09 us (20%)
  local copies, waits for them, and re-layouts  2.59 us (6%)
  other arithmetic  1.04 us (3%)
    pallas_call x4, Pallas kernels, call(): pl.pallas_call(kernel, in_specs=[pl.BlockSpec(memory_space=pltpu.SMEM)] +...  16.2 us
    ppermute x3, waiting for transfers between devices, swap_b(): return lax.ppermute(values, axes, pairs + [(j, i) for i, j in pairs])  6.2 us
    ppermute x3, waiting for transfers between devices, swap_a(): return lax.ppermute(values, axes, [(i, i ^ 1) for i in range(count)])  5.73 us
    ppermute x3, starting transfers between devices, swap_b(): return lax.ppermute(values, axes, pairs + [(j, i) for i, j in pairs])  4.23 us
    ppermute x3, starting transfers between devices, swap_a(): return lax.ppermute(values, axes, [(i, i ^ 1) for i in range(count)])  2.31 us
    ppermute x1, starting transfers between devices, per_device(): lax.ppermute(columns((me + s) % count), 'gz', [(i, (i + s) % count) for i...  1.56 us
    mul x5, local copies, waits for them, and re-layouts, per_device(): basis = basis * jnp.eye(row_count, dtype=eof_basis.dtype)[:, None, None, :]  1.39 us
    dynamic_slice x1, local copies, waits for them, and re-layouts, columns(): return lax.dynamic_slice_in_dim(panels, of * col_count, col_count, axis=4)  1.08 us
  transfers between devices with their start and end apart: 7, of which 5 were waited for; matrix products, arithmetic and copies ran while one was open for 6% of the time, Pallas kernels for 14%

profile of v1, /device:TPU:16, one launch (start us, length us, event | category | flops | bytes accessed | tf_op | source)
XLA Modules:
  0.0 40.0 jit_solution(4486431217443691125)
XLA Ops:
  0.0 0.0 copy-start
  0.0 1.1 %constant_dynamic-slice_fusion = (bf16[4,4,8,8,128]{4,3,2,1,0:T(8,128)(2,1)S(1)}, bf16[4,4,8,8,128]{4,3,2,1,0:T(8,128)(2,1)S(1)}) fusion(bf16[4,4,8,8,256]{4,3,2,1,0:T(8,128)(2,1)} %param.4, s32[]{:T(128)S(6)} %select_n.25, s32[]{:T(128)S(6)} %select_n.23), kind=kLoop, calls=%fused_computation.5 | loop fusion | bytes 1048584 | tf_op jit(solution)/shard_map/dynamic_slice | solution.py:429
  1.1 1.6 %collective-permute-start.2 = (bf16[4,4,8,8,128]{4,3,2,1,0:T(8,128)(2,1)S(1)}, bf16[4,4,8,8,128]{4,3,2,1,0:T(8,128)(2,1)S(1)}, u32[]{:S(2)}, u32[]{:S(2)}) collective-permute-start(bf16[4,4,8,8,128]{4,3,2,1,0:T(8,128)(2,1)S(1)} %get-tuple-element.23), channel_id=1, source_target_pairs={{0,1},{1,0},{2,3},{3,2},{4,5},{5,4},{6,7},{7,6},{8,9},{9,8},{10,11... | collective-permute-start | bytes 786440 | tf_op jit(solution)/shard_map/ppermute | solution.py:432
  2.6 0.9 %pad_maximum_fusion.own = f32[352,128]{1,0:T(8,128)S(1)} fusion(f32[32,128]{1,0:T(8,128)} %bitcast.17, f32[320,128]{1,0:T(8,128)} %bitcast.15), kind=kLoop, calls=%fused_computation | loop fusion | flops 45056 | bytes 360448 | tf_op jit(solution)/shard_map/concatenate | solution.py:439
  3.6 1.6 %collective-permute-start = (f32[352,128]{1,0:T(8,128)S(1)}, f32[352,128]{1,0:T(8,128)S(1)}, u32[]{:S(2)}, u32[]{:S(2)}) collective-permute-start(f32[352,128]{1,0:T(8,128)S(1)} %pad_maximum_fusion.own), channel_id=1, source_target_pairs={{0,2},{2,0},{4,6},{6,4},{1,3},{3,1},{5,7},{7,5},{8,10},{10,8},{12,... | collective-permute-start | bytes 540680 | tf_op jit(solution)/shard_map/ppermute | solution.py:28
  5.2 1.9 %collective-permute-start.1 = (f32[352,128]{1,0:T(8,128)S(1)}, f32[352,128]{1,0:T(8,128)S(1)}, u32[]{:S(2)}, u32[]{:S(2)}) collective-permute-start(f32[352,128]{1,0:T(8,128)S(1)} %pad_maximum_fusion.own), channel_id=1, source_target_pairs={{2,4},{4,2},{3,5},{5,3},{10,12},{12,10},{11,13},{13,11},{18,20},{2... | collective-permute-start | bytes 540680 | tf_op jit(solution)/shard_map/ppermute | solution.py:36
  7.2 0.0 copy-done
  7.2 0.1 copy.6
  7.3 0.1 copy.7
  7.4 0.3 mul.39
  7.7 0.8 %mul.40 = bf16[2,4,80,64]{3,2,1,0:T(8,128)(2,1)S(1)} reshape(bf16[2,4,10,8,8,8]{5,4,3,2,1,0:T(8,128)(2,1)S(1)} %mul.39) | data formatting | bytes 163840 | tf_op jit(solution)/shard_map/mul | solution.py:448
  8.6 0.1 mul.42
  8.7 0.1 pad_add_fusion.place_ref
  8.8 0.9 %collective-permute-done.from_a = f32[352,128]{1,0:T(8,128)S(1)} collective-permute-done((f32[352,128]{1,0:T(8,128)S(1)}, f32[352,128]{1,0:T(8,128)S(1)}, u32[]{:S(2)}, u32[]{:S(2)}) %collective-permute-start) | collective-permute-done | bytes 180256 | tf_op jit(solution)/shard_map/ppermute | solution.py:28
  9.7 3.2 %collective-permute-done.1.from_b = f32[352,128]{1,0:T(8,128)S(1)} collective-permute-done((f32[352,128]{1,0:T(8,128)S(1)}, f32[352,128]{1,0:T(8,128)S(1)}, u32[]{:S(2)}, u32[]{:S(2)}) %collective-permute-start.1) | collective-permute-done | bytes 180256 | tf_op jit(solution)/shard_map/ppermute | solution.py:36
  12.8 0.0 collective-permute-done.2.rest_0_
  12.9 1.0 %shard_map.46 = (f32[272,128]{1,0:T(8,128)S(1)}, f32[272,128]{1,0:T(8,128)S(1)}) custom-call(s32[3]{0:T(128)S(1)} %pad_add_fusion.place_ref, f32[352,128]{1,0:T(8,128)S(1)} %pad_maximum_fusion.own, f32[352,128]{1,0:T(8,128)S(1)} %collective-permute-done.from_a, f32[352,128]{1,0:T(8,128)S(1)} %collective-permute-done.1.from_b, ...), custom_call_target="tpu_custom_call" | custom-call | flops 1000000 | bytes 1343500 | tf_op jit(solution)/shard_map/pallas_call | solution.py:409
  13.8 0.6 %collective-permute-start.3 = (f32[272,128]{1,0:T(8,128)S(1)}, f32[272,128]{1,0:T(8,128)S(1)}, u32[]{:S(2)}, u32[]{:S(2)}) collective-permute-start(f32[272,128]{1,0:T(8,128)S(1)} %get-tuple-element.14), channel_id=1, source_target_pairs={{0,1},{1,0},{8,9},{9,8},{16,17},{17,16},{24,25},{25,24},{2,3},{3,2... | collective-permute-start | bytes 417800 | tf_op jit(solution)/shard_map/ppermute | solution.py:28
  14.4 0.1 collective-permute-start.4
  14.6 5.5 %shard_map.47 = (f32[320,128]{1,0:T(8,128)S(1)}, f32[4,320,128]{2,1,0:T(8,128)S(1)}, f32[3,192,128]{2,1,0:T(8,128)S(1)}, f32[4,24,128]{2,1,0:T(8,128)S(1)}, f32[2,4,24,128]{3,2,1,0:T(8,128)S(1)}) custom-call(s32[3]{0:T(128)S(1)} %pad_add_fusion.place_ref, f32[352,128]{1,0:T(8,128)S(1)} %pad_maximum_fusion.own, f32[352,128]{1,0:T(8,128)S(1)} %collective-permute-done.from_a, ...), custom_call_target="tpu_custom_call" | custom-call | flops 20000000 | bytes 2408460 | tf_op jit(solution)/shard_map/pallas_call | solution.py:409
  20.1 0.0 collective-permute-done.3.got_a
  20.1 1.1 %collective-permute-done.4.got_b = f32[272,128]{1,0:T(8,128)S(1)} collective-permute-done((f32[272,128]{1,0:T(8,128)S(1)}, f32[272,128]{1,0:T(8,128)S(1)}, u32[]{:S(2)}, u32[]{:S(2)}) %collective-permute-start.4) | collective-permute-done | bytes 139296 | tf_op jit(solution)/shard_map/ppermute | solution.py:36
  21.2 2.6 %shard_map.48 = (f32[360,128]{1,0:T(8,128)S(1)}, f32[2,4,24,128]{3,2,1,0:T(8,128)S(1)}) custom-call(s32[3]{0:T(128)S(1)} %pad_add_fusion.place_ref, f32[272,128]{1,0:T(8,128)S(1)} %collective-permute-done.3.got_a, f32[272,128]{1,0:T(8,128)S(1)} %collective-permute-done.4.got_b, bf16[2,4,80,64]{3,2,1,0:T(8,128)(2,1)S(1)} %broadcast_multiply_fusion.basis, ...), custom_call_target="tpu_custom_call" | custom-call | flops 1000000 | bytes 1855500 | tf_op jit(solution)/shard_map/pallas_call | solution.py:409
  23.8 0.1 collective-permute-start.5
  23.8 2.2 %collective-permute-start.6 = (f32[360,128]{1,0:T(8,128)S(1)}, f32[360,128]{1,0:T(8,128)S(1)}, u32[]{:S(2)}, u32[]{:S(2)}) collective-permute-start(f32[360,128]{1,0:T(8,128)S(1)} %get-tuple-element.20.own), channel_id=1, source_target_pairs={{2,4},{4,2},{3,5},{5,3},{10,12},{12,10},{11,13},{13,11},{18,20},{2... | collective-permute-start | bytes 552968 | tf_op jit(solution)/shard_map/ppermute | solution.py:36
  26.1 4.9 %collective-permute-done.5.from_a = f32[360,128]{1,0:T(8,128)S(1)} collective-permute-done((f32[360,128]{1,0:T(8,128)S(1)}, f32[360,128]{1,0:T(8,128)S(1)}, u32[]{:S(2)}, u32[]{:S(2)}) %collective-permute-start.5) | collective-permute-done | bytes 184352 | tf_op jit(solution)/shard_map/ppermute | solution.py:28
  30.9 1.9 %collective-permute-done.6.from_b = f32[360,128]{1,0:T(8,128)S(1)} collective-permute-done((f32[360,128]{1,0:T(8,128)S(1)}, f32[360,128]{1,0:T(8,128)S(1)}, u32[]{:S(2)}, u32[]{:S(2)}) %collective-permute-start.6) | collective-permute-done | bytes 184352 | tf_op jit(solution)/shard_map/ppermute | solution.py:36
  32.8 7.2 %shard_map.49 = f32[320,128]{1,0:T(8,128)} custom-call(s32[3]{0:T(128)S(1)} %pad_add_fusion.place_ref, f32[360,128]{1,0:T(8,128)S(1)} %get-tuple-element.20.own, f32[360,128]{1,0:T(8,128)S(1)} %collective-permute-done.5.from_a, f32[360,128]{1,0:T(8,128)S(1)} %collective-permute-done.6.from_b, f32[4,24,128]{2,1,0:T(8,128)S(1)} %get-tuple-element.21.coeff_main, ...), custom_call_target="tpu_custom_call" | custom-call | flops 1000000 | bytes 864268 | tf_op jit(solution)/shard_map/pallas_call | solution.py:409
  (3 shorter events, 0.0 us)
Async XLA Ops:
  0.0 7.2 %copy-start = (bf16[4,16,10]{1,0,2:T(4,128)(2,1)S(1)}, bf16[4,16,10]{1,0,2:T(4,128)(2,1)}, u32[]{:S(2)}) copy-start(bf16[4,16,10]{1,0,2:T(4,128)(2,1)} %param.5) | copy-start | bytes 3844
  1.1 11.8 %collective-permute-start.2 = (bf16[4,4,8,8,128]{4,3,2,1,0:T(8,128)(2,1)S(1)}, bf16[4,4,8,8,128]{4,3,2,1,0:T(8,128)(2,1)S(1)}, u32[]{:S(2)}, u32[]{:S(2)}) collective-permute-start(bf16[4,4,8,8,128]{4,3,2,1,0:T(8,128)(2,1)S(1)} %get-tuple-element.23), channel_id=1, source_target_pairs={{0,1},{1,0},{2,3},{3,2},{4,5},{5,4},{6,7},{7,6},{8,9},{9,8},{10,11... | collective-permute-start | bytes 786440 | tf_op jit(solution)/shard_map/ppermute | solution.py:432
  3.6 6.1 %collective-permute-start = (f32[352,128]{1,0:T(8,128)S(1)}, f32[352,128]{1,0:T(8,128)S(1)}, u32[]{:S(2)}, u32[]{:S(2)}) collective-permute-start(f32[352,128]{1,0:T(8,128)S(1)} %pad_maximum_fusion.own), channel_id=1, source_target_pairs={{0,2},{2,0},{4,6},{6,4},{1,3},{3,1},{5,7},{7,5},{8,10},{10,8},{12,... | collective-permute-start | bytes 540680 | tf_op jit(solution)/shard_map/ppermute | solution.py:28
  5.2 7.6 %collective-permute-start.1 = (f32[352,128]{1,0:T(8,128)S(1)}, f32[352,128]{1,0:T(8,128)S(1)}, u32[]{:S(2)}, u32[]{:S(2)}) collective-permute-start(f32[352,128]{1,0:T(8,128)S(1)} %pad_maximum_fusion.own), channel_id=1, source_target_pairs={{2,4},{4,2},{3,5},{5,3},{10,12},{12,10},{11,13},{13,11},{18,20},{2... | collective-permute-start | bytes 540680 | tf_op jit(solution)/shard_map/ppermute | solution.py:36
  13.8 6.3 %collective-permute-start.3 = (f32[272,128]{1,0:T(8,128)S(1)}, f32[272,128]{1,0:T(8,128)S(1)}, u32[]{:S(2)}, u32[]{:S(2)}) collective-permute-start(f32[272,128]{1,0:T(8,128)S(1)} %get-tuple-element.14), channel_id=1, source_target_pairs={{0,1},{1,0},{8,9},{9,8},{16,17},{17,16},{24,25},{25,24},{2,3},{3,2... | collective-permute-start | bytes 417800 | tf_op jit(solution)/shard_map/ppermute | solution.py:28
  14.4 6.8 %collective-permute-start.4 = (f32[272,128]{1,0:T(8,128)S(1)}, f32[272,128]{1,0:T(8,128)S(1)}, u32[]{:S(2)}, u32[]{:S(2)}) collective-permute-start(f32[272,128]{1,0:T(8,128)S(1)} %get-tuple-element.15), channel_id=1, source_target_pairs={{1,8},{9,16},{17,24},{25,0},{8,1},{16,9},{24,17},{0,25},{3,10},{11... | collective-permute-start | bytes 417800 | tf_op jit(solution)/shard_map/ppermute | solution.py:36
  23.8 7.2 %collective-permute-start.5 = (f32[360,128]{1,0:T(8,128)S(1)}, f32[360,128]{1,0:T(8,128)S(1)}, u32[]{:S(2)}, u32[]{:S(2)}) collective-permute-start(f32[360,128]{1,0:T(8,128)S(1)} %get-tuple-element.20.own), channel_id=1, source_target_pairs={{0,2},{2,0},{4,6},{6,4},{1,3},{3,1},{5,7},{7,5},{8,10},{10,8},{12,... | collective-permute-start | bytes 552968 | tf_op jit(solution)/shard_map/ppermute | solution.py:28
  23.8 9.0 %collective-permute-start.6 = (f32[360,128]{1,0:T(8,128)S(1)}, f32[360,128]{1,0:T(8,128)S(1)}, u32[]{:S(2)}, u32[]{:S(2)}) collective-permute-start(f32[360,128]{1,0:T(8,128)S(1)} %get-tuple-element.20.own), channel_id=1, source_target_pairs={{2,4},{4,2},{3,5},{5,3},{10,12},{12,10},{11,13},{13,11},{18,20},{2... | collective-permute-start | bytes 552968 | tf_op jit(solution)/shard_map/ppermute | solution.py:36

commit v2 on v1

--- a/solution.py
+++ b/solution.py
@@ -44,27 +44,42 @@
     return lax.broadcasted_iota(jnp.int32, (SUB, LANES), 1)
 
 
-def diffuse(rows, coeff, adjoint):
+def diffuse(read, write, coeff, groups, first, second, adjoint):
+    state, spare = None, first
     for step in range(STEPS):
         low, high = step, WINDOW - 1 - step
-        moved = {}
-        if adjoint:
-            seen = {w: coeff(3, w) * rows[w] for w in range(low, high + 1)}
-        else:
-            seen = rows
-        south = None
+
+        def fetch(w):
+            if state is None:
+                return [read(w, g) for g in range(groups)]
+            return [state[w, pl.ds(g * SUB, SUB), :] for g in range(groups)]
+
+        here, seen, south = fetch(low), None, None
         for w in range(low, high):
-            east_diff = turn(seen[w], -1) - seen[w]
-            north_diff = seen[w + 1] - seen[w]
-            cross = coeff(1, w)
-            flux_north = cross * east_diff + coeff(2, w) * north_diff
-            if w > low:
-                flux_east = coeff(0, w) * east_diff + cross * north_diff
-                div = flux_east - turn(flux_east, 1) + (flux_north - south)
-                moved[w] = rows[w] + (div if adjoint else coeff(3, w) * div)
-            south = flux_north
-        rows = moved
-    return rows
+            k = [coeff(i, w) for i in range(4)]
+            north = fetch(w + 1)
+            if adjoint:
+                if seen is None:
+                    seen = [k[3][g] * here[g] for g in range(groups)]
+                area = coeff(3, w + 1)
+                seen_north = [area[g] * north[g] for g in range(groups)]
+            else:
+                seen, seen_north = here, north
+            flux = []
+            for g in range(groups):
+                east_diff = turn(seen[g], -1) - seen[g]
+                north_diff = seen_north[g] - seen[g]
+                flux.append(k[1][g] * east_diff + k[2][g] * north_diff)
+                if w > low:
+                    flux_east = k[0][g] * east_diff + k[1][g] * north_diff
+                    div = flux_east - turn(flux_east, 1) + (flux[g] - south[g])
+                    moved = here[g] + (div if adjoint else k[3][g] * div)
+                    if step == STEPS - 1:
+                        write(w, g, moved)
+                    else:
+                        spare[w, pl.ds(g * SUB, SUB), :] = moved
+            here, seen, south = north, seen_north, flux
+        state, spare = spare, (second if spare is first else first)
 
 
 def tile_picker(own, from_a, from_b, odd):
@@ -152,7 +167,8 @@
 def main_kernel(
     fields, eofs, members, place_ref, own, from_a, from_b, basis, panel, *rest
 ):
-    arrived, (adj, proj, strip, coeff_main, coeff_strip, wide) = rest[:-6], rest[-6:]
+    arrived = rest[:-8]
+    adj, proj, strip, coeff_main, coeff_strip, wide, first, second = rest[-8:]
     odd, me = place_ref[1] == 1, place_ref[2]
     tile = tile_picker(own, from_a, from_b, odd)
     row = row_picker(own, from_a, from_b, odd)
@@ -194,14 +210,12 @@
         for w in range(WINDOW):
             wide[k, w] = jnp.broadcast_to(coeff_main[k, pl.ds(w + 2, 1), :], (SUB, LANES))
 
-    def group(g, carry):
-        rows = {w: row(w, g) for w in range(WINDOW)}
-        rows = diffuse(rows, lambda k, w: wide[k, w], True)
-        for y in range(SUB):
-            adj[pl.ds(g * SUB * SUB + y, SUB, stride=SUB), :] = rows[y + STEPS]
-        return carry
-
-    lax.fori_loop(0, fields * eofs // SUB, group, 0)
+    groups = fields * eofs // SUB
+
+    def write(w, g, cells):
+        adj[pl.ds(g * SUB * SUB + w - STEPS, SUB, stride=SUB), :] = cells
+
+    diffuse(row, write, lambda k, w: [wide[k, w]] * groups, groups, first, second, True)
 
     for t in range(3):
         for e in range(eofs):
@@ -228,9 +242,23 @@
             wide_strip[k, w, pl.ds(2 * SUB, SUB), :] = east
 
 
+def diffuse_strip(strip, out, wide_strip, first, second, adjoint):
+    def read(w, g):
+        t, y = place(w)
+        return strip[t, pl.ds(g * SUB * SUB + y, SUB, stride=SUB), :]
+
+    def write(w, g, cells):
+        out[pl.ds(g * SUB * SUB + w - STEPS, SUB, stride=SUB), :] = cells
+
+    def coeff(k, w):
+        return [wide_strip[k, w, pl.ds(g * SUB, SUB), :] for g in range(3)]
+
+    diffuse(read, write, coeff, 3, first, second, adjoint)
+
+
 def combine_kernel(
     fields, eofs, members, place_ref, got_a, got_b, basis, adj, proj, strip_own, coeff_own,
-    combined, coeff_strip, strip, wide_strip, adj_strip, panel_in, proj_strip,
+    combined, coeff_strip, strip, wide_strip, adj_strip, panel_in, proj_strip, first, second,
 ):
     ring_odd = place_ref[0] == 1
     lane = lane_grid()
@@ -274,14 +302,7 @@
                 coeff_strip[side, k, at, :] = jnp.where(mask, mine, coeff_own[side, k, at, :])
     strip_coefficients(coeff_strip, wide_strip, eofs)
 
-    for g in range(3):
-        rows = {}
-        for w in range(WINDOW):
-            t, y = place(w)
-            rows[w] = strip[t, pl.ds(g * SUB * SUB + y, SUB, stride=SUB), :]
-        rows = diffuse(rows, lambda k, w: wide_strip[k, w, pl.ds(g * SUB, SUB), :], True)
-        for y in range(SUB):
-            adj_strip[pl.ds(g * SUB * SUB + y, SUB, stride=SUB), :] = rows[y + STEPS]
+    diffuse_strip(strip, adj_strip, wide_strip, first, second, True)
 
     base = 3 * (pair + 1) * SUB
     levels = got_a.shape[0] - base
@@ -345,7 +366,7 @@
 
 def forward_kernel(
     fields, eofs, place_ref, own, from_a, from_b, coeff_main, coeff_strip,
-    out, strip, strip_out, wide, wide_strip,
+    out, strip, strip_out, wide, wide_strip, first, second,
 ):
     odd = place_ref[1] == 1
     tile = tile_picker(own, from_a, from_b, odd)
@@ -376,23 +397,13 @@
                 strip[t, pl.ds(i * SUB, SUB), :] = jnp.where(halo, beyond, cells)
         strip[t, pl.ds(2 * eofs * SUB, 4 * SUB), :] = jnp.zeros((4 * SUB, LANES), jnp.float32)
 
-    for g in range(3):
-        rows = {}
-        for w in range(WINDOW):
-            t, y = place(w)
-            rows[w] = strip[t, pl.ds(g * SUB * SUB + y, SUB, stride=SUB), :]
-        rows = diffuse(rows, lambda k, w: wide_strip[k, w, pl.ds(g * SUB, SUB), :], False)
-        for y in range(SUB):
-            strip_out[pl.ds(g * SUB * SUB + y, SUB, stride=SUB), :] = rows[y + STEPS]
-
-    def group(g, carry):
-        rows = {w: row(w, g) for w in range(WINDOW)}
-        rows = diffuse(rows, lambda k, w: wide[k, w], False)
-        for y in range(SUB):
-            out[pl.ds(g * SUB * SUB + y, SUB, stride=SUB), :] = rows[y + STEPS]
-        return carry
-
-    lax.fori_loop(0, fields * eofs // SUB, group, 0)
+    diffuse_strip(strip, strip_out, wide_strip, first, second, False)
+    groups = fields * eofs // SUB
+
+    def write(w, g, cells):
+        out[pl.ds(g * SUB * SUB + w - STEPS, SUB, stride=SUB), :] = cells
+
+    diffuse(row, write, lambda k, w: [wide[k, w]] * groups, groups, first, second, False)
     for f in range(fields):
         for e in range(eofs):
             at = pl.ds((f * eofs + e) * SUB, SUB)
@@ -470,7 +481,8 @@
             f32(4, 3 * row_count, col_count),
             f32(2, 4, 3 * row_count, col_count),
         ],
-        [pltpu.VMEM((4, WINDOW, SUB, LANES), jnp.float32)],
+        [pltpu.VMEM((4, WINDOW, SUB, LANES), jnp.float32)]
+        + [pltpu.VMEM((WINDOW, total_fields, LANES), jnp.float32)] * 2,
         flops=20_000_000,
     )
     combined, coeff_strip = call(
@@ -486,7 +498,8 @@
             pltpu.VMEM((strip_rows, LANES), jnp.float32),
             pltpu.VMEM((count * depth * row_count, 2 * LANES), jnp.bfloat16),
             pltpu.VMEM((strip_rows, LANES), jnp.float32),
-        ],
+        ]
+        + [pltpu.VMEM((WINDOW, 3 * SUB, LANES), jnp.float32)] * 2,
     )
     from_a, from_b = swap_a(combined, "gy"), swap_b(combined, "gy", False)
     (result,) = call(
@@ -498,7 +511,8 @@
             pltpu.VMEM((strip_rows, LANES), jnp.float32),
             pltpu.VMEM((4, WINDOW, SUB, LANES), jnp.float32),
             pltpu.VMEM((4, WINDOW, 3 * SUB, LANES), jnp.float32),
-        ],
+        ]
+        + [pltpu.VMEM((WINDOW, total_fields, LANES), jnp.float32)] * 2,
     )
     return result.reshape(control.shape)
 

time: 40.3 us -> 37.1 us (0.921)
  Pallas kernels: 16.2 us -> 9.83 us
  waiting for transfers between devices: 11.9 us -> 15.1 us
    pallas_call x4, Pallas kernels: 16.2 us -> 9.83 us  [call(): pl.pallas_call(kernel, in_specs=[pl.BlockSpec(memory_space=pltpu.SMEM)] +...]
    ppermute x3, waiting for transfers between devices: 5.73 us -> 8.38 us  [swap_a(): return lax.ppermute(values, axes, [(i, i ^ 1) for i in range(count)])]
    ppermute x3, waiting for transfers between devices: 6.2 us -> 6.75 us  [swap_b(): return lax.ppermute(values, axes, pairs + [(j, i) for i, j in pairs])]
  transfers between devices with their start and end apart: 7 -> 7, of which waited for: 5 -> 6; matrix products, arithmetic and copies ran while one was open for 6% -> 7% of each run, Pallas kernels for 14% -> 6%
where the time goes in v2:
time: 37.1 us; the launch traced here: 36.8 us
  waiting for transfers between devices  15.1 us (41%)
  Pallas kernels  9.83 us (26%)
  starting transfers between devices  8.1 us (22%)
  local copies, waits for them, and re-layouts  2.59 us (7%)
  other arithmetic  1.04 us (3%)
    pallas_call x4, Pallas kernels, call(): pl.pallas_call(kernel, in_specs=[pl.BlockSpec(memory_space=pltpu.SMEM)] +...  9.83 us
    ppermute x3, waiting for transfers between devices, swap_a(): return lax.ppermute(values, axes, [(i, i ^ 1) for i in range(count)])  8.38 us
    ppermute x3, waiting for transfers between devices, swap_b(): return lax.ppermute(values, axes, pairs + [(j, i) for i, j in pairs])  6.75 us
    ppermute x3, starting transfers between devices, swap_b(): return lax.ppermute(values, axes, pairs + [(j, i) for i, j in pairs])  4.23 us
    ppermute x3, starting transfers between devices, swap_a(): return lax.ppermute(values, axes, [(i, i ^ 1) for i in range(count)])  2.31 us
    ppermute x1, starting transfers between devices, per_device(): lax.ppermute(columns((me + s) % count), 'gz', [(i, (i + s) % count) for i...  1.56 us
    mul x5, local copies, waits for them, and re-layouts, per_device(): basis = basis * jnp.eye(row_count, dtype=eof_basis.dtype)[:, None, None, :]  1.39 us
    dynamic_slice x1, local copies, waits for them, and re-layouts, columns(): return lax.dynamic_slice_in_dim(panels, of * col_count, col_count, axis=4)  1.08 us
  transfers between devices with their start and end apart: 7, of which 6 were waited for; matrix products, arithmetic and copies ran while one was open for 7% of the time, Pallas kernels for 6%

profile of v2, /device:TPU:16, one launch (start us, length us, event | category | flops | bytes accessed | tf_op | source)
XLA Modules:
  0.0 36.8 jit_solution(10884294182898205996)
XLA Ops:
  0.0 0.0 copy-start
  0.0 1.1 %constant_dynamic-slice_fusion = (bf16[4,4,8,8,128]{4,3,2,1,0:T(8,128)(2,1)S(1)}, bf16[4,4,8,8,128]{4,3,2,1,0:T(8,128)(2,1)S(1)}) fusion(bf16[4,4,8,8,256]{4,3,2,1,0:T(8,128)(2,1)} %param.4, s32[]{:T(128)S(6)} %select_n.25, s32[]{:T(128)S(6)} %select_n.23), kind=kLoop, calls=%fused_computation.5 | loop fusion | bytes 1048584 | tf_op jit(solution)/shard_map/dynamic_slice | solution.py:440
  1.1 1.6 %collective-permute-start.2 = (bf16[4,4,8,8,128]{4,3,2,1,0:T(8,128)(2,1)S(1)}, bf16[4,4,8,8,128]{4,3,2,1,0:T(8,128)(2,1)S(1)}, u32[]{:S(2)}, u32[]{:S(2)}) collective-permute-start(bf16[4,4,8,8,128]{4,3,2,1,0:T(8,128)(2,1)S(1)} %get-tuple-element.23), channel_id=1, source_target_pairs={{0,1},{1,0},{2,3},{3,2},{4,5},{5,4},{6,7},{7,6},{8,9},{9,8},{10,11... | collective-permute-start | bytes 786440 | tf_op jit(solution)/shard_map/ppermute | solution.py:443
  2.6 0.9 %pad_maximum_fusion.own = f32[352,128]{1,0:T(8,128)S(1)} fusion(f32[32,128]{1,0:T(8,128)} %bitcast.17, f32[320,128]{1,0:T(8,128)} %bitcast.15), kind=kLoop, calls=%fused_computation | loop fusion | flops 45056 | bytes 360448 | tf_op jit(solution)/shard_map/concatenate | solution.py:450
  3.6 1.6 %collective-permute-start = (f32[352,128]{1,0:T(8,128)S(1)}, f32[352,128]{1,0:T(8,128)S(1)}, u32[]{:S(2)}, u32[]{:S(2)}) collective-permute-start(f32[352,128]{1,0:T(8,128)S(1)} %pad_maximum_fusion.own), channel_id=1, source_target_pairs={{0,2},{2,0},{4,6},{6,4},{1,3},{3,1},{5,7},{7,5},{8,10},{10,8},{12,... | collective-permute-start | bytes 540680 | tf_op jit(solution)/shard_map/ppermute | solution.py:28
  5.2 1.9 %collective-permute-start.1 = (f32[352,128]{1,0:T(8,128)S(1)}, f32[352,128]{1,0:T(8,128)S(1)}, u32[]{:S(2)}, u32[]{:S(2)}) collective-permute-start(f32[352,128]{1,0:T(8,128)S(1)} %pad_maximum_fusion.own), channel_id=1, source_target_pairs={{2,4},{4,2},{3,5},{5,3},{10,12},{12,10},{11,13},{13,11},{18,20},{2... | collective-permute-start | bytes 540680 | tf_op jit(solution)/shard_map/ppermute | solution.py:36
  7.2 0.0 copy-done
  7.2 0.1 copy.6
  7.3 0.1 copy.7
  7.4 0.3 mul.39
  7.7 0.8 %mul.40 = bf16[2,4,80,64]{3,2,1,0:T(8,128)(2,1)S(1)} reshape(bf16[2,4,10,8,8,8]{5,4,3,2,1,0:T(8,128)(2,1)S(1)} %mul.39) | data formatting | bytes 163840 | tf_op jit(solution)/shard_map/mul | solution.py:459
  8.6 0.1 mul.42
  8.7 0.1 pad_add_fusion.place_ref
  8.8 0.9 %collective-permute-done.from_a = f32[352,128]{1,0:T(8,128)S(1)} collective-permute-done((f32[352,128]{1,0:T(8,128)S(1)}, f32[352,128]{1,0:T(8,128)S(1)}, u32[]{:S(2)}, u32[]{:S(2)}) %collective-permute-start) | collective-permute-done | bytes 180256 | tf_op jit(solution)/shard_map/ppermute | solution.py:28
  9.7 3.2 %collective-permute-done.1.from_b = f32[352,128]{1,0:T(8,128)S(1)} collective-permute-done((f32[352,128]{1,0:T(8,128)S(1)}, f32[352,128]{1,0:T(8,128)S(1)}, u32[]{:S(2)}, u32[]{:S(2)}) %collective-permute-start.1) | collective-permute-done | bytes 180256 | tf_op jit(solution)/shard_map/ppermute | solution.py:36
  12.8 0.0 collective-permute-done.2.rest_0_
  12.9 1.0 %shard_map.46 = (f32[272,128]{1,0:T(8,128)S(1)}, f32[272,128]{1,0:T(8,128)S(1)}) custom-call(s32[3]{0:T(128)S(1)} %pad_add_fusion.place_ref, f32[352,128]{1,0:T(8,128)S(1)} %pad_maximum_fusion.own, f32[352,128]{1,0:T(8,128)S(1)} %collective-permute-done.from_a, f32[352,128]{1,0:T(8,128)S(1)} %collective-permute-done.1.from_b, ...), custom_call_target="tpu_custom_call" | custom-call | flops 1000000 | bytes 1343500 | tf_op jit(solution)/shard_map/pallas_call | solution.py:420
  13.8 0.6 %collective-permute-start.3 = (f32[272,128]{1,0:T(8,128)S(1)}, f32[272,128]{1,0:T(8,128)S(1)}, u32[]{:S(2)}, u32[]{:S(2)}) collective-permute-start(f32[272,128]{1,0:T(8,128)S(1)} %get-tuple-element.14), channel_id=1, source_target_pairs={{0,1},{1,0},{8,9},{9,8},{16,17},{17,16},{24,25},{25,24},{2,3},{3,2... | collective-permute-start | bytes 417800 | tf_op jit(solution)/shard_map/ppermute | solution.py:28
  14.4 0.1 collective-permute-start.4
  14.6 2.3 %shard_map.47 = (f32[320,128]{1,0:T(8,128)S(1)}, f32[4,320,128]{2,1,0:T(8,128)S(1)}, f32[3,192,128]{2,1,0:T(8,128)S(1)}, f32[4,24,128]{2,1,0:T(8,128)S(1)}, f32[2,4,24,128]{3,2,1,0:T(8,128)S(1)}) custom-call(s32[3]{0:T(128)S(1)} %pad_add_fusion.place_ref, f32[352,128]{1,0:T(8,128)S(1)} %pad_maximum_fusion.own, f32[352,128]{1,0:T(8,128)S(1)} %collective-permute-done.from_a, ...), custom_call_target="tpu_custom_call" | custom-call | flops 20000000 | bytes 2408460 | tf_op jit(solution)/shard_map/pallas_call | solution.py:420
  16.9 2.7 %collective-permute-done.3.got_a = f32[272,128]{1,0:T(8,128)S(1)} collective-permute-done((f32[272,128]{1,0:T(8,128)S(1)}, f32[272,128]{1,0:T(8,128)S(1)}, u32[]{:S(2)}, u32[]{:S(2)}) %collective-permute-start.3) | collective-permute-done | bytes 139296 | tf_op jit(solution)/shard_map/ppermute | solution.py:28
  19.5 1.7 %collective-permute-done.4.got_b = f32[272,128]{1,0:T(8,128)S(1)} collective-permute-done((f32[272,128]{1,0:T(8,128)S(1)}, f32[272,128]{1,0:T(8,128)S(1)}, u32[]{:S(2)}, u32[]{:S(2)}) %collective-permute-start.4) | collective-permute-done | bytes 139296 | tf_op jit(solution)/shard_map/ppermute | solution.py:36
  21.2 2.6 %shard_map.48 = (f32[360,128]{1,0:T(8,128)S(1)}, f32[2,4,24,128]{3,2,1,0:T(8,128)S(1)}) custom-call(s32[3]{0:T(128)S(1)} %pad_add_fusion.place_ref, f32[272,128]{1,0:T(8,128)S(1)} %collective-permute-done.3.got_a, f32[272,128]{1,0:T(8,128)S(1)} %collective-permute-done.4.got_b, bf16[2,4,80,64]{3,2,1,0:T(8,128)(2,1)S(1)} %broadcast_multiply_fusion.basis, ...), custom_call_target="tpu_custom_call" | custom-call | flops 1000000 | bytes 1855500 | tf_op jit(solution)/shard_map/pallas_call | solution.py:420
  23.8 0.1 collective-permute-start.5
  23.9 2.2 %collective-permute-start.6 = (f32[360,128]{1,0:T(8,128)S(1)}, f32[360,128]{1,0:T(8,128)S(1)}, u32[]{:S(2)}, u32[]{:S(2)}) collective-permute-start(f32[360,128]{1,0:T(8,128)S(1)} %get-tuple-element.20.own), channel_id=1, source_target_pairs={{2,4},{4,2},{3,5},{5,3},{10,12},{12,10},{11,13},{13,11},{18,20},{2... | collective-permute-start | bytes 552968 | tf_op jit(solution)/shard_map/ppermute | solution.py:36
  26.1 4.9 %collective-permute-done.5.from_a = f32[360,128]{1,0:T(8,128)S(1)} collective-permute-done((f32[360,128]{1,0:T(8,128)S(1)}, f32[360,128]{1,0:T(8,128)S(1)}, u32[]{:S(2)}, u32[]{:S(2)}) %collective-permute-start.5) | collective-permute-done | bytes 184352 | tf_op jit(solution)/shard_map/ppermute | solution.py:28
  31.0 1.9 %collective-permute-done.6.from_b = f32[360,128]{1,0:T(8,128)S(1)} collective-permute-done((f32[360,128]{1,0:T(8,128)S(1)}, f32[360,128]{1,0:T(8,128)S(1)}, u32[]{:S(2)}, u32[]{:S(2)}) %collective-permute-start.6) | collective-permute-done | bytes 184352 | tf_op jit(solution)/shard_map/ppermute | solution.py:36
  32.9 3.9 %shard_map.49 = f32[320,128]{1,0:T(8,128)} custom-call(s32[3]{0:T(128)S(1)} %pad_add_fusion.place_ref, f32[360,128]{1,0:T(8,128)S(1)} %get-tuple-element.20.own, f32[360,128]{1,0:T(8,128)S(1)} %collective-permute-done.5.from_a, f32[360,128]{1,0:T(8,128)S(1)} %collective-permute-done.6.from_b, f32[4,24,128]{2,1,0:T(8,128)S(1)} %get-tuple-element.21.coeff_main, ...), custom_call_target="tpu_custom_call" | custom-call | flops 1000000 | bytes 864268 | tf_op jit(solution)/shard_map/pallas_call | solution.py:420
  (3 shorter events, 0.0 us)
Async XLA Ops:
  0.0 7.2 %copy-start = (bf16[4,16,10]{1,0,2:T(4,128)(2,1)S(1)}, bf16[4,16,10]{1,0,2:T(4,128)(2,1)}, u32[]{:S(2)}) copy-start(bf16[4,16,10]{1,0,2:T(4,128)(2,1)} %param.5) | copy-start | bytes 3844
  1.1 11.8 %collective-permute-start.2 = (bf16[4,4,8,8,128]{4,3,2,1,0:T(8,128)(2,1)S(1)}, bf16[4,4,8,8,128]{4,3,2,1,0:T(8,128)(2,1)S(1)}, u32[]{:S(2)}, u32[]{:S(2)}) collective-permute-start(bf16[4,4,8,8,128]{4,3,2,1,0:T(8,128)(2,1)S(1)} %get-tuple-element.23), channel_id=1, source_target_pairs={{0,1},{1,0},{2,3},{3,2},{4,5},{5,4},{6,7},{7,6},{8,9},{9,8},{10,11... | collective-permute-start | bytes 786440 | tf_op jit(solution)/shard_map/ppermute | solution.py:443
  3.6 6.1 %collective-permute-start = (f32[352,128]{1,0:T(8,128)S(1)}, f32[352,128]{1,0:T(8,128)S(1)}, u32[]{:S(2)}, u32[]{:S(2)}) collective-permute-start(f32[352,128]{1,0:T(8,128)S(1)} %pad_maximum_fusion.own), channel_id=1, source_target_pairs={{0,2},{2,0},{4,6},{6,4},{1,3},{3,1},{5,7},{7,5},{8,10},{10,8},{12,... | collective-permute-start | bytes 540680 | tf_op jit(solution)/shard_map/ppermute | solution.py:28
  5.2 7.6 %collective-permute-start.1 = (f32[352,128]{1,0:T(8,128)S(1)}, f32[352,128]{1,0:T(8,128)S(1)}, u32[]{:S(2)}, u32[]{:S(2)}) collective-permute-start(f32[352,128]{1,0:T(8,128)S(1)} %pad_maximum_fusion.own), channel_id=1, source_target_pairs={{2,4},{4,2},{3,5},{5,3},{10,12},{12,10},{11,13},{13,11},{18,20},{2... | collective-permute-start | bytes 540680 | tf_op jit(solution)/shard_map/ppermute | solution.py:36
  13.8 5.7 %collective-permute-start.3 = (f32[272,128]{1,0:T(8,128)S(1)}, f32[272,128]{1,0:T(8,128)S(1)}, u32[]{:S(2)}, u32[]{:S(2)}) collective-permute-start(f32[272,128]{1,0:T(8,128)S(1)} %get-tuple-element.14), channel_id=1, source_target_pairs={{0,1},{1,0},{8,9},{9,8},{16,17},{17,16},{24,25},{25,24},{2,3},{3,2... | collective-permute-start | bytes 417800 | tf_op jit(solution)/shard_map/ppermute | solution.py:28
  14.4 6.8 %collective-permute-start.4 = (f32[272,128]{1,0:T(8,128)S(1)}, f32[272,128]{1,0:T(8,128)S(1)}, u32[]{:S(2)}, u32[]{:S(2)}) collective-permute-start(f32[272,128]{1,0:T(8,128)S(1)} %get-tuple-element.15), channel_id=1, source_target_pairs={{1,8},{9,16},{17,24},{25,0},{8,1},{16,9},{24,17},{0,25},{3,10},{11... | collective-permute-start | bytes 417800 | tf_op jit(solution)/shard_map/ppermute | solution.py:36
  23.8 7.2 %collective-permute-start.5 = (f32[360,128]{1,0:T(8,128)S(1)}, f32[360,128]{1,0:T(8,128)S(1)}, u32[]{:S(2)}, u32[]{:S(2)}) collective-permute-start(f32[360,128]{1,0:T(8,128)S(1)} %get-tuple-element.20.own), channel_id=1, source_target_pairs={{0,2},{2,0},{4,6},{6,4},{1,3},{3,1},{5,7},{7,5},{8,10},{10,8},{12,... | collective-permute-start | bytes 552968 | tf_op jit(solution)/shard_map/ppermute | solution.py:28
  23.9 9.0 %collective-permute-start.6 = (f32[360,128]{1,0:T(8,128)S(1)}, f32[360,128]{1,0:T(8,128)S(1)}, u32[]{:S(2)}, u32[]{:S(2)}) collective-permute-start(f32[360,128]{1,0:T(8,128)S(1)} %get-tuple-element.20.own), channel_id=1, source_target_pairs={{2,4},{4,2},{3,5},{5,3},{10,12},{12,10},{11,13},{13,11},{18,20},{2... | collective-permute-start | bytes 552968 | tf_op jit(solution)/shard_map/ppermute | solution.py:36

commit v3 on v2

v3 whole, which is shorter than its diff:
```python
import functools

import jax
import jax.numpy as jnp
from jax import lax
from jax.experimental import pallas as pl
from jax.experimental.pallas import tpu as pltpu
from jax.sharding import PartitionSpec as P

STEPS = 6
LANES = 128
SUB = 8
RING = ("gx", "gz")

time_step = 0.09

WINDOW = SUB + 2 * STEPS
HALO = 2 * STEPS
SLOT = 32


def turn(cells, shift):
    return pltpu.roll(cells, shift % LANES, 1)


def swap_a(values, axes):
    count = lax.axis_size(axes)
    return lax.ppermute(values, axes, [(i, i ^ 1) for i in range(count)])


def swap_b(values, axes, closed):
    count = lax.axis_size(axes)
    pairs = [(i, i + 1) for i in range(1, count - 1, 2)]
    if closed:
        pairs.append((count - 1, 0))
    return lax.ppermute(values, axes, pairs + [(j, i) for i, j in pairs])


def place(w):
    return (w + 2) // SUB, (w + 2) % SUB


def lane_grid():
    return lax.broadcasted_iota(jnp.int32, (SUB, LANES), 1)


def diffuse(read, write, coeff, groups, first, second, adjoint):
    state, spare = None, first
    for step in range(STEPS):
        low, high = step, WINDOW - 1 - step

        def fetch(w):
            if state is None:
                return [read(w, g) for g in range(groups)]
            return [state[w, pl.ds(g * SUB, SUB), :] for g in range(groups)]

        here, seen, south = fetch(low), None, None
        for w in range(low, high):
            k = [coeff(i, w) for i in range(4)]
            north = fetch(w + 1)
            if adjoint:
                if seen is None:
                    seen = [k[3][g] * here[g] for g in range(groups)]
                area = coeff(3, w + 1)
                seen_north = [area[g] * north[g] for g in range(groups)]
            else:
                seen, seen_north = here, north
            flux = []
            for g in range(groups):
                east_diff = turn(seen[g], -1) - seen[g]
                north_diff = seen_north[g] - seen[g]
                flux.append(k[1][g] * east_diff + k[2][g] * north_diff)
                if w > low:
                    flux_east = k[0][g] * east_diff + k[1][g] * north_diff
                    div = flux_east - turn(flux_east, 1) + (flux[g] - south[g])
                    moved = here[g] + (div if adjoint else k[3][g] * div)
                    if step == STEPS - 1:
                        write(w, g, moved)
                    else:
                        spare[w, pl.ds(g * SUB, SUB), :] = moved
            here, seen, south = north, seen_north, flux
        state, spare = spare, (second if spare is first else first)


def read_pair(ref, pair):
    cells = ref[pl.ds(pair * 2 * SUB, 2 * SUB), :].astype(jnp.float32)
    return cells[:SUB], cells[SUB:]


def write_pair(ref, pair, first, second):
    cells = jnp.concatenate([first, second], axis=0).astype(jnp.bfloat16)
    ref[pl.ds(pair * 2 * SUB, 2 * SUB), :] = cells


def split(cells):
    high = cells.astype(jnp.bfloat16).astype(jnp.float32)
    return high, cells - high


def encode_rows(cells, sub):
    high, low = split(cells)
    edge = SUB - STEPS
    to_north = jnp.where(sub < STEPS, high, pltpu.roll(low, STEPS, 0))
    to_south = jnp.where(sub >= edge, high, pltpu.roll(low, edge, 0))
    return to_north, to_south


def decode_rows(from_a, from_b, odd, sub, pair):
    edge = SUB - STEPS
    north, south = [], []
    for a, b in zip(read_pair(from_a, pair), read_pair(from_b, pair)):
        above, below = jnp.where(odd, a, b), jnp.where(odd, b, a)
        north.append(above + jnp.where(sub >= STEPS, pltpu.roll(above, STEPS, 0), 0.0))
        south.append(below + jnp.where(sub < edge, pltpu.roll(below, edge, 0), 0.0))
    return north, south


def send_rows_kernel(place_ref, control, coefficients, out_a, out_b):
    odd = place_ref[1] == 1
    sub = lax.broadcasted_iota(jnp.int32, (SUB, LANES), 0)
    first = control.shape[0] // SUB
    count = first + coefficients.shape[0] // SUB

    def tile(i):
        if i < first:
            return control[pl.ds(i * SUB, SUB), :]
        return coefficients[pl.ds((i - first) * SUB, SUB), :]

    put_rows(out_a, out_b, [tile(i) for i in range(count)], odd, sub)


def put_rows(out_a, out_b, tiles, odd, sub):
    for pair in range(len(tiles) // 2):
        north, south = zip(*[encode_rows(t, sub) for t in tiles[2 * pair : 2 * pair + 2]])
        write_pair(out_a, pair, *[jnp.where(odd, n, s) for n, s in zip(north, south)])
        write_pair(out_b, pair, *[jnp.where(odd, s, n) for n, s in zip(north, south)])


def strip_tiles(fields, eofs, tile, lane):
    pair = eofs // 2
    zero = jnp.zeros((SUB, LANES), jnp.float32)
    west_out, east_out = [], []
    at = lane & (SLOT // 2 - 1)
    for j in range(pair):
        west, east = zero, zero
        for half in range(2):
            for f in range(fields):
                cells = tile(f * eofs + half * pair + j)
                start = f * SLOT + half * (SLOT // 2)
                mask = (lane >= start) & (lane < start + HALO)
                west = jnp.where(mask, turn(cells, start), west)
                east = jnp.where(mask, turn(cells, start + HALO - LANES), east)
        high, low = split(west)
        west_out.append(jnp.where(at < HALO, high, turn(low, HALO)))
        high, low = split(east)
        east_out.append(jnp.where(at < HALO, high, turn(low, 4)))
    west, east = zero, zero
    for k in range(4):
        cells = tile(fields * eofs + k)
        start = k * SLOT
        mask = (lane >= start) & (lane < start + HALO)
        west = jnp.where(mask, turn(cells, start), west)
        east = jnp.where(mask, turn(cells, start + HALO - LANES), east)
    for cells, out in ((west, west_out), (east, east_out)):
        high, low = split(cells)
        out.append(high + turn(low, SLOT // 2))
    return west_out, east_out


def own_strips_kernel(fields, eofs, members, control, coefficients, *rest):
    panels, (west, east, edges) = rest[:-3], rest[-3:]
    lane = lane_grid()
    total = fields * eofs

    def tile(i):
        if i < total:
            return control[pl.ds(i * SUB, SUB), :]
        return coefficients[pl.ds((i - total) * SUB, SUB), :]

    for ref, tiles in zip((west, east), strip_tiles(fields, eofs, tile, lane)):
        for pair in range(len(tiles) // 2):
            write_pair(ref, pair, *tiles[2 * pair : 2 * pair + 2])

    depth = panels[0].shape[2] * SUB
    column = lax.broadcasted_iota(jnp.int32, (LANES, 2 * LANES), 0)
    target = lax.broadcasted_iota(jnp.int32, (LANES, 2 * LANES), 1)
    west_ok = (target < LANES) & (column < STEPS)
    east_ok = (target >= LANES) & (column >= LANES - STEPS)
    offset = jnp.where(
        west_ok,
        target - column,
        jnp.where(east_ok, target - LANES - column + LANES - STEPS, -1),
    )
    for s, block in enumerate(panels):
        total = jnp.zeros((depth, 2 * LANES), jnp.float32)
        for m in range(members):
            for f in range(fields):
                pick = (offset == f * SLOT + m * SUB).astype(jnp.bfloat16)
                total += jnp.dot(
                    block[m, f].reshape(depth, LANES), pick, preferred_element_type=jnp.float32
                )
        total = total.astype(jnp.bfloat16)
        edges[s, 0] = total[:, :LANES]
        edges[s, 1] = total[:, LANES:]


def pack_kernel(fields, eofs, place_ref, from_a, from_b, west, east, *rest):
    panel_edges, (out_a, out_b, north, south) = rest[:-4], rest[-4:]
    ring_odd, odd = place_ref[0] == 1, place_ref[1] == 1
    lane = lane_grid()
    sub = lax.broadcasted_iota(jnp.int32, (SUB, LANES), 0)
    for pair in range((fields * eofs + 4) // 2):
        above, below = decode_rows(from_a, from_b, odd, sub, pair)
        at = pl.ds(pair * 2 * SUB, 2 * SUB)
        north[at, :] = jnp.concatenate(above, axis=0)
        south[at, :] = jnp.concatenate(below, axis=0)

    def put(pair, mine_west, mine_east):
        write_pair(out_a, pair, *[jnp.where(ring_odd, w, e) for w, e in zip(mine_west, mine_east)])
        write_pair(out_b, pair, *[jnp.where(ring_odd, e, w) for w, e in zip(mine_west, mine_east)])

    pairs = (eofs // 2 + 1) // 2
    for t, ref in ((0, north), (2, south)):
        tiles = strip_tiles(fields, eofs, lambda i: ref[pl.ds(i * SUB, SUB), :], lane)
        for j in range(pairs):
            put(t * pairs + j, tiles[0][2 * j : 2 * j + 2], tiles[1][2 * j : 2 * j + 2])
    for j in range(pairs):
        put(pairs + j, read_pair(west, j), read_pair(east, j))
    for edges in panel_edges:
        for j in range(edges.shape[2] // (2 * SUB)):
            put(3 * pairs + j, read_pair(edges.at[0, 0], j), read_pair(edges.at[0, 1], j))


def own_columns(fields, eofs, tile, strip, t, lane):
    shifted = (lane + STEPS) & (LANES - 1)
    zero = jnp.zeros((SUB, LANES), jnp.float32)
    for e in range(eofs):
        west, east = zero, zero
        for f in range(fields):
            cells = tile(f * eofs + e)
            west = jnp.where(lane // SLOT == f, turn(cells, f * SLOT + HALO), west)
            east = jnp.where(
                shifted // SLOT == f, turn(cells, f * SLOT - STEPS - LANES + HALO), east
            )
        strip[t, pl.ds(e * SUB, SUB), :] = west
        strip[t, pl.ds((eofs + e) * SUB, SUB), :] = east
    strip[t, pl.ds(2 * eofs * SUB, 4 * SUB), :] = jnp.zeros((4 * SUB, LANES), jnp.float32)


def main_kernel(
    fields, eofs, control, coefficients, north, south,
    adj, strip, coeff_main, coeff_strip, wide, first, second,
):
    lane = lane_grid()
    inner = lane & (SLOT - 1)
    shifted = (lane + STEPS) & (LANES - 1)
    zero = jnp.zeros((SUB, LANES), jnp.float32)
    total = fields * eofs

    def tile(t, i):
        if t != 1:
            return (north, south)[t // 2][pl.ds(i * SUB, SUB), :]
        if i < total:
            return control[pl.ds(i * SUB, SUB), :]
        return coefficients[pl.ds((i - total) * SUB, SUB), :]

    for k in range(4):
        for t in range(3):
            cells = tile(t, total + k)
            if k < 3:
                cells = time_step * cells
            at = pl.ds(t * SUB, SUB)
            coeff_main[k, at, :] = cells
            west, east = zero, zero
            for f in range(fields):
                start = f * SLOT
                west = jnp.where(lane // SLOT == f, turn(cells, start + HALO), west)
                east = jnp.where(
                    shifted // SLOT == f, turn(cells, start - STEPS - LANES + HALO), east
                )
            coeff_strip[0, k, at, :] = jnp.where((inner >= HALO) & (inner < 2 * HALO), west, 0.0)
            coeff_strip[1, k, at, :] = jnp.where((shifted & (SLOT - 1)) < HALO, east, 0.0)
    main_coefficients(coeff_main, wide)
    diffuse_main(control, north, south, adj, wide, first, second, True)
    for t in range(3):
        own_columns(fields, eofs, lambda i: tile(t, i), strip, t, lane)


def project_kernel(fields, eofs, members, place_ref, basis, panel, *rest):
    arrived, proj = rest[:-1], rest[-1]
    me = place_ref[2]
    blocks = (panel,) + arrived
    count = len(blocks)
    depth = panel.shape[2] * SUB
    for f in range(fields):
        total = None
        for s, block in enumerate(blocks):
            cells = jnp.concatenate(
                [block[m, f].reshape(depth, LANES) for m in range(members)], axis=1
            )
            part = jnp.dot(
                basis[lax.rem(me - s + count, count), f], cells, preferred_element_type=jnp.float32
            )
            total = part if total is None else total + part
        for m in range(members):
            proj[m, pl.ds(f * eofs * SUB, eofs * SUB), :] = total[:, m * LANES : (m + 1) * LANES]


def main_coefficients(coeff_main, wide):
    for k in range(4):
        for w in range(WINDOW):
            wide[k, w] = jnp.broadcast_to(coeff_main[k, pl.ds(w + 2, 1), :], (SUB, LANES))


def strip_coefficients(coeff_strip, wide_strip, eofs):
    sub = lax.broadcasted_iota(jnp.int32, (SUB, LANES), 0)
    for k in range(4):
        for w in range(WINDOW):
            west = jnp.broadcast_to(coeff_strip[0, k, pl.ds(w + 2, 1), :], (SUB, LANES))
            east = jnp.broadcast_to(coeff_strip[1, k, pl.ds(w + 2, 1), :], (SUB, LANES))
            wide_strip[k, w, pl.ds(0, SUB), :] = west
            wide_strip[k, w, pl.ds(SUB, SUB), :] = jnp.where(sub < eofs - SUB, west, east)
            wide_strip[k, w, pl.ds(2 * SUB, SUB), :] = east


def diffuse_main(own, north, south, out, wide, first, second, adjoint):
    groups = own.shape[0] // (SUB * SUB)

    def read(w, g):
        t, y = place(w)
        return (north, own, south)[t][pl.ds(g * SUB * SUB + y, SUB, stride=SUB), :]

    def write(w, g, cells):
        out[pl.ds(g * SUB * SUB + w - STEPS, SUB, stride=SUB), :] = cells

    diffuse(read, write, lambda k, w: [wide[k, w]] * groups, groups, first, second, adjoint)


def diffuse_strip(strip, out, wide_strip, first, second, adjoint):
    def read(w, g):
        t, y = place(w)
        return strip[t, pl.ds(g * SUB * SUB + y, SUB, stride=SUB), :]

    def write(w, g, cells):
        out[pl.ds(g * SUB * SUB + w - STEPS, SUB, stride=SUB), :] = cells

    def coeff(k, w):
        return [wide_strip[k, w, pl.ds(g * SUB, SUB), :] for g in range(3)]

    diffuse(read, write, coeff, 3, first, second, adjoint)


def combine_kernel(fields, eofs, members, place_ref, got_a, got_b, *rest):
    (
        basis, adj, proj, strip_own, coeff_own,
        out_a, out_b, combined, halo_out, coeff_strip,
        strip, wide_strip, adj_strip, panel_in, proj_strip, first, second,
    ) = rest[-17:]
    panel_parts = rest[:-17]
    ring_odd, odd, me = place_ref[0] == 1, place_ref[1] == 1, place_ref[2]
    lane = lane_grid()
    sub = lax.broadcasted_iota(jnp.int32, (SUB, LANES), 0)
    inner = lane & (SLOT - 1)
    pair = eofs // 2

    def got(j):
        found = zip(read_pair(got_a, j), read_pair(got_b, j))
        sides = [(jnp.where(ring_odd, a, b), jnp.where(ring_odd, b, a)) for a, b in found]
        return zip(*sides)

    west_mask = inner < HALO
    east_mask = (inner >= STEPS) & (inner < STEPS + HALO)
    at16 = lane & (SLOT // 2 - 1)
    pairs = (pair + 1) // 2
    for t in range(3):
        west_tiles, east_tiles = [], []
        for j in range(pairs):
            west, east = got(t * pairs + j)
            west_tiles += west
            east_tiles += east
        for j in range(pair):
            west, east = west_tiles[j], east_tiles[j]
            west = west + jnp.where((at16 >= HALO - 4) & (at16 < HALO), turn(west, -4), 0.0)
            east = east + jnp.where(at16 < 4, turn(east, -HALO), 0.0)
            for half in range(2):
                e = half * pair + j
                at = pl.ds(e * SUB, SUB)
                strip[t, at, :] = jnp.where(
                    west_mask, turn(west, -half * (SLOT // 2)), strip_own[t, at, :]
                )
                at = pl.ds((eofs + e) * SUB, SUB)
                strip[t, at, :] = jnp.where(
                    east_mask, turn(east, STEPS - half * (SLOT // 2)), strip_own[t, at, :]
                )
        at = pl.ds(2 * eofs * SUB, 4 * SUB)
        strip[t, at, :] = strip_own[t, at, :]
        at = pl.ds(t * SUB, SUB)
        for side, (cells, mask) in enumerate(
            ((west_tiles[pair], west_mask), (east_tiles[pair], east_mask))
        ):
            cells = cells + turn(cells, -(SLOT // 2))
            for k in range(4):
                mine = jnp.where(lane // SLOT == k, cells, 0.0)
                mine = mine + turn(mine, SLOT)
                mine = mine + turn(mine, 2 * SLOT)
                if side == 1:
                    mine = turn(mine, STEPS)
                if k < 3:
                    mine = time_step * mine
                coeff_strip[side, k, at, :] = jnp.where(mask, mine, coeff_own[side, k, at, :])
    strip_coefficients(coeff_strip, wide_strip, eofs)
    diffuse_strip(strip, adj_strip, wide_strip, first, second, True)

    count, depth = basis.shape[0], basis.shape[3]
    if len(panel_parts) == 2:
        edges, far = panel_parts
        near_west, near_east, far = edges[1, 0], edges[1, 1], far[...]
        at = pl.ds(3 * pairs * 2 * SUB, depth)
        a, b = got_a[at, :], got_b[at, :]
        wests = [jnp.where(ring_odd, near_east, far), jnp.where(ring_odd, a, b)]
        easts = [jnp.where(ring_odd, far, near_west), jnp.where(ring_odd, b, a)]
    else:
        wests = [ref[...] for ref in panel_parts[:count]]
        easts = [ref[...] for ref in panel_parts[count:]]
    for s in range(count):
        panel_in[s] = jnp.concatenate([wests[s], easts[s]], axis=1)
    wide_lane = lax.broadcasted_iota(jnp.int32, (eofs * SUB, 2 * LANES), 1) & (LANES - 1)
    halo = jnp.zeros((eofs * SUB, 2 * LANES), jnp.float32)
    for f in range(fields):
        total = None
        for s in range(count):
            part = jnp.dot(
                basis[lax.rem(me + s, count), f], panel_in[s], preferred_element_type=jnp.float32
            )
            total = part if total is None else total + part
        halo = jnp.where(wide_lane // SLOT == f, total, halo)
    proj_strip[pl.ds(0, eofs * SUB), :] = halo[:, :LANES]
    proj_strip[pl.ds(eofs * SUB, eofs * SUB), :] = halo[:, LANES:]

    scores = [jnp.zeros((SUB, LANES), jnp.float32) for _ in range(members)]
    for f in range(fields):
        for e in range(eofs):
            at = pl.ds((f * eofs + e) * SUB, SUB)
            west = turn(adj_strip[pl.ds(e * SUB, SUB), :], -f * SLOT - HALO)
            east = turn(adj_strip[pl.ds((eofs + e) * SUB, SUB), :], LANES - STEPS - f * SLOT)
            cells = jnp.where(
                lane < STEPS, west, jnp.where(lane >= LANES - STEPS, east, adj[at, :])
            )
            for m in range(members):
                scores[m] = scores[m] + proj[m, at, :] * cells
    scores = [s / (members - 1) for s in scores]
    tiles = []
    for i in range(fields * eofs):
        at = pl.ds(i * SUB, SUB)
        total = proj[0, at, :] * scores[0]
        for m in range(1, members):
            total = total + proj[m, at, :] * scores[m]
        combined[at, :] = total
        tiles.append(total)

    slot = inner // SUB
    packed = [jnp.zeros((SUB, LANES), jnp.float32) for _ in range(2 * eofs // 4)]
    for side in range(2):
        total = jnp.zeros((SUB, LANES), jnp.float32)
        for e in range(eofs):
            at = pl.ds((side * eofs + e) * SUB, SUB)
            cells = adj_strip[at, :]
            spread = turn(cells, -STEPS)
            for m in range(1, members):
                spread = jnp.where(slot == m, turn(cells, m * SUB - STEPS), spread)
            total = total + proj_strip[at, :] * spread
        total = total + turn(total, SLOT)
        total = (total + turn(total, 2 * SLOT)) / (members - 1)
        for e in range(eofs):
            i = side * eofs + e
            cells = proj_strip[pl.ds(i * SUB, SUB), :] * total
            cells = cells + turn(cells, -2 * SUB)
            cells = cells + turn(cells, -SUB)
            packed[i // 4] = jnp.where(slot == i % 4, turn(cells, (i % 4) * SUB), packed[i // 4])
    for j, cells in enumerate(packed):
        halo_out[pl.ds(j * SUB, SUB), :] = cells
    tiles += packed
    if len(tiles) % 2:
        tiles.append(jnp.zeros((SUB, LANES), jnp.float32))
    put_rows(out_a, out_b, tiles, odd, sub)


def beyond_columns(eofs, packed, strip, t, lane):
    inner = lane & (SLOT - 1)
    mask = (inner >= STEPS) & (inner < HALO)
    for i in range(2 * eofs):
        cells = turn(packed[pl.ds(i // 4 * SUB, SUB), :], STEPS - (i % 4) * SUB)
        at = pl.ds(i * SUB, SUB)
        strip[t, at, :] = jnp.where(mask, cells, strip[t, at, :])


def before_forward_kernel(fields, eofs, own, halo, coeff_main, coeff_strip, wide, wide_strip, strip):
    lane = lane_grid()
    main_coefficients(coeff_main, wide)
    strip_coefficients(coeff_strip, wide_strip, eofs)
    own_columns(fields, eofs, lambda i: own[pl.ds(i * SUB, SUB), :], strip, 0, lane)
    beyond_columns(eofs, halo, strip, 0, lane)


def forward_kernel(
    fields, eofs, place_ref, own, from_a, from_b, wide, wide_strip, strip_own,
    out, north, south, strip, strip_out, first, second,
):
    odd = place_ref[1] == 1
    lane = lane_grid()
    sub = lax.broadcasted_iota(jnp.int32, (SUB, LANES), 0)
    total = fields * eofs
    for pair in range(north.shape[0] // (2 * SUB)):
        above, below = decode_rows(from_a, from_b, odd, sub, pair)
        at = pl.ds(pair * 2 * SUB, 2 * SUB)
        north[at, :] = jnp.concatenate(above, axis=0)
        south[at, :] = jnp.concatenate(below, axis=0)
    for t, ref in ((0, north), (2, south)):
        own_columns(fields, eofs, lambda i: ref[pl.ds(i * SUB, SUB), :], strip, t, lane)
        beyond_columns(eofs, ref.at[pl.ds(total * SUB, 2 * eofs // 4 * SUB)], strip, t, lane)
    strip[1] = strip_own[0]
    diffuse_strip(strip, strip_out, wide_strip, first, second, False)
    diffuse_main(own, north, south, out, wide, first, second, False)
    for f in range(fields):
        for e in range(eofs):
            at = pl.ds((f * eofs + e) * SUB, SUB)
            west = turn(strip_out[pl.ds(e * SUB, SUB), :], -f * SLOT - HALO)
            east = turn(strip_out[pl.ds((eofs + e) * SUB, SUB), :], LANES - STEPS - f * SLOT)
            out[at, :] = jnp.where(
                lane < STEPS, west, jnp.where(lane >= LANES - STEPS, east, out[at, :])
            )


def call(kernel, args, outs, scratch=(), flops=1_000_000):
    whole = pl.BlockSpec(memory_space=pltpu.VMEM)
    scalars = pl.BlockSpec(memory_space=pltpu.SMEM)
    moved = sum(a.size * a.dtype.itemsize for a in list(args) + list(outs))
    return pl.pallas_call(
        kernel,
        in_specs=[scalars if a.dtype == jnp.int32 else whole for a in args],
        out_specs=[whole] * len(outs),
        out_shape=list(outs),
        scratch_shapes=[pltpu.VMEM(*s) for s in scratch],
        compiler_params=pltpu.CompilerParams(vmem_limit_bytes=24 * 2**20),
        cost_estimate=pl.CostEstimate(flops=flops, bytes_accessed=moved, transcendentals=0),
    )(*args)


def panel_edges_apart(edges, count, me):
    groups = lax.axis_size("gx")
    wests, easts = [], []
    for s in range(count):
        for side, into in ((1, wests), (0, easts)):
            pairs = []
            for group in range(groups):
                for held in range(count):
                    tile = (held - s) % count
                    if side == 1:
                        to = group + (tile == 0)
                    else:
                        to = group - (tile == count - 1)
                    pairs.append((group * count + held, to % groups * count + tile))
            ahead = (-s - 1) if side == 1 else (1 - s)
            into.append(lax.ppermute(edges[ahead % count, side], RING, pairs))
    return wests + easts


def per_device(panels, eof_basis, control, coefficients):
    members, fields, depth, row_count, _ = panels.shape
    _, eofs, _, col_count = control.shape
    count = lax.axis_size("gz")
    me = lax.axis_index("gz")
    ring = lax.axis_index("gx") * count + me
    where_am_i = jnp.stack([ring % 2, lax.axis_index("gy") % 2, me]).astype(jnp.int32)
    total = fields * eofs
    rows = total * row_count
    control_in = control.reshape(rows, col_count)
    coeff_in = coefficients.reshape(4 * row_count, col_count)
    f32 = lambda *shape: jax.ShapeDtypeStruct(shape, jnp.float32)
    bf16 = lambda *shape: jax.ShapeDtypeStruct(shape, jnp.bfloat16)

    def columns(of):
        return lax.dynamic_slice_in_dim(panels, of * col_count, col_count, axis=4)

    tiles = [columns((me + s) % count) for s in range(count)]
    arrived = [
        lax.ppermute(tiles[s], "gz", [(i, (i + s) % count) for i in range(count)])
        for s in range(1, count)
    ]

    sent_a, sent_b = call(
        send_rows_kernel,
        [where_am_i, control_in, coeff_in],
        [bf16(rows + 4 * row_count, col_count)] * 2,
    )
    from_a, from_b = swap_a(sent_a, "gy"), swap_b(sent_b, "gy", False)

    strip_sent = (eofs // 2 + 1) * row_count
    west, east, edges = call(
        functools.partial(own_strips_kernel, fields, eofs, members),
        [control_in, coeff_in, *tiles],
        [bf16(strip_sent, col_count)] * 2 + [bf16(count, 2, depth * row_count, col_count)],
    )
    if count == 2:
        groups = lax.axis_size("gx")
        pairs = [(2 * g, (g + 1) % groups * 2) for g in range(groups)]
        pairs += [(2 * g + 1, (g - 1) % groups * 2 + 1) for g in range(groups)]
        far = lax.ppermute(jnp.where(me == 1, edges[1, 0], edges[1, 1]), RING, pairs)
        panel_sent, panel_parts = [edges], [edges, far]
    else:
        panel_sent, panel_parts = [], panel_edges_apart(edges, count, me)

    basis = eof_basis.transpose(0, 2, 1).reshape(fields, eofs, 1, count, depth, 1)
    basis = basis * jnp.eye(row_count, dtype=eof_basis.dtype)[:, None, None, :]
    basis = basis.transpose(3, 0, 1, 2, 4, 5).reshape(
        count, fields, eofs * row_count, depth * row_count
    )

    sent_a, sent_b, north, south = call(
        functools.partial(pack_kernel, fields, eofs),
        [where_am_i, from_a, from_b, west, east, *panel_sent],
        [bf16(3 * strip_sent + len(panel_sent) * depth * row_count, col_count)] * 2
        + [f32(rows + 4 * row_count, col_count)] * 2,
    )
    got_a, got_b = swap_a(sent_a, RING), swap_b(sent_b, RING, True)

    strip_rows = (2 * eofs + 4) * row_count
    main_scratch = [((WINDOW, total, LANES), jnp.float32)] * 2
    strip_scratch = [((WINDOW, 3 * SUB, LANES), jnp.float32)] * 2
    adj, strip, coeff_main, coeff_strip = call(
        functools.partial(main_kernel, fields, eofs),
        [control_in, coeff_in, north, south],
        [
            f32(rows, col_count),
            f32(3, strip_rows, col_count),
            f32(4, 3 * row_count, col_count),
            f32(2, 4, 3 * row_count, col_count),
        ],
        [((4, WINDOW, SUB, LANES), jnp.float32)] + main_scratch,
        flops=20_000_000,
    )
    (proj,) = call(
        functools.partial(project_kernel, fields, eofs, members),
        [where_am_i, basis, tiles[0], *arrived],
        [f32(members, rows, col_count)],
        flops=20_000_000,
    )
    packed = 2 * eofs // 4
    sent_a, sent_b, combined, halo, coeff_strip = call(
        functools.partial(combine_kernel, fields, eofs, members),
        [where_am_i, got_a, got_b, *panel_parts, basis, adj, proj, strip, coeff_strip],
        [bf16((total + packed + 1) // 2 * 2 * row_count, col_count)] * 2
        + [
            f32(rows, col_count),
            f32(packed * row_count, col_count),
            f32(2, 4, 3 * row_count, col_count),
        ],
        [
            ((3, strip_rows, LANES), jnp.float32),
            ((4, WINDOW, 3 * SUB, LANES), jnp.float32),
            ((strip_rows, LANES), jnp.float32),
            ((count, depth * row_count, 2 * LANES), jnp.bfloat16),
            ((2 * eofs * row_count, LANES), jnp.float32),
        ]
        + strip_scratch,
    )
    from_a, from_b = swap_a(sent_a, "gy"), swap_b(sent_b, "gy", False)
    wide, wide_strip, strip = call(
        functools.partial(before_forward_kernel, fields, eofs),
        [combined, halo, coeff_main, coeff_strip],
        [
            f32(4, WINDOW, SUB, LANES),
            f32(4, WINDOW, 3 * SUB, LANES),
            f32(1, strip_rows, LANES),
        ],
        flops=20_000_000,
    )
    (result,) = call(
        functools.partial(forward_kernel, fields, eofs),
        [where_am_i, combined, from_a, from_b, wide, wide_strip, strip],
        [f32(rows, col_count)],
        [((sent_a.shape[0], LANES), jnp.float32)] * 2
        + [((3, strip_rows, LANES), jnp.float32), ((strip_rows, LANES), jnp.float32)]
        + main_scratch,
    )
    return result.reshape(control.shape)


def solution(mesh):
    in_specs = (
        P(None, None, "gz", "gy", "gx"),
        P(),
        P(None, None, "gy", ("gx", "gz")),
        P(None, "gy", ("gx", "gz")),
    )
    out_specs = P(None, None, "gy", ("gx", "gz"))
    return jax.shard_map(
        per_device, mesh=mesh, in_specs=in_specs, out_specs=out_specs, check_vma=False
    )
```

time: 37.1 us -> 33 us (0.89)
  waiting for transfers between devices: 15.1 us -> 9.09 us
  local copies, waits for them, and re-layouts: 2.59 us -> 4.27 us
  Pallas kernels: 9.83 us -> 11.3 us
  other arithmetic: 1.04 us -> 0.1 us
    ppermute x3, waiting for transfers between devices: 8.38 us -> 3.43 us  [swap_a(): return lax.ppermute(values, axes, [(i, i ^ 1) for i in range(count)])]
    unnamed x3 -> x11, local copies, waits for them, and re-layouts: 0.12 us -> 1.76 us
    pallas_call x4 -> x8, Pallas kernels: 9.83 us -> 11.3 us  [call(): pl.pallas_call(kernel, in_specs=[scalars if a.dtype == jnp.int32 else who...]
    ppermute x3, waiting for transfers between devices: 6.75 us -> 5.65 us  [swap_b(): return lax.ppermute(values, axes, pairs + [(j, i) for i, j in pairs])]
    concatenate x1 -> x0, other arithmetic: 0.95 us -> none  [per_device(): jnp.concatenate([control.reshape(total_fields * row_count, col_count), co...]
    ppermute x3, starting transfers between devices: 4.23 us -> 3.83 us  [swap_b(): return lax.ppermute(values, axes, pairs + [(j, i) for i, j in pairs])]
    ppermute x1 -> x2, starting transfers between devices: 1.56 us -> 1.61 us  [the longest x1 1.56 us: per_device(): lax.ppermute(tiles[s], 'gz', [(i, (i + s) % count) for i in range(count)])]
  transfers between devices with their start and end apart: 7 -> 8, of which waited for: 6 -> 5; matrix products, arithmetic and copies ran while one was open for 7% -> 5% of each run, Pallas kernels for 6% -> 15%
where the time goes in v3:
time: 33 us; the launch traced here: 32.7 us
  Pallas kernels  11.3 us (34%)
  waiting for transfers between devices  9.09 us (28%)
  starting transfers between devices  7.76 us (24%)
  local copies, waits for them, and re-layouts  4.27 us (13%)
    pallas_call x8, Pallas kernels, call(): pl.pallas_call(kernel, in_specs=[scalars if a.dtype == jnp.int32 else who...  11.3 us
    ppermute x3, waiting for transfers between devices, swap_b(): return lax.ppermute(values, axes, pairs + [(j, i) for i, j in pairs])  5.65 us
    ppermute x3, starting transfers between devices, swap_b(): return lax.ppermute(values, axes, pairs + [(j, i) for i, j in pairs])  3.83 us
    ppermute x3, waiting for transfers between devices, swap_a(): return lax.ppermute(values, axes, [(i, i ^ 1) for i in range(count)])  3.43 us
    ppermute x3, starting transfers between devices, swap_a(): return lax.ppermute(values, axes, [(i, i ^ 1) for i in range(count)])  2.31 us
    unnamed x11, local copies, waits for them, and re-layouts  1.76 us
    ppermute x1, starting transfers between devices, per_device(): lax.ppermute(tiles[s], 'gz', [(i, (i + s) % count) for i in range(count)])  1.56 us
    mul x5, local copies, waits for them, and re-layouts, per_device(): basis = basis * jnp.eye(row_count, dtype=eof_basis.dtype)[:, None, None, :]  1.37 us
  transfers between devices with their start and end apart: 8, of which 5 were waited for; matrix products, arithmetic and copies ran while one was open for 5% of the time, Pallas kernels for 15%

profile of v3, /device:TPU:16, one launch (start us, length us, event | category | flops | bytes accessed | tf_op | source)
XLA Modules:
  0.0 32.7 jit_solution(15779670706746747531)
XLA Ops:
  0.0 0.0 copy-start.1
  0.0 0.0 copy-start.3
  0.0 0.0 copy-start.4
  0.0 1.1 %constant_dynamic-slice_fusion = (bf16[4,4,8,8,128]{4,3,2,1,0:T(8,128)(2,1)S(1)}, bf16[4,4,8,8,128]{4,3,2,1,0:T(8,128)(2,1)S(1)}) fusion(bf16[4,4,8,8,256]{4,3,2,1,0:T(8,128)(2,1)} %param.4, s32[]{:T(128)S(6)} %select_n.41, s32[]{:T(128)S(6)} %select_n.39), kind=kLoop, calls=%fused_computation.5 | loop fusion | bytes 1048584 | tf_op jit(solution)/shard_map/dynamic_slice | solution.py:583
  1.2 1.6 %collective-permute-start.5 = (bf16[4,4,8,8,128]{4,3,2,1,0:T(8,128)(2,1)S(1)}, bf16[4,4,8,8,128]{4,3,2,1,0:T(8,128)(2,1)S(1)}, u32[]{:S(2)}, u32[]{:S(2)}) collective-permute-start(bf16[4,4,8,8,128]{4,3,2,1,0:T(8,128)(2,1)S(1)} %get-tuple-element.47.rest_1_), channel_id=1, source_target_pairs={{0,1},{1,0},{2,3},{3,2},{4,5},{5,4},{6,7},{7,6},{8,9},{9,8},{10,11... | collective-permute-start | bytes 786440 | tf_op jit(solution)/shard_map/ppermute | solution.py:587
  2.7 0.1 pad_add_fusion.place_ref
  2.8 0.0 copy-start
  2.8 0.9 %copy-done = f32[4,10,8,128]{3,2,1,0:T(8,128)S(1)} copy-done((f32[4,10,8,128]{3,2,1,0:T(8,128)S(1)}, f32[4,10,8,128]{3,2,1,0:T(8,128)}, u32[]{:S(2)}) %copy-start) | copy-done | bytes 163864
  3.7 0.0 copy-start.2
  3.7 0.7 %copy-done.2 = f32[4,8,128]{2,1,0:T(8,128)S(1)} copy-done((f32[4,8,128]{2,1,0:T(8,128)S(1)}, f32[4,8,128]{2,1,0:T(8,128)}, u32[]{:S(2)}) %copy-start.2) | copy-done | bytes 16408
  4.5 0.6 %shard_map.46 = (bf16[352,128]{1,0:T(8,128)(2,1)S(1)}, bf16[352,128]{1,0:T(8,128)(2,1)S(1)}) custom-call(s32[3]{0:T(128)S(1)} %pad_add_fusion.place_ref, f32[320,128]{1,0:T(8,128)S(1)} %bitcast.17, f32[32,128]{1,0:T(8,128)S(1)} %bitcast.20), custom_call_target="tpu_custom_call" | custom-call | flops 1000000 | bytes 360460 | tf_op jit(solution)/shard_map/pallas_call | solution.py:538
  5.1 1.6 %collective-permute-start = (bf16[352,128]{1,0:T(8,128)(2,1)S(1)}, bf16[352,128]{1,0:T(8,128)(2,1)S(1)}, u32[]{:S(2)}, u32[]{:S(2)}) collective-permute-start(bf16[352,128]{1,0:T(8,128)(2,1)S(1)} %get-tuple-element.26), channel_id=1, source_target_pairs={{0,2},{2,0},{4,6},{6,4},{1,3},{3,1},{5,7},{7,5},{8,10},{10,8},{12,... | collective-permute-start | bytes 270344 | tf_op jit(solution)/shard_map/ppermute | solution.py:28
  6.7 1.9 %collective-permute-start.1 = (bf16[352,128]{1,0:T(8,128)(2,1)S(1)}, bf16[352,128]{1,0:T(8,128)(2,1)S(1)}, u32[]{:S(2)}, u32[]{:S(2)}) collective-permute-start(bf16[352,128]{1,0:T(8,128)(2,1)S(1)} %get-tuple-element.27), channel_id=1, source_target_pairs={{2,4},{4,2},{3,5},{5,3},{10,12},{12,10},{11,13},{13,11},{18,20},{2... | collective-permute-start | bytes 270344 | tf_op jit(solution)/shard_map/ppermute | solution.py:36
  8.6 0.0 copy-done.1
  8.6 0.0 copy-done.3
  8.6 0.4 %shard_map.47 = (bf16[48,128]{1,0:T(8,128)(2,1)S(1)}, bf16[48,128]{1,0:T(8,128)(2,1)S(1)}, bf16[2,2,64,128]{3,2,1,0:T(8,128)(2,1)S(1)}) custom-call(f32[320,128]{1,0:T(8,128)S(1)} %bitcast.18, f32[32,128]{1,0:T(8,128)S(1)} %bitcast.21, bf16[4,4,8,8,128]{4,3,2,1,0:T(8,128)(2,1)S(1)} %get-tuple-element.48.rest_0_.panel, ...), custom_call_target="tpu_custom_call" | custom-call | flops 1000000 | bytes 794624 | tf_op jit(solution)/shard_map/pallas_call | solution.py:538
  9.1 0.1 collective-permute-start.4
  9.2 0.0 copy-done.4
  9.2 0.1 copy.6
  9.3 0.1 copy.7
  9.4 0.3 mul.39
  9.7 0.8 %mul.40 = bf16[2,4,80,64]{3,2,1,0:T(8,128)(2,1)S(1)} reshape(bf16[2,4,10,8,8,8]{5,4,3,2,1,0:T(8,128)(2,1)S(1)} %mul.39) | data formatting | bytes 163840 | tf_op jit(solution)/shard_map/mul | solution.py:614
  10.6 0.1 mul.42
  10.7 0.0 collective-permute-done.from_a
  10.7 2.4 %collective-permute-done.1.from_b = bf16[352,128]{1,0:T(8,128)(2,1)S(1)} collective-permute-done((bf16[352,128]{1,0:T(8,128)(2,1)S(1)}, bf16[352,128]{1,0:T(8,128)(2,1)S(1)}, u32[]{:S(2)}, u32[]{:S(2)}) %collective-permute-start.1) | collective-permute-done | bytes 90144 | tf_op jit(solution)/shard_map/ppermute | solution.py:36
  13.1 1.1 %shard_map.48 = (bf16[208,128]{1,0:T(8,128)(2,1)S(1)}, bf16[208,128]{1,0:T(8,128)(2,1)S(1)}, f32[352,128]{1,0:T(8,128)S(1)}, f32[352,128]{1,0:T(8,128)S(1)}) custom-call(s32[3]{0:T(128)S(1)} %pad_add_fusion.place_ref, bf16[352,128]{1,0:T(8,128)(2,1)S(1)} %collective-permute-done.from_a, bf16[352,128]{1,0:T(8,128)(2,1)S(1)} %collective-permute-done.1.from_b, ...), custom_call_target="tpu_custom_call" | custom-call | flops 1000000 | bytes 737292 | tf_op jit(solution)/shard_map/pallas_call | solution.py:538
  14.2 0.6 %collective-permute-start.2 = (bf16[208,128]{1,0:T(8,128)(2,1)S(1)}, bf16[208,128]{1,0:T(8,128)(2,1)S(1)}, u32[]{:S(2)}, u32[]{:S(2)}) collective-permute-start(bf16[208,128]{1,0:T(8,128)(2,1)S(1)} %get-tuple-element.31), channel_id=1, source_target_pairs={{0,1},{1,0},{8,9},{9,8},{16,17},{17,16},{24,25},{25,24},{2,3},{3,2... | collective-permute-start | bytes 159752 | tf_op jit(solution)/shard_map/ppermute | solution.py:28
  14.8 0.0 collective-permute-start.3
  14.8 1.7 %shard_map.49 = (f32[320,128]{1,0:T(8,128)S(1)}, f32[3,192,128]{2,1,0:T(8,128)S(1)}, f32[4,24,128]{2,1,0:T(8,128)S(1)}, f32[2,4,24,128]{3,2,1,0:T(8,128)S(1)}) custom-call(f32[320,128]{1,0:T(8,128)S(1)} %bitcast.19, f32[32,128]{1,0:T(8,128)S(1)} %bitcast.22, f32[352,128]{1,0:T(8,128)S(1)} %get-tuple-element.33.north, f32[352,128]{1,0:T(8,128)S(1)} %get-tuple-element.34.south), custom_call_target="tpu_custom_call" | custom-call | flops 20000000 | bytes 1146880 | tf_op jit(solution)/shard_map/pallas_call | solution.py:538
  16.5 0.0 collective-permute-done.5.rest_0_
  16.6 0.8 %shard_map.50.rest_4_ = f32[4,320,128]{2,1,0:T(8,128)S(1)} custom-call(s32[3]{0:T(128)S(1)} %pad_add_fusion.place_ref, bf16[2,4,80,64]{3,2,1,0:T(8,128)(2,1)S(1)} %broadcast_multiply_fusion.basis.rest_2_, bf16[4,4,8,8,128]{4,3,2,1,0:T(8,128)(2,1)S(1)} %get-tuple-element.48.rest_0_.panel, bf16[4,4,8,8,128]{4,3,2,1,0:T(8,128)(2,1)S(1)} %collective-permute-done.5.rest_0_), custom_call_target="tpu_custom_call" | custom-call | flops 20000000 | bytes 1261580 | tf_op jit(solution)/shard_map/pallas_call | solution.py:538
  17.4 0.0 collective-permute-done.4.rest_1_
  17.4 1.0 %collective-permute-done.2.got_a = bf16[208,128]{1,0:T(8,128)(2,1)S(1)} collective-permute-done((bf16[208,128]{1,0:T(8,128)(2,1)S(1)}, bf16[208,128]{1,0:T(8,128)(2,1)S(1)}, u32[]{:S(2)}, u32[]{:S(2)}) %collective-permute-start.2) | collective-permute-done | bytes 53280 | tf_op jit(solution)/shard_map/ppermute | solution.py:28
  18.4 1.3 %collective-permute-done.3.got_b = bf16[208,128]{1,0:T(8,128)(2,1)S(1)} collective-permute-done((bf16[208,128]{1,0:T(8,128)(2,1)S(1)}, bf16[208,128]{1,0:T(8,128)(2,1)S(1)}, u32[]{:S(2)}, u32[]{:S(2)}) %collective-permute-start.3) | collective-permute-done | bytes 53280 | tf_op jit(solution)/shard_map/ppermute | solution.py:36
  19.7 2.6 %shard_map.51 = (bf16[368,128]{1,0:T(8,128)(2,1)S(1)}, bf16[368,128]{1,0:T(8,128)(2,1)S(1)}, f32[320,128]{1,0:T(8,128)S(1)}, f32[40,128]{1,0:T(8,128)S(1)}, f32[2,4,24,128]{3,2,1,0:T(8,128)S(1)}) custom-call(s32[3]{0:T(128)S(1)} %pad_add_fusion.place_ref, bf16[208,128]{1,0:T(8,128)(2,1)S(1)} %collective-permute-done.2.got_a, ...), custom_call_target="tpu_custom_call" | custom-call | flops 1000000 | bytes 1953804 | tf_op jit(solution)/shard_map/pallas_call | solution.py:538
  22.3 0.1 collective-permute-start.6
  22.4 1.9 %collective-permute-start.7 = (bf16[368,128]{1,0:T(8,128)(2,1)S(1)}, bf16[368,128]{1,0:T(8,128)(2,1)S(1)}, u32[]{:S(2)}, u32[]{:S(2)}) collective-permute-start(bf16[368,128]{1,0:T(8,128)(2,1)S(1)} %get-tuple-element.40), channel_id=1, source_target_pairs={{2,4},{4,2},{3,5},{5,3},{10,12},{12,10},{11,13},{13,11},{18,20},{2... | collective-permute-start | bytes 282632 | tf_op jit(solution)/shard_map/ppermute | solution.py:36
  24.3 0.2 shard_map.52
  24.5 2.5 %collective-permute-done.6.from_a = bf16[368,128]{1,0:T(8,128)(2,1)S(1)} collective-permute-done((bf16[368,128]{1,0:T(8,128)(2,1)S(1)}, bf16[368,128]{1,0:T(8,128)(2,1)S(1)}, u32[]{:S(2)}, u32[]{:S(2)}) %collective-permute-start.6) | collective-permute-done | bytes 94240 | tf_op jit(solution)/shard_map/ppermute | solution.py:28
  27.0 1.9 %collective-permute-done.7.from_b = bf16[368,128]{1,0:T(8,128)(2,1)S(1)} collective-permute-done((bf16[368,128]{1,0:T(8,128)(2,1)S(1)}, bf16[368,128]{1,0:T(8,128)(2,1)S(1)}, u32[]{:S(2)}, u32[]{:S(2)}) %collective-permute-start.7) | collective-permute-done | bytes 94240 | tf_op jit(solution)/shard_map/ppermute | solution.py:36
  28.9 3.9 %shard_map.53 = f32[320,128]{1,0:T(8,128)} custom-call(s32[3]{0:T(128)S(1)} %pad_add_fusion.place_ref, f32[320,128]{1,0:T(8,128)S(1)} %get-tuple-element.38.own, bf16[368,128]{1,0:T(8,128)(2,1)S(1)} %collective-permute-done.6.from_a, bf16[368,128]{1,0:T(8,128)(2,1)S(1)} %collective-permute-done.7.from_b, f32[4,20,8,128]{3,2,1,0:T(8,128)S(1)} %get-tuple-element.44.wide, ...), custom_call_target="tpu_custom_call" | custom-call | flops 1000000 | bytes 1925132 | tf_op jit(solution)/shard_map/pallas_call | solution.py:538
  (4 shorter events, 0.1 us)
Async XLA Ops:
  0.0 8.6 %copy-start.1 = (f32[4,10,8,128]{3,2,1,0:T(8,128)S(1)}, f32[4,10,8,128]{3,2,1,0:T(8,128)}, u32[]{:S(2)}) copy-start(f32[4,10,8,128]{3,2,1,0:T(8,128)} %param.6) | copy-start | bytes 491524
  0.0 8.6 %copy-start.3 = (f32[4,8,128]{2,1,0:T(8,128)S(1)}, f32[4,8,128]{2,1,0:T(8,128)}, u32[]{:S(2)}) copy-start(f32[4,8,128]{2,1,0:T(8,128)} %param.7) | copy-start | bytes 49156
  0.0 9.2 %copy-start.4 = (bf16[4,16,10]{1,0,2:T(4,128)(2,1)S(1)}, bf16[4,16,10]{1,0,2:T(4,128)(2,1)}, u32[]{:S(2)}) copy-start(bf16[4,16,10]{1,0,2:T(4,128)(2,1)} %param.5) | copy-start | bytes 3844
  1.2 15.4 %collective-permute-start.5 = (bf16[4,4,8,8,128]{4,3,2,1,0:T(8,128)(2,1)S(1)}, bf16[4,4,8,8,128]{4,3,2,1,0:T(8,128)(2,1)S(1)}, u32[]{:S(2)}, u32[]{:S(2)}) collective-permute-start(bf16[4,4,8,8,128]{4,3,2,1,0:T(8,128)(2,1)S(1)} %get-tuple-element.47.rest_1_), channel_id=1, source_target_pairs={{0,1},{1,0},{2,3},{3,2},{4,5},{5,4},{6,7},{7,6},{8,9},{9,8},{10,11... | collective-permute-start | bytes 786440 | tf_op jit(solution)/shard_map/ppermute | solution.py:587
  2.8 0.9 %copy-start = (f32[4,10,8,128]{3,2,1,0:T(8,128)S(1)}, f32[4,10,8,128]{3,2,1,0:T(8,128)}, u32[]{:S(2)}) copy-start(f32[4,10,8,128]{3,2,1,0:T(8,128)} %param.6) | copy-start | bytes 491524
  3.7 0.7 %copy-start.2 = (f32[4,8,128]{2,1,0:T(8,128)S(1)}, f32[4,8,128]{2,1,0:T(8,128)}, u32[]{:S(2)}) copy-start(f32[4,8,128]{2,1,0:T(8,128)} %param.7) | copy-start | bytes 49156
  5.1 5.6 %collective-permute-start = (bf16[352,128]{1,0:T(8,128)(2,1)S(1)}, bf16[352,128]{1,0:T(8,128)(2,1)S(1)}, u32[]{:S(2)}, u32[]{:S(2)}) collective-permute-start(bf16[352,128]{1,0:T(8,128)(2,1)S(1)} %get-tuple-element.26), channel_id=1, source_target_pairs={{0,2},{2,0},{4,6},{6,4},{1,3},{3,1},{5,7},{7,5},{8,10},{10,8},{12,... | collective-permute-start | bytes 270344 | tf_op jit(solution)/shard_map/ppermute | solution.py:28
  6.7 6.4 %collective-permute-start.1 = (bf16[352,128]{1,0:T(8,128)(2,1)S(1)}, bf16[352,128]{1,0:T(8,128)(2,1)S(1)}, u32[]{:S(2)}, u32[]{:S(2)}) collective-permute-start(bf16[352,128]{1,0:T(8,128)(2,1)S(1)} %get-tuple-element.27), channel_id=1, source_target_pairs={{2,4},{4,2},{3,5},{5,3},{10,12},{12,10},{11,13},{13,11},{18,20},{2... | collective-permute-start | bytes 270344 | tf_op jit(solution)/shard_map/ppermute | solution.py:36
  9.1 8.3 %collective-permute-start.4 = (bf16[64,128]{1,0:T(8,128)(2,1)S(1)}, bf16[64,128]{1,0:T(8,128)(2,1)S(1)}, u32[]{:S(2)}, u32[]{:S(2)}) collective-permute-start(bf16[64,128]{1,0:T(8,128)(2,1)S(1)} %select_bitcast_fusion), channel_id=1, source_target_pairs={{0,8},{8,16},{16,24},{24,0},{1,25},{9,1},{17,9},{25,17},{2,10},{10... | collective-permute-start | bytes 49160 | tf_op jit(solution)/shard_map/ppermute | solution.py:608
  14.2 4.2 %collective-permute-start.2 = (bf16[208,128]{1,0:T(8,128)(2,1)S(1)}, bf16[208,128]{1,0:T(8,128)(2,1)S(1)}, u32[]{:S(2)}, u32[]{:S(2)}) collective-permute-start(bf16[208,128]{1,0:T(8,128)(2,1)S(1)} %get-tuple-element.31), channel_id=1, source_target_pairs={{0,1},{1,0},{8,9},{9,8},{16,17},{17,16},{24,25},{25,24},{2,3},{3,2... | collective-permute-start | bytes 159752 | tf_op jit(solution)/shard_map/ppermute | solution.py:28
  14.8 4.9 %collective-permute-start.3 = (bf16[208,128]{1,0:T(8,128)(2,1)S(1)}, bf16[208,128]{1,0:T(8,128)(2,1)S(1)}, u32[]{:S(2)}, u32[]{:S(2)}) collective-permute-start(bf16[208,128]{1,0:T(8,128)(2,1)S(1)} %get-tuple-element.32), channel_id=1, source_target_pairs={{1,8},{9,16},{17,24},{25,0},{8,1},{16,9},{24,17},{0,25},{3,10},{11... | collective-permute-start | bytes 159752 | tf_op jit(solution)/shard_map/ppermute | solution.py:36
  22.3 4.6 %collective-permute-start.6 = (bf16[368,128]{1,0:T(8,128)(2,1)S(1)}, bf16[368,128]{1,0:T(8,128)(2,1)S(1)}, u32[]{:S(2)}, u32[]{:S(2)}) collective-permute-start(bf16[368,128]{1,0:T(8,128)(2,1)S(1)} %get-tuple-element.39), channel_id=1, source_target_pairs={{0,2},{2,0},{4,6},{6,4},{1,3},{3,1},{5,7},{7,5},{8,10},{10,8},{12,... | collective-permute-start | bytes 282632 | tf_op jit(solution)/shard_map/ppermute | solution.py:28
  22.4 6.5 %collective-permute-start.7 = (bf16[368,128]{1,0:T(8,128)(2,1)S(1)}, bf16[368,128]{1,0:T(8,128)(2,1)S(1)}, u32[]{:S(2)}, u32[]{:S(2)}) collective-permute-start(bf16[368,128]{1,0:T(8,128)(2,1)S(1)} %get-tuple-element.40), channel_id=1, source_target_pairs={{2,4},{4,2},{3,5},{5,3},{10,12},{12,10},{11,13},{13,11},{18,20},{2... | collective-permute-start | bytes 282632 | tf_op jit(solution)/shard_map/ppermute | solution.py:36

commit v4 on v3

--- a/solution.py
+++ b/solution.py
@@ -38,6 +38,12 @@
 
 def place(w):
     return (w + 2) // SUB, (w + 2) % SUB
+
+
+def position():
+    me = lax.axis_index("gz")
+    ring = lax.axis_index("gx") * lax.axis_size("gz") + me
+    return lax.rem(ring, 2) == 1, lax.rem(lax.axis_index("gy"), 2) == 1, me
 
 
 def lane_grid():
@@ -115,18 +121,11 @@
     return north, south
 
 
-def send_rows_kernel(place_ref, control, coefficients, out_a, out_b):
-    odd = place_ref[1] == 1
+def start_kernel(own, out_a, out_b):
+    _, odd, _ = position()
     sub = lax.broadcasted_iota(jnp.int32, (SUB, LANES), 0)
-    first = control.shape[0] // SUB
-    count = first + coefficients.shape[0] // SUB
-
-    def tile(i):
-        if i < first:
-            return control[pl.ds(i * SUB, SUB), :]
-        return coefficients[pl.ds((i - first) * SUB, SUB), :]
-
-    put_rows(out_a, out_b, [tile(i) for i in range(count)], odd, sub)
+    tiles = [own[pl.ds(i * SUB, SUB), :] for i in range(own.shape[0] // SUB)]
+    put_rows(out_a, out_b, tiles, odd, sub)
 
 
 def put_rows(out_a, out_b, tiles, odd, sub):
@@ -167,21 +166,24 @@
     return west_out, east_out
 
 
-def own_strips_kernel(fields, eofs, members, control, coefficients, *rest):
-    panels, (west, east, edges) = rest[:-3], rest[-3:]
+def own_strips_kernel(fields, eofs, members, own, panels, west, east, edges, *tiles):
+    _, _, me = position()
     lane = lane_grid()
-    total = fields * eofs
 
     def tile(i):
-        if i < total:
-            return control[pl.ds(i * SUB, SUB), :]
-        return coefficients[pl.ds((i - total) * SUB, SUB), :]
-
-    for ref, tiles in zip((west, east), strip_tiles(fields, eofs, tile, lane)):
-        for pair in range(len(tiles) // 2):
-            write_pair(ref, pair, *tiles[2 * pair : 2 * pair + 2])
-
-    depth = panels[0].shape[2] * SUB
+        return own[pl.ds(i * SUB, SUB), :]
+
+    for ref, packed in zip((west, east), strip_tiles(fields, eofs, tile, lane)):
+        for pair in range(len(packed) // 2):
+            write_pair(ref, pair, *packed[2 * pair : 2 * pair + 2])
+
+    count = len(tiles)
+    for s, block in enumerate(tiles):
+        start = pl.multiple_of(lax.rem(me + s, count) * LANES, LANES)
+        for m in range(members):
+            for f in range(fields):
+                block[m, f] = panels[m, f, :, :, pl.ds(start, LANES)]
+    depth = panels.shape[2] * SUB
     column = lax.broadcasted_iota(jnp.int32, (LANES, 2 * LANES), 0)
     target = lax.broadcasted_iota(jnp.int32, (LANES, 2 * LANES), 1)
     west_ok = (target < LANES) & (column < STEPS)
@@ -191,7 +193,7 @@
         target - column,
         jnp.where(east_ok, target - LANES - column + LANES - STEPS, -1),
     )
-    for s, block in enumerate(panels):
+    for s, block in enumerate(tiles):
         total = jnp.zeros((depth, 2 * LANES), jnp.float32)
         for m in range(members):
             for f in range(fields):
@@ -204,9 +206,9 @@
         edges[s, 1] = total[:, LANES:]
 
 
-def pack_kernel(fields, eofs, place_ref, from_a, from_b, west, east, *rest):
+def pack_kernel(fields, eofs, from_a, from_b, west, east, *rest):
     panel_edges, (out_a, out_b, north, south) = rest[:-4], rest[-4:]
-    ring_odd, odd = place_ref[0] == 1, place_ref[1] == 1
+    ring_odd, odd, _ = position()
     lane = lane_grid()
     sub = lax.broadcasted_iota(jnp.int32, (SUB, LANES), 0)
     for pair in range((fields * eofs + 4) // 2):
@@ -248,7 +250,7 @@
 
 
 def main_kernel(
-    fields, eofs, control, coefficients, north, south,
+    fields, eofs, own, north, south,
     adj, strip, coeff_main, coeff_strip, wide, first, second,
 ):
     lane = lane_grid()
@@ -258,11 +260,7 @@
     total = fields * eofs
 
     def tile(t, i):
-        if t != 1:
-            return (north, south)[t // 2][pl.ds(i * SUB, SUB), :]
-        if i < total:
-            return control[pl.ds(i * SUB, SUB), :]
-        return coefficients[pl.ds((i - total) * SUB, SUB), :]
+        return (north, own, south)[t][pl.ds(i * SUB, SUB), :]
 
     for k in range(4):
         for t in range(3):
@@ -281,17 +279,38 @@
             coeff_strip[0, k, at, :] = jnp.where((inner >= HALO) & (inner < 2 * HALO), west, 0.0)
             coeff_strip[1, k, at, :] = jnp.where((shifted & (SLOT - 1)) < HALO, east, 0.0)
     main_coefficients(coeff_main, wide)
-    diffuse_main(control, north, south, adj, wide, first, second, True)
+    groups = total // SUB
+    read, write = main_rows(own, north, south, adj)
+    diffuse(read, write, lambda k, w: [wide[k, w]] * groups, groups, first, second, True)
     for t in range(3):
         own_columns(fields, eofs, lambda i: tile(t, i), strip, t, lane)
 
 
-def project_kernel(fields, eofs, members, place_ref, basis, panel, *rest):
-    arrived, proj = rest[:-1], rest[-1]
-    me = place_ref[2]
+def project_kernel(fields, eofs, members, eof_basis, panel, *rest):
+    arrived, (basis, proj) = rest[:-2], rest[-2:]
+    _, _, me = position()
     blocks = (panel,) + arrived
     count = len(blocks)
     depth = panel.shape[2] * SUB
+    levels = eof_basis.shape[1]
+
+    def grid(shape, dim):
+        return lax.broadcasted_iota(jnp.int32, shape, dim)
+
+    shape = (eofs * SUB, eofs)
+    widen = (grid(shape, 0) // SUB == grid(shape, 1)).astype(jnp.bfloat16)
+    shape = (levels, levels * SUB)
+    spread = (grid(shape, 1) // SUB == grid(shape, 0)).astype(jnp.bfloat16)
+    shape = (eofs * SUB, levels * SUB)
+    same_row = grid(shape, 0) % SUB == grid(shape, 1) % SUB
+    for f in range(fields):
+        wide = lax.dot_general(
+            widen, eof_basis[f], (((1,), (1,)), ((), ())), preferred_element_type=jnp.float32
+        ).astype(jnp.bfloat16)
+        wide = jnp.dot(wide, spread, preferred_element_type=jnp.float32)
+        wide = jnp.where(same_row, wide, 0.0).astype(jnp.bfloat16)
+        for h in range(count):
+            basis[h, f] = wide[:, h * depth : (h + 1) * depth]
     for f in range(fields):
         total = None
         for s, block in enumerate(blocks):
@@ -323,9 +342,7 @@
             wide_strip[k, w, pl.ds(2 * SUB, SUB), :] = east
 
 
-def diffuse_main(own, north, south, out, wide, first, second, adjoint):
-    groups = own.shape[0] // (SUB * SUB)
-
+def main_rows(own, north, south, out):
     def read(w, g):
         t, y = place(w)
         return (north, own, south)[t][pl.ds(g * SUB * SUB + y, SUB, stride=SUB), :]
@@ -333,10 +350,10 @@
     def write(w, g, cells):
         out[pl.ds(g * SUB * SUB + w - STEPS, SUB, stride=SUB), :] = cells
 
-    diffuse(read, write, lambda k, w: [wide[k, w]] * groups, groups, first, second, adjoint)
-
-
-def diffuse_strip(strip, out, wide_strip, first, second, adjoint):
+    return read, write
+
+
+def strip_rows(strip, out, wide_strip):
     def read(w, g):
         t, y = place(w)
         return strip[t, pl.ds(g * SUB * SUB + y, SUB, stride=SUB), :]
@@ -347,17 +364,17 @@
     def coeff(k, w):
         return [wide_strip[k, w, pl.ds(g * SUB, SUB), :] for g in range(3)]
 
-    diffuse(read, write, coeff, 3, first, second, adjoint)
-
-
-def combine_kernel(fields, eofs, members, place_ref, got_a, got_b, *rest):
+    return read, write, coeff
+
+
+def combine_kernel(fields, eofs, members, got_a, got_b, *rest):
     (
         basis, adj, proj, strip_own, coeff_own,
         out_a, out_b, combined, halo_out, coeff_strip,
         strip, wide_strip, adj_strip, panel_in, proj_strip, first, second,
     ) = rest[-17:]
     panel_parts = rest[:-17]
-    ring_odd, odd, me = place_ref[0] == 1, place_ref[1] == 1, place_ref[2]
+    ring_odd, odd, me = position()
     lane = lane_grid()
     sub = lax.broadcasted_iota(jnp.int32, (SUB, LANES), 0)
     inner = lane & (SLOT - 1)
@@ -409,7 +426,8 @@
                     mine = time_step * mine
                 coeff_strip[side, k, at, :] = jnp.where(mask, mine, coeff_own[side, k, at, :])
     strip_coefficients(coeff_strip, wide_strip, eofs)
-    diffuse_strip(strip, adj_strip, wide_strip, first, second, True)
+    read, write, coeff = strip_rows(strip, adj_strip, wide_strip)
+    diffuse(read, write, coeff, 3, first, second, True)
 
     count, depth = basis.shape[0], basis.shape[3]
     if len(panel_parts) == 2:
@@ -503,10 +521,10 @@
 
 
 def forward_kernel(
-    fields, eofs, place_ref, own, from_a, from_b, wide, wide_strip, strip_own,
+    fields, eofs, own, from_a, from_b, wide, wide_strip, strip_own,
     out, north, south, strip, strip_out, first, second,
 ):
-    odd = place_ref[1] == 1
+    _, odd, _ = position()
     lane = lane_grid()
     sub = lax.broadcasted_iota(jnp.int32, (SUB, LANES), 0)
     total = fields * eofs
@@ -519,8 +537,23 @@
         own_columns(fields, eofs, lambda i: ref[pl.ds(i * SUB, SUB), :], strip, t, lane)
         beyond_columns(eofs, ref.at[pl.ds(total * SUB, 2 * eofs // 4 * SUB)], strip, t, lane)
     strip[1] = strip_own[0]
-    diffuse_strip(strip, strip_out, wide_strip, first, second, False)
-    diffuse_main(own, north, south, out, wide, first, second, False)
+    groups = total // SUB
+    read_main, write_main = main_rows(own, north, south, out)
+    read_strip, write_strip, coeff_strip = strip_rows(strip, strip_out, wide_strip)
+
+    def read(w, g):
+        return read_main(w, g) if g < groups else read_strip(w, g - groups)
+
+    def write(w, g, cells):
+        if g < groups:
+            write_main(w, g, cells)
+        else:
+            write_strip(w, g - groups, cells)
+
+    def coeff(k, w):
+        return [wide[k, w]] * groups + coeff_strip(k, w)
+
+    diffuse(read, write, coeff, groups + 3, first, second, False)
     for f in range(fields):
         for e in range(eofs):
             at = pl.ds((f * eofs + e) * SUB, SUB)
@@ -533,11 +566,10 @@
 
 def call(kernel, args, outs, scratch=(), flops=1_000_000):
     whole = pl.BlockSpec(memory_space=pltpu.VMEM)
-    scalars = pl.BlockSpec(memory_space=pltpu.SMEM)
     moved = sum(a.size * a.dtype.itemsize for a in list(args) + list(outs))
     return pl.pallas_call(
         kernel,
-        in_specs=[scalars if a.dtype == jnp.int32 else whole for a in args],
+        in_specs=[whole] * len(args),
         out_specs=[whole] * len(outs),
         out_shape=list(outs),
         scratch_shapes=[pltpu.VMEM(*s) for s in scratch],
@@ -570,37 +602,30 @@
     _, eofs, _, col_count = control.shape
     count = lax.axis_size("gz")
     me = lax.axis_index("gz")
-    ring = lax.axis_index("gx") * count + me
-    where_am_i = jnp.stack([ring % 2, lax.axis_index("gy") % 2, me]).astype(jnp.int32)
     total = fields * eofs
     rows = total * row_count
-    control_in = control.reshape(rows, col_count)
-    coeff_in = coefficients.reshape(4 * row_count, col_count)
     f32 = lambda *shape: jax.ShapeDtypeStruct(shape, jnp.float32)
     bf16 = lambda *shape: jax.ShapeDtypeStruct(shape, jnp.bfloat16)
 
-    def columns(of):
-        return lax.dynamic_slice_in_dim(panels, of * col_count, col_count, axis=4)
-
-    tiles = [columns((me + s) % count) for s in range(count)]
+    all_rows = rows + 4 * row_count
+    own = jnp.concatenate(
+        [control.reshape(rows, col_count), coefficients.reshape(4 * row_count, col_count)]
+    )
+    sent_a, sent_b = call(start_kernel, [own], [bf16(all_rows, col_count)] * 2)
+    from_a, from_b = swap_a(sent_a, "gy"), swap_b(sent_b, "gy", False)
+    strip_sent = (eofs // 2 + 1) * row_count
+    west, east, edges, *tiles = call(
+        functools.partial(own_strips_kernel, fields, eofs, members),
+        [own, panels],
+        [bf16(strip_sent, col_count)] * 2
+        + [bf16(count, 2, depth * row_count, col_count)]
+        + [bf16(*panels.shape[:-1], col_count)] * count,
+    )
     arrived = [
         lax.ppermute(tiles[s], "gz", [(i, (i + s) % count) for i in range(count)])
         for s in range(1, count)
     ]
 
-    sent_a, sent_b = call(
-        send_rows_kernel,
-        [where_am_i, control_in, coeff_in],
-        [bf16(rows + 4 * row_count, col_count)] * 2,
-    )
-    from_a, from_b = swap_a(sent_a, "gy"), swap_b(sent_b, "gy", False)
-
-    strip_sent = (eofs // 2 + 1) * row_count
-    west, east, edges = call(
-        functools.partial(own_strips_kernel, fields, eofs, members),
-        [control_in, coeff_in, *tiles],
-        [bf16(strip_sent, col_count)] * 2 + [bf16(count, 2, depth * row_count, col_count)],
-    )
     if count == 2:
         groups = lax.axis_size("gx")
         pairs = [(2 * g, (g + 1) % groups * 2) for g in range(groups)]
@@ -610,15 +635,9 @@
     else:
         panel_sent, panel_parts = [], panel_edges_apart(edges, count, me)
 
-    basis = eof_basis.transpose(0, 2, 1).reshape(fields, eofs, 1, count, depth, 1)
-    basis = basis * jnp.eye(row_count, dtype=eof_basis.dtype)[:, None, None, :]
-    basis = basis.transpose(3, 0, 1, 2, 4, 5).reshape(
-        count, fields, eofs * row_count, depth * row_count
-    )
-
     sent_a, sent_b, north, south = call(
         functools.partial(pack_kernel, fields, eofs),
-        [where_am_i, from_a, from_b, west, east, *panel_sent],
+        [from_a, from_b, west, east, *panel_sent],
         [bf16(3 * strip_sent + len(panel_sent) * depth * row_count, col_count)] * 2
         + [f32(rows + 4 * row_count, col_count)] * 2,
     )
@@ -629,7 +648,7 @@
     strip_scratch = [((WINDOW, 3 * SUB, LANES), jnp.float32)] * 2
     adj, strip, coeff_main, coeff_strip = call(
         functools.partial(main_kernel, fields, eofs),
-        [control_in, coeff_in, north, south],
+        [own, north, south],
         [
             f32(rows, col_count),
             f32(3, strip_rows, col_count),
@@ -639,16 +658,19 @@
         [((4, WINDOW, SUB, LANES), jnp.float32)] + main_scratch,
         flops=20_000_000,
     )
-    (proj,) = call(
+    basis, proj = call(
         functools.partial(project_kernel, fields, eofs, members),
-        [where_am_i, basis, tiles[0], *arrived],
-        [f32(members, rows, col_count)],
+        [eof_basis, tiles[0], *arrived],
+        [
+            bf16(count, fields, eofs * row_count, depth * row_count),
+            f32(members, rows, col_count),
+        ],
         flops=20_000_000,
     )
     packed = 2 * eofs // 4
     sent_a, sent_b, combined, halo, coeff_strip = call(
         functools.partial(combine_kernel, fields, eofs, members),
-        [where_am_i, got_a, got_b, *panel_parts, basis, adj, proj, strip, coeff_strip],
+        [got_a, got_b, *panel_parts, basis, adj, proj, strip, coeff_strip],
         [bf16((total + packed + 1) // 2 * 2 * row_count, col_count)] * 2
         + [
             f32(rows, col_count),
@@ -677,11 +699,11 @@
     )
     (result,) = call(
         functools.partial(forward_kernel, fields, eofs),
-        [where_am_i, combined, from_a, from_b, wide, wide_strip, strip],
+        [combined, from_a, from_b, wide, wide_strip, strip],
         [f32(rows, col_count)],
         [((sent_a.shape[0], LANES), jnp.float32)] * 2
         + [((3, strip_rows, LANES), jnp.float32), ((strip_rows, LANES), jnp.float32)]
-        + main_scratch,
+        + [((WINDOW, total + 3 * SUB, LANES), jnp.float32)] * 2,
     )
     return result.reshape(control.shape)
 

time: 33 us -> 28.7 us (0.87)
  the two profiles are of different devices: /device:TPU:16 before, /device:TPU:10 now
where the time goes in v4:
time: 28.7 us; the launch traced here: 28.2 us
  starting transfers between devices  11.9 us (41%)
  Pallas kernels  8.3 us (29%)
  waiting for transfers between devices  6.74 us (23%)
  other arithmetic  1.01 us (4%)
    pallas_call x8, Pallas kernels, call(): pl.pallas_call(kernel, in_specs=[whole] * len(args), out_specs=[whole] *...  8.3 us
    ppermute x3, starting transfers between devices, swap_b(): return lax.ppermute(values, axes, pairs + [(j, i) for i, j in pairs])  7.46 us
    ppermute x3, waiting for transfers between devices, swap_b(): return lax.ppermute(values, axes, pairs + [(j, i) for i, j in pairs])  3.34 us
    ppermute x1, starting transfers between devices, per_device(): lax.ppermute(jnp.where(me == 1, edges[1, 0], edges[1, 1]), RING, pairs)  2.67 us
    ppermute x3, waiting for transfers between devices, swap_a(): return lax.ppermute(values, axes, [(i, i ^ 1) for i in range(count)])  2.32 us
    ppermute x3, starting transfers between devices, swap_a(): return lax.ppermute(values, axes, [(i, i ^ 1) for i in range(count)])  1.19 us
    ppermute x1, waiting for transfers between devices, per_device(): lax.ppermute(tiles[s], 'gz', [(i, (i + s) % count) for i in range(count)])  1.07 us
    concatenate x1, other arithmetic, per_device(): jnp.concatenate([control.reshape(rows, col_count), coefficients.reshape(4...  1 us
  transfers between devices with their start and end apart: 8, of which 4 were waited for; matrix products, arithmetic and copies ran while one was open for 0% of the time, Pallas kernels for 12%

profile of v4, /device:TPU:10, one launch (start us, length us, event | category | flops | bytes accessed | tf_op | source)
XLA Modules:
  0.0 28.2 jit_solution(13257543154714449216)
XLA Ops:
  0.0 0.0 copy-start
  0.0 1.0 %pad_maximum_fusion.own = f32[352,128]{1,0:T(8,128)S(1)} fusion(f32[32,128]{1,0:T(8,128)} %bitcast.6, f32[320,128]{1,0:T(8,128)} %bitcast.5), kind=kLoop, calls=%fused_computation | loop fusion | flops 45056 | bytes 360448 | tf_op jit(solution)/shard_map/concatenate | solution.py:611
  1.0 0.1 shard_map.46
  1.1 0.5 %collective-permute-start = (bf16[352,128]{1,0:T(8,128)(2,1)S(1)}, bf16[352,128]{1,0:T(8,128)(2,1)S(1)}, u32[]{:S(2)}, u32[]{:S(2)}) collective-permute-start(bf16[352,128]{1,0:T(8,128)(2,1)S(1)} %get-tuple-element.30), channel_id=1, source_target_pairs={{0,2},{2,0},{4,6},{6,4},{1,3},{3,1},{5,7},{7,5},{8,10},{10,8},{12,... | collective-permute-start | bytes 270344 | tf_op jit(solution)/shard_map/ppermute | solution.py:28
  1.6 4.6 %collective-permute-start.1 = (bf16[352,128]{1,0:T(8,128)(2,1)S(1)}, bf16[352,128]{1,0:T(8,128)(2,1)S(1)}, u32[]{:S(2)}, u32[]{:S(2)}) collective-permute-start(bf16[352,128]{1,0:T(8,128)(2,1)S(1)} %get-tuple-element.31), channel_id=1, source_target_pairs={{2,4},{4,2},{3,5},{5,3},{10,12},{12,10},{11,13},{13,11},{18,20},{2... | collective-permute-start | bytes 270344 | tf_op jit(solution)/shard_map/ppermute | solution.py:36
  6.2 0.0 copy-done
  6.2 0.4 %shard_map.47 = (bf16[48,128]{1,0:T(8,128)(2,1)S(1)}, bf16[48,128]{1,0:T(8,128)(2,1)S(1)}, bf16[2,2,64,128]{3,2,1,0:T(8,128)(2,1)S(1)}, bf16[4,4,8,8,128]{4,3,2,...) custom-call(f32[352,128]{1,0:T(8,128)S(1)} %pad_maximum_fusion.own, bf16[4,4,8,8,256]{4,3,2,1,0:T(8,128)(2,1)S(1)} %copy-done), custom_call_target="tpu_custom_call" | custom-call | flops 1000000 | bytes 1318912 | tf_op jit(solution)/shard_map/pallas_call | solution.py:570
  6.7 0.6 %collective-permute-start.5 = (bf16[4,4,8,8,128]{4,3,2,1,0:T(8,128)(2,1)S(1)}, bf16[4,4,8,8,128]{4,3,2,1,0:T(8,128)(2,1)S(1)}, u32[]{:S(2)}, u32[]{:S(2)}) collective-permute-start(bf16[4,4,8,8,128]{4,3,2,1,0:T(8,128)(2,1)S(1)} %get-tuple-element.38), channel_id=1, source_target_pairs={{0,1},{1,0},{2,3},{3,2},{4,5},{5,4},{6,7},{7,6},{8,9},{9,8},{10,11... | collective-permute-start | bytes 786440 | tf_op jit(solution)/shard_map/ppermute | solution.py:625
  7.3 0.0 collective-permute-done.from_a
  7.3 1.4 %collective-permute-done.1.from_b = bf16[352,128]{1,0:T(8,128)(2,1)S(1)} collective-permute-done((bf16[352,128]{1,0:T(8,128)(2,1)S(1)}, bf16[352,128]{1,0:T(8,128)(2,1)S(1)}, u32[]{:S(2)}, u32[]{:S(2)}) %collective-permute-start.1) | collective-permute-done | bytes 90144 | tf_op jit(solution)/shard_map/ppermute | solution.py:36
  8.7 0.5 %shard_map.48 = (bf16[208,128]{1,0:T(8,128)(2,1)S(1)}, bf16[208,128]{1,0:T(8,128)(2,1)S(1)}, f32[352,128]{1,0:T(8,128)S(1)}, f32[352,128]{1,0:T(8,128)S(1)}) custom-call(bf16[352,128]{1,0:T(8,128)(2,1)S(1)} %collective-permute-done.from_a, bf16[352,128]{1,0:T(8,128)(2,1)S(1)} %collective-permute-done.1.from_b, bf16[48,128]{1,0:T(8,128)(2,1)S(1)} %get-tuple-element.32.west, ...), custom_call_target="tpu_custom_call" | custom-call | flops 1000000 | bytes 737280 | tf_op jit(solution)/shard_map/pallas_call | solution.py:570
  9.2 0.6 %collective-permute-start.2 = (bf16[208,128]{1,0:T(8,128)(2,1)S(1)}, bf16[208,128]{1,0:T(8,128)(2,1)S(1)}, u32[]{:S(2)}, u32[]{:S(2)}) collective-permute-start(bf16[208,128]{1,0:T(8,128)(2,1)S(1)} %get-tuple-element.35), channel_id=1, source_target_pairs={{0,1},{1,0},{8,9},{9,8},{16,17},{17,16},{24,25},{25,24},{2,3},{3,2... | collective-permute-start | bytes 159752 | tf_op jit(solution)/shard_map/ppermute | solution.py:28
  9.8 0.0 copy-start.1
  9.8 0.0 collective-permute-start.3
  9.8 2.7 %collective-permute-start.4 = (bf16[64,128]{1,0:T(8,128)(2,1)S(1)}, bf16[64,128]{1,0:T(8,128)(2,1)S(1)}, u32[]{:S(2)}, u32[]{:S(2)}) collective-permute-start(bf16[64,128]{1,0:T(8,128)(2,1)S(1)} %select_bitcast_fusion), channel_id=1, source_target_pairs={{0,8},{8,16},{16,24},{24,0},{1,25},{9,1},{17,9},{25,17},{2,10},{10... | collective-permute-start | bytes 49160 | tf_op jit(solution)/shard_map/ppermute | solution.py:633
  12.5 0.0 copy-done.1
  12.5 0.1 copy.5.eof_basis
  12.6 1.7 %shard_map.50 = (f32[320,128]{1,0:T(8,128)S(1)}, f32[3,192,128]{2,1,0:T(8,128)S(1)}, f32[4,24,128]{2,1,0:T(8,128)S(1)}, f32[2,4,24,128]{3,2,1,0:T(8,128)S(1)}) custom-call(f32[352,128]{1,0:T(8,128)S(1)} %pad_maximum_fusion.own, f32[352,128]{1,0:T(8,128)S(1)} %get-tuple-element.40.north, f32[352,128]{1,0:T(8,128)S(1)} %get-tuple-element.41.south), custom_call_target="tpu_custom_call" | custom-call | flops 20000000 | bytes 1146880 | tf_op jit(solution)/shard_map/pallas_call | solution.py:570
  14.3 1.1 %collective-permute-done.5.rest_0_ = bf16[4,4,8,8,128]{4,3,2,1,0:T(8,128)(2,1)S(1)} collective-permute-done((bf16[4,4,8,8,128]{4,3,2,1,0:T(8,128)(2,1)S(1)}, bf16[4,4,8,8,128]{4,3,2,1,0:T(8,128)(2,1)S(1)}, u32[]{:S(2)}, u32[]{:S(2)}) %collective-permute-start.5) | collective-permute-done | bytes 262176 | tf_op jit(solution)/shard_map/ppermute | solution.py:625
  15.4 0.7 %shard_map.49 = (bf16[2,4,80,64]{3,2,1,0:T(8,128)(2,1)S(1)}, f32[4,320,128]{2,1,0:T(8,128)S(1)}) custom-call(bf16[4,16,10]{2,1,0:T(8,128)(2,1)S(1)} %copy.5.eof_basis, bf16[4,4,8,8,128]{4,3,2,1,0:T(8,128)(2,1)S(1)} %get-tuple-element.37.panel, bf16[4,4,8,8,128]{4,3,2,1,0:T(8,128)(2,1)S(1)} %collective-permute-done.5.rest_0_), custom_call_target="tpu_custom_call" | custom-call | flops 20000000 | bytes 1262848 | tf_op jit(solution)/shard_map/pallas_call | solution.py:570
  16.1 0.0 collective-permute-done.4.rest_1_
  16.1 0.0 collective-permute-done.2.got_a
  16.1 0.0 collective-permute-done.3.got_b
  16.1 1.9 %shard_map.51 = (bf16[368,128]{1,0:T(8,128)(2,1)S(1)}, bf16[368,128]{1,0:T(8,128)(2,1)S(1)}, f32[320,128]{1,0:T(8,128)S(1)}, f32[40,128]{1,0:T(8,128)S(1)}, f32[2,4,24,128]{3,2,1,0:T(8,128)S(1)}) custom-call(bf16[208,128]{1,0:T(8,128)(2,1)S(1)} %collective-permute-done.2.got_a, bf16[208,128]{1,0:T(8,128)(2,1)S(1)} %collective-permute-done.3.got_b, ...), custom_call_target="tpu_custom_call" | custom-call | flops 1000000 | bytes 1953792 | tf_op jit(solution)/shard_map/pallas_call | solution.py:570
  18.0 0.1 collective-permute-start.6
  18.1 2.9 %collective-permute-start.7 = (bf16[368,128]{1,0:T(8,128)(2,1)S(1)}, bf16[368,128]{1,0:T(8,128)(2,1)S(1)}, u32[]{:S(2)}, u32[]{:S(2)}) collective-permute-start(bf16[368,128]{1,0:T(8,128)(2,1)S(1)} %get-tuple-element.48), channel_id=1, source_target_pairs={{2,4},{4,2},{3,5},{5,3},{10,12},{12,10},{11,13},{13,11},{18,20},{2... | collective-permute-start | bytes 282632 | tf_op jit(solution)/shard_map/ppermute | solution.py:36
  20.9 0.2 shard_map.52
  21.1 2.3 %collective-permute-done.6.from_a = bf16[368,128]{1,0:T(8,128)(2,1)S(1)} collective-permute-done((bf16[368,128]{1,0:T(8,128)(2,1)S(1)}, bf16[368,128]{1,0:T(8,128)(2,1)S(1)}, u32[]{:S(2)}, u32[]{:S(2)}) %collective-permute-start.6) | collective-permute-done | bytes 94240 | tf_op jit(solution)/shard_map/ppermute | solution.py:28
  23.4 1.9 %collective-permute-done.7.from_b = bf16[368,128]{1,0:T(8,128)(2,1)S(1)} collective-permute-done((bf16[368,128]{1,0:T(8,128)(2,1)S(1)}, bf16[368,128]{1,0:T(8,128)(2,1)S(1)}, u32[]{:S(2)}, u32[]{:S(2)}) %collective-permute-start.7) | collective-permute-done | bytes 94240 | tf_op jit(solution)/shard_map/ppermute | solution.py:36
  25.3 2.9 %shard_map.53 = f32[320,128]{1,0:T(8,128)} custom-call(f32[320,128]{1,0:T(8,128)S(1)} %get-tuple-element.46.own, bf16[368,128]{1,0:T(8,128)(2,1)S(1)} %collective-permute-done.6.from_a, bf16[368,128]{1,0:T(8,128)(2,1)S(1)} %collective-permute-done.7.from_b, f32[4,20,8,128]{3,2,1,0:T(8,128)S(1)} %get-tuple-element.52.wide, ...), custom_call_target="tpu_custom_call" | custom-call | flops 1000000 | bytes 1925120 | tf_op jit(solution)/shard_map/pallas_call | solution.py:570
  (1 shorter events, 0.0 us)
Async XLA Ops:
  0.0 6.2 %copy-start = (bf16[4,4,8,8,256]{4,3,2,1,0:T(8,128)(2,1)S(1)}, bf16[4,4,8,8,256]{4,3,2,1,0:T(8,128)(2,1)}, u32[]{:S(2)}) copy-start(bf16[4,4,8,8,256]{4,3,2,1,0:T(8,128)(2,1)} %panels.1) | copy-start | bytes 1572868
  1.1 6.2 %collective-permute-start = (bf16[352,128]{1,0:T(8,128)(2,1)S(1)}, bf16[352,128]{1,0:T(8,128)(2,1)S(1)}, u32[]{:S(2)}, u32[]{:S(2)}) collective-permute-start(bf16[352,128]{1,0:T(8,128)(2,1)S(1)} %get-tuple-element.30), channel_id=1, source_target_pairs={{0,2},{2,0},{4,6},{6,4},{1,3},{3,1},{5,7},{7,5},{8,10},{10,8},{12,... | collective-permute-start | bytes 270344 | tf_op jit(solution)/shard_map/ppermute | solution.py:28
  1.6 7.1 %collective-permute-start.1 = (bf16[352,128]{1,0:T(8,128)(2,1)S(1)}, bf16[352,128]{1,0:T(8,128)(2,1)S(1)}, u32[]{:S(2)}, u32[]{:S(2)}) collective-permute-start(bf16[352,128]{1,0:T(8,128)(2,1)S(1)} %get-tuple-element.31), channel_id=1, source_target_pairs={{2,4},{4,2},{3,5},{5,3},{10,12},{12,10},{11,13},{13,11},{18,20},{2... | collective-permute-start | bytes 270344 | tf_op jit(solution)/shard_map/ppermute | solution.py:36
  6.7 8.7 %collective-permute-start.5 = (bf16[4,4,8,8,128]{4,3,2,1,0:T(8,128)(2,1)S(1)}, bf16[4,4,8,8,128]{4,3,2,1,0:T(8,128)(2,1)S(1)}, u32[]{:S(2)}, u32[]{:S(2)}) collective-permute-start(bf16[4,4,8,8,128]{4,3,2,1,0:T(8,128)(2,1)S(1)} %get-tuple-element.38), channel_id=1, source_target_pairs={{0,1},{1,0},{2,3},{3,2},{4,5},{5,4},{6,7},{7,6},{8,9},{9,8},{10,11... | collective-permute-start | bytes 786440 | tf_op jit(solution)/shard_map/ppermute | solution.py:625
  9.2 6.9 %collective-permute-start.2 = (bf16[208,128]{1,0:T(8,128)(2,1)S(1)}, bf16[208,128]{1,0:T(8,128)(2,1)S(1)}, u32[]{:S(2)}, u32[]{:S(2)}) collective-permute-start(bf16[208,128]{1,0:T(8,128)(2,1)S(1)} %get-tuple-element.35), channel_id=1, source_target_pairs={{0,1},{1,0},{8,9},{9,8},{16,17},{17,16},{24,25},{25,24},{2,3},{3,2... | collective-permute-start | bytes 159752 | tf_op jit(solution)/shard_map/ppermute | solution.py:28
  9.8 2.7 %copy-start.1 = (bf16[4,16,10]{1,0,2:T(4,128)(2,1)S(1)}, bf16[4,16,10]{1,0,2:T(4,128)(2,1)}, u32[]{:S(2)}) copy-start(bf16[4,16,10]{1,0,2:T(4,128)(2,1)} %param.5) | copy-start | bytes 3844
  9.8 6.3 %collective-permute-start.3 = (bf16[208,128]{1,0:T(8,128)(2,1)S(1)}, bf16[208,128]{1,0:T(8,128)(2,1)S(1)}, u32[]{:S(2)}, u32[]{:S(2)}) collective-permute-start(bf16[208,128]{1,0:T(8,128)(2,1)S(1)} %get-tuple-element.36), channel_id=1, source_target_pairs={{1,8},{9,16},{17,24},{25,0},{8,1},{16,9},{24,17},{0,25},{3,10},{11... | collective-permute-start | bytes 159752 | tf_op jit(solution)/shard_map/ppermute | solution.py:36
  9.8 6.3 %collective-permute-start.4 = (bf16[64,128]{1,0:T(8,128)(2,1)S(1)}, bf16[64,128]{1,0:T(8,128)(2,1)S(1)}, u32[]{:S(2)}, u32[]{:S(2)}) collective-permute-start(bf16[64,128]{1,0:T(8,128)(2,1)S(1)} %select_bitcast_fusion), channel_id=1, source_target_pairs={{0,8},{8,16},{16,24},{24,0},{1,25},{9,1},{17,9},{25,17},{2,10},{10... | collective-permute-start | bytes 49160 | tf_op jit(solution)/shard_map/ppermute | solution.py:633
  18.0 5.4 %collective-permute-start.6 = (bf16[368,128]{1,0:T(8,128)(2,1)S(1)}, bf16[368,128]{1,0:T(8,128)(2,1)S(1)}, u32[]{:S(2)}, u32[]{:S(2)}) collective-permute-start(bf16[368,128]{1,0:T(8,128)(2,1)S(1)} %get-tuple-element.47), channel_id=1, source_target_pairs={{0,2},{2,0},{4,6},{6,4},{1,3},{3,1},{5,7},{7,5},{8,10},{10,8},{12,... | collective-permute-start | bytes 282632 | tf_op jit(solution)/shard_map/ppermute | solution.py:28
  18.1 7.3 %collective-permute-start.7 = (bf16[368,128]{1,0:T(8,128)(2,1)S(1)}, bf16[368,128]{1,0:T(8,128)(2,1)S(1)}, u32[]{:S(2)}, u32[]{:S(2)}) collective-permute-start(bf16[368,128]{1,0:T(8,128)(2,1)S(1)} %get-tuple-element.48), channel_id=1, source_target_pairs={{2,4},{4,2},{3,5},{5,3},{10,12},{12,10},{11,13},{13,11},{18,20},{2... | collective-permute-start | bytes 282632 | tf_op jit(solution)/shard_map/ppermute | solution.py:36

commit v5 on v4

--- a/solution.py
+++ b/solution.py
@@ -78,7 +78,7 @@
                 flux.append(k[1][g] * east_diff + k[2][g] * north_diff)
                 if w > low:
                     flux_east = k[0][g] * east_diff + k[1][g] * north_diff
-                    div = flux_east - turn(flux_east, 1) + (flux[g] - south[g])
+                    div = (flux[g] - south[g]) + flux_east - turn(flux_east, 1)
                     moved = here[g] + (div if adjoint else k[3][g] * div)
                     if step == STEPS - 1:
                         write(w, g, moved)
@@ -135,39 +135,48 @@
         write_pair(out_b, pair, *[jnp.where(odd, s, n) for n, s in zip(north, south)])
 
 
+def edge_columns(fields, tile, lane):
+    edges = turn(tile(0), HALO)
+    for f in range(1, fields):
+        edges = jnp.where(lane // SLOT == f, turn(tile(f), f * SLOT + HALO), edges)
+    return edges
+
+
 def strip_tiles(fields, eofs, tile, lane):
     pair = eofs // 2
-    zero = jnp.zeros((SUB, LANES), jnp.float32)
     west_out, east_out = [], []
+    inner = lane & (SLOT - 1)
     at = lane & (SLOT // 2 - 1)
     for j in range(pair):
-        west, east = zero, zero
-        for half in range(2):
-            for f in range(fields):
-                cells = tile(f * eofs + half * pair + j)
-                start = f * SLOT + half * (SLOT // 2)
-                mask = (lane >= start) & (lane < start + HALO)
-                west = jnp.where(mask, turn(cells, start), west)
-                east = jnp.where(mask, turn(cells, start + HALO - LANES), east)
+        first = edge_columns(fields, lambda f: tile(f * eofs + j), lane)
+        second = edge_columns(fields, lambda f: tile(f * eofs + pair + j), lane)
+        second = turn(second, SLOT // 2)
+        west = jnp.where((inner >= HALO - 4) & (inner < 2 * HALO), first, second)
         high, low = split(west)
-        west_out.append(jnp.where(at < HALO, high, turn(low, HALO)))
+        west_out.append(jnp.where((at >= HALO - 4) & (at < HALO), turn(low, -4), high))
+        east = jnp.where(inner < SLOT // 2, first, second)
         high, low = split(east)
         east_out.append(jnp.where(at < HALO, high, turn(low, 4)))
-    west, east = zero, zero
-    for k in range(4):
-        cells = tile(fields * eofs + k)
-        start = k * SLOT
-        mask = (lane >= start) & (lane < start + HALO)
-        west = jnp.where(mask, turn(cells, start), west)
-        east = jnp.where(mask, turn(cells, start + HALO - LANES), east)
+    edges = edge_columns(4, lambda k: tile(fields * eofs + k), lane)
+    west = jnp.where((inner >= HALO) & (inner < 2 * HALO), edges, 0.0)
+    east = jnp.where(inner < HALO, edges, 0.0)
     for cells, out in ((west, west_out), (east, east_out)):
         high, low = split(cells)
         out.append(high + turn(low, SLOT // 2))
     return west_out, east_out
 
 
-def own_strips_kernel(fields, eofs, members, own, panels, west, east, edges, *tiles):
+def slice_kernel(members, fields, panels, *tiles):
     _, _, me = position()
+    for s, block in enumerate(tiles):
+        start = pl.multiple_of(lax.rem(me + s, len(tiles)) * LANES, LANES)
+        for m in range(members):
+            for f in range(fields):
+                block[m, f] = panels[m, f, :, :, pl.ds(start, LANES)]
+
+
+def own_strips_kernel(fields, eofs, members, own, eof_basis, *rest):
+    tiles, (west, east, edges, basis) = rest[:-4], rest[-4:]
     lane = lane_grid()
 
     def tile(i):
@@ -178,12 +187,7 @@
             write_pair(ref, pair, *packed[2 * pair : 2 * pair + 2])
 
     count = len(tiles)
-    for s, block in enumerate(tiles):
-        start = pl.multiple_of(lax.rem(me + s, count) * LANES, LANES)
-        for m in range(members):
-            for f in range(fields):
-                block[m, f] = panels[m, f, :, :, pl.ds(start, LANES)]
-    depth = panels.shape[2] * SUB
+    depth = tiles[0].shape[2] * SUB
     column = lax.broadcasted_iota(jnp.int32, (LANES, 2 * LANES), 0)
     target = lax.broadcasted_iota(jnp.int32, (LANES, 2 * LANES), 1)
     west_ok = (target < LANES) & (column < STEPS)
@@ -205,93 +209,6 @@
         edges[s, 0] = total[:, :LANES]
         edges[s, 1] = total[:, LANES:]
 
-
-def pack_kernel(fields, eofs, from_a, from_b, west, east, *rest):
-    panel_edges, (out_a, out_b, north, south) = rest[:-4], rest[-4:]
-    ring_odd, odd, _ = position()
-    lane = lane_grid()
-    sub = lax.broadcasted_iota(jnp.int32, (SUB, LANES), 0)
-    for pair in range((fields * eofs + 4) // 2):
-        above, below = decode_rows(from_a, from_b, odd, sub, pair)
-        at = pl.ds(pair * 2 * SUB, 2 * SUB)
-        north[at, :] = jnp.concatenate(above, axis=0)
-        south[at, :] = jnp.concatenate(below, axis=0)
-
-    def put(pair, mine_west, mine_east):
-        write_pair(out_a, pair, *[jnp.where(ring_odd, w, e) for w, e in zip(mine_west, mine_east)])
-        write_pair(out_b, pair, *[jnp.where(ring_odd, e, w) for w, e in zip(mine_west, mine_east)])
-
-    pairs = (eofs // 2 + 1) // 2
-    for t, ref in ((0, north), (2, south)):
-        tiles = strip_tiles(fields, eofs, lambda i: ref[pl.ds(i * SUB, SUB), :], lane)
-        for j in range(pairs):
-            put(t * pairs + j, tiles[0][2 * j : 2 * j + 2], tiles[1][2 * j : 2 * j + 2])
-    for j in range(pairs):
-        put(pairs + j, read_pair(west, j), read_pair(east, j))
-    for edges in panel_edges:
-        for j in range(edges.shape[2] // (2 * SUB)):
-            put(3 * pairs + j, read_pair(edges.at[0, 0], j), read_pair(edges.at[0, 1], j))
-
-
-def own_columns(fields, eofs, tile, strip, t, lane):
-    shifted = (lane + STEPS) & (LANES - 1)
-    zero = jnp.zeros((SUB, LANES), jnp.float32)
-    for e in range(eofs):
-        west, east = zero, zero
-        for f in range(fields):
-            cells = tile(f * eofs + e)
-            west = jnp.where(lane // SLOT == f, turn(cells, f * SLOT + HALO), west)
-            east = jnp.where(
-                shifted // SLOT == f, turn(cells, f * SLOT - STEPS - LANES + HALO), east
-            )
-        strip[t, pl.ds(e * SUB, SUB), :] = west
-        strip[t, pl.ds((eofs + e) * SUB, SUB), :] = east
-    strip[t, pl.ds(2 * eofs * SUB, 4 * SUB), :] = jnp.zeros((4 * SUB, LANES), jnp.float32)
-
-
-def main_kernel(
-    fields, eofs, own, north, south,
-    adj, strip, coeff_main, coeff_strip, wide, first, second,
-):
-    lane = lane_grid()
-    inner = lane & (SLOT - 1)
-    shifted = (lane + STEPS) & (LANES - 1)
-    zero = jnp.zeros((SUB, LANES), jnp.float32)
-    total = fields * eofs
-
-    def tile(t, i):
-        return (north, own, south)[t][pl.ds(i * SUB, SUB), :]
-
-    for k in range(4):
-        for t in range(3):
-            cells = tile(t, total + k)
-            if k < 3:
-                cells = time_step * cells
-            at = pl.ds(t * SUB, SUB)
-            coeff_main[k, at, :] = cells
-            west, east = zero, zero
-            for f in range(fields):
-                start = f * SLOT
-                west = jnp.where(lane // SLOT == f, turn(cells, start + HALO), west)
-                east = jnp.where(
-                    shifted // SLOT == f, turn(cells, start - STEPS - LANES + HALO), east
-                )
-            coeff_strip[0, k, at, :] = jnp.where((inner >= HALO) & (inner < 2 * HALO), west, 0.0)
-            coeff_strip[1, k, at, :] = jnp.where((shifted & (SLOT - 1)) < HALO, east, 0.0)
-    main_coefficients(coeff_main, wide)
-    groups = total // SUB
-    read, write = main_rows(own, north, south, adj)
-    diffuse(read, write, lambda k, w: [wide[k, w]] * groups, groups, first, second, True)
-    for t in range(3):
-        own_columns(fields, eofs, lambda i: tile(t, i), strip, t, lane)
-
-
-def project_kernel(fields, eofs, members, eof_basis, panel, *rest):
-    arrived, (basis, proj) = rest[:-2], rest[-2:]
-    _, _, me = position()
-    blocks = (panel,) + arrived
-    count = len(blocks)
-    depth = panel.shape[2] * SUB
     levels = eof_basis.shape[1]
 
     def grid(shape, dim):
@@ -311,6 +228,74 @@
         wide = jnp.where(same_row, wide, 0.0).astype(jnp.bfloat16)
         for h in range(count):
             basis[h, f] = wide[:, h * depth : (h + 1) * depth]
+
+
+def pack_kernel(fields, eofs, from_a, from_b, west, east, *rest):
+    panel_edges, (out_a, out_b, north, south) = rest[:-4], rest[-4:]
+    ring_odd, odd, _ = position()
+    lane = lane_grid()
+    sub = lax.broadcasted_iota(jnp.int32, (SUB, LANES), 0)
+    for pair in range((fields * eofs + 4) // 2):
+        above, below = decode_rows(from_a, from_b, odd, sub, pair)
+        at = pl.ds(pair * 2 * SUB, 2 * SUB)
+        north[at, :] = jnp.concatenate(above, axis=0)
+        south[at, :] = jnp.concatenate(below, axis=0)
+
+    def put(pair, mine_west, mine_east):
+        write_pair(out_a, pair, *[jnp.where(ring_odd, w, e) for w, e in zip(mine_west, mine_east)])
+        write_pair(out_b, pair, *[jnp.where(ring_odd, e, w) for w, e in zip(mine_west, mine_east)])
+
+    pairs = (eofs // 2 + 1) // 2
+    for t, ref in ((0, north), (2, south)):
+        tiles = strip_tiles(fields, eofs, lambda i: ref[pl.ds(i * SUB, SUB), :], lane)
+        for j in range(pairs):
+            put(t * pairs + j, tiles[0][2 * j : 2 * j + 2], tiles[1][2 * j : 2 * j + 2])
+    for j in range(pairs):
+        put(pairs + j, read_pair(west, j), read_pair(east, j))
+    for edges in panel_edges[:1]:
+        for j in range(edges.shape[2] // (2 * SUB)):
+            put(3 * pairs + j, read_pair(edges.at[0, 0], j), read_pair(edges.at[0, 1], j))
+
+
+def main_kernel(
+    fields, eofs, own, north, south,
+    adj, strip, coeff_main, coeff_strip, wide, first, second,
+):
+    lane = lane_grid()
+    inner = lane & (SLOT - 1)
+    total = fields * eofs
+
+    def tile(t, i):
+        return (north, own, south)[t][pl.ds(i * SUB, SUB), :]
+
+    for k in range(4):
+        for t in range(3):
+            cells = tile(t, total + k)
+            if k < 3:
+                cells = time_step * cells
+            at = pl.ds(t * SUB, SUB)
+            coeff_main[k, at, :] = cells
+            edges = edge_columns(fields, lambda f: cells, lane)
+            west = (inner >= HALO) & (inner < 2 * HALO)
+            coeff_strip[0, k, at, :] = jnp.where(west, edges, 0.0)
+            coeff_strip[1, k, at, :] = jnp.where(inner < HALO, edges, 0.0)
+    main_coefficients(coeff_main, wide)
+    groups = total // SUB
+    read, write = main_rows(own, north, south, adj)
+    diffuse(read, write, lambda k, w: [wide[k, w]] * groups, groups, first, second, True)
+    for t in range(3):
+        for e in range(eofs):
+            strip[t, pl.ds(e * SUB, SUB), :] = edge_columns(
+                fields, lambda f: tile(t, f * eofs + e), lane
+            )
+
+
+def project_kernel(fields, eofs, members, basis, panel, *rest):
+    arrived, proj = rest[:-1], rest[-1]
+    _, _, me = position()
+    blocks = (panel,) + arrived
+    count = len(blocks)
+    depth = panel.shape[2] * SUB
     for f in range(fields):
         total = None
         for s, block in enumerate(blocks):
@@ -386,7 +371,7 @@
         return zip(*sides)
 
     west_mask = inner < HALO
-    east_mask = (inner >= STEPS) & (inner < STEPS + HALO)
+    east_mask = (inner >= HALO) & (inner < 2 * HALO)
     at16 = lane & (SLOT // 2 - 1)
     pairs = (pair + 1) // 2
     for t in range(3):
@@ -398,30 +383,25 @@
         for j in range(pair):
             west, east = west_tiles[j], east_tiles[j]
             west = west + jnp.where((at16 >= HALO - 4) & (at16 < HALO), turn(west, -4), 0.0)
-            east = east + jnp.where(at16 < 4, turn(east, -HALO), 0.0)
+            east = east + jnp.where(at16 >= HALO, turn(east, 4), 0.0)
             for half in range(2):
                 e = half * pair + j
-                at = pl.ds(e * SUB, SUB)
-                strip[t, at, :] = jnp.where(
-                    west_mask, turn(west, -half * (SLOT // 2)), strip_own[t, at, :]
-                )
-                at = pl.ds((eofs + e) * SUB, SUB)
-                strip[t, at, :] = jnp.where(
-                    east_mask, turn(east, STEPS - half * (SLOT // 2)), strip_own[t, at, :]
-                )
-        at = pl.ds(2 * eofs * SUB, 4 * SUB)
-        strip[t, at, :] = strip_own[t, at, :]
+                mine = strip_own[t, pl.ds(e * SUB, SUB), :]
+                if half:
+                    west, east = turn(west, -(SLOT // 2)), turn(east, -(SLOT // 2))
+                strip[t, pl.ds(e * SUB, SUB), :] = jnp.where(west_mask, west, mine)
+                strip[t, pl.ds((eofs + e) * SUB, SUB), :] = jnp.where(east_mask, east, mine)
+        strip[t, pl.ds(2 * eofs * SUB, 4 * SUB), :] = jnp.zeros((4 * SUB, LANES), jnp.float32)
         at = pl.ds(t * SUB, SUB)
         for side, (cells, mask) in enumerate(
             ((west_tiles[pair], west_mask), (east_tiles[pair], east_mask))
         ):
             cells = cells + turn(cells, -(SLOT // 2))
+            turned = [cells] + [turn(cells, i * SLOT) for i in range(1, 4)]
             for k in range(4):
-                mine = jnp.where(lane // SLOT == k, cells, 0.0)
-                mine = mine + turn(mine, SLOT)
-                mine = mine + turn(mine, 2 * SLOT)
-                if side == 1:
-                    mine = turn(mine, STEPS)
+                mine = turned[-k % 4]
+                for f in range(1, 4):
+                    mine = jnp.where(lane // SLOT == f, turned[(f - k) % 4], mine)
                 if k < 3:
                     mine = time_step * mine
                 coeff_strip[side, k, at, :] = jnp.where(mask, mine, coeff_own[side, k, at, :])
@@ -456,14 +436,11 @@
     proj_strip[pl.ds(eofs * SUB, eofs * SUB), :] = halo[:, LANES:]
 
     scores = [jnp.zeros((SUB, LANES), jnp.float32) for _ in range(members)]
-    for f in range(fields):
-        for e in range(eofs):
+    for e in range(eofs):
+        edges = both_edges(eofs, adj_strip, e, inner)
+        for f in range(fields):
             at = pl.ds((f * eofs + e) * SUB, SUB)
-            west = turn(adj_strip[pl.ds(e * SUB, SUB), :], -f * SLOT - HALO)
-            east = turn(adj_strip[pl.ds((eofs + e) * SUB, SUB), :], LANES - STEPS - f * SLOT)
-            cells = jnp.where(
-                lane < STEPS, west, jnp.where(lane >= LANES - STEPS, east, adj[at, :])
-            )
+            cells = jnp.where(own_edge(lane), turn(edges, -f * SLOT - HALO), adj[at, :])
             for m in range(members):
                 scores[m] = scores[m] + proj[m, at, :] * cells
     scores = [s / (members - 1) for s in scores]
@@ -483,9 +460,10 @@
         for e in range(eofs):
             at = pl.ds((side * eofs + e) * SUB, SUB)
             cells = adj_strip[at, :]
-            spread = turn(cells, -STEPS)
+            start = HALO if side else STEPS
+            spread = turn(cells, -start)
             for m in range(1, members):
-                spread = jnp.where(slot == m, turn(cells, m * SUB - STEPS), spread)
+                spread = jnp.where(slot == m, turn(cells, m * SUB - start), spread)
             total = total + proj_strip[at, :] * spread
         total = total + turn(total, SLOT)
         total = (total + turn(total, 2 * SLOT)) / (members - 1)
@@ -503,26 +481,39 @@
     put_rows(out_a, out_b, tiles, odd, sub)
 
 
-def beyond_columns(eofs, packed, strip, t, lane):
+def both_edges(eofs, strip, e, inner):
+    west, east = strip[pl.ds(e * SUB, SUB), :], strip[pl.ds((eofs + e) * SUB, SUB), :]
+    return jnp.where(inner < HALO, east, west)
+
+
+def own_edge(lane):
+    return (lane < STEPS) | (lane >= LANES - STEPS)
+
+
+def fill_strip(fields, eofs, tile, packed, strip, t, lane):
     inner = lane & (SLOT - 1)
-    mask = (inner >= STEPS) & (inner < HALO)
-    for i in range(2 * eofs):
-        cells = turn(packed[pl.ds(i // 4 * SUB, SUB), :], STEPS - (i % 4) * SUB)
-        at = pl.ds(i * SUB, SUB)
-        strip[t, at, :] = jnp.where(mask, cells, strip[t, at, :])
+    west = (inner >= STEPS) & (inner < HALO)
+    east = (inner >= HALO) & (inner < HALO + STEPS)
+    for e in range(eofs):
+        edges = edge_columns(fields, lambda f: tile(f * eofs + e), lane)
+        for side, mask in enumerate((west, east)):
+            i = side * eofs + e
+            shift = (HALO if side else STEPS) - (i % 4) * SUB
+            beyond = turn(packed[pl.ds(i // 4 * SUB, SUB), :], shift)
+            strip[t, pl.ds(i * SUB, SUB), :] = jnp.where(mask, beyond, edges)
+    strip[t, pl.ds(2 * eofs * SUB, 4 * SUB), :] = jnp.zeros((4 * SUB, LANES), jnp.float32)
 
 
 def before_forward_kernel(fields, eofs, own, halo, coeff_main, coeff_strip, wide, wide_strip, strip):
     lane = lane_grid()
     main_coefficients(coeff_main, wide)
     strip_coefficients(coeff_strip, wide_strip, eofs)
-    own_columns(fields, eofs, lambda i: own[pl.ds(i * SUB, SUB), :], strip, 0, lane)
-    beyond_columns(eofs, halo, strip, 0, lane)
+    fill_strip(fields, eofs, lambda i: own[pl.ds(i * SUB, SUB), :], halo, strip, 0, lane)
 
 
 def forward_kernel(
     fields, eofs, own, from_a, from_b, wide, wide_strip, strip_own,
-    out, north, south, strip, strip_out, first, second,
+    result, out, north, south, strip, strip_out, first, second, sems,
 ):
     _, odd, _ = position()
     lane = lane_grid()
@@ -534,45 +525,50 @@
         north[at, :] = jnp.concatenate(above, axis=0)
         south[at, :] = jnp.concatenate(below, axis=0)
     for t, ref in ((0, north), (2, south)):
-        own_columns(fields, eofs, lambda i: ref[pl.ds(i * SUB, SUB), :], strip, t, lane)
-        beyond_columns(eofs, ref.at[pl.ds(total * SUB, 2 * eofs // 4 * SUB)], strip, t, lane)
+        packed = ref.at[pl.ds(total * SUB, 2 * eofs // 4 * SUB)]
+        fill_strip(
+            fields, eofs, lambda i: ref[pl.ds(i * SUB, SUB), :], packed, strip, t, lane
+        )
     strip[1] = strip_own[0]
     groups = total // SUB
     read_main, write_main = main_rows(own, north, south, out)
     read_strip, write_strip, coeff_strip = strip_rows(strip, strip_out, wide_strip)
 
     def read(w, g):
-        return read_main(w, g) if g < groups else read_strip(w, g - groups)
+        return read_strip(w, g) if g < 3 else read_main(w, g - 3)
 
     def write(w, g, cells):
-        if g < groups:
-            write_main(w, g, cells)
+        if g < 3:
+            write_strip(w, g, cells)
         else:
-            write_strip(w, g - groups, cells)
+            write_main(w, g - 3, cells)
 
     def coeff(k, w):
-        return [wide[k, w]] * groups + coeff_strip(k, w)
+        return coeff_strip(k, w) + [wide[k, w]] * groups
 
     diffuse(read, write, coeff, groups + 3, first, second, False)
+    edges = [both_edges(eofs, strip_out, e, lane & (SLOT - 1)) for e in range(eofs)]
+    copies = []
     for f in range(fields):
         for e in range(eofs):
             at = pl.ds((f * eofs + e) * SUB, SUB)
-            west = turn(strip_out[pl.ds(e * SUB, SUB), :], -f * SLOT - HALO)
-            east = turn(strip_out[pl.ds((eofs + e) * SUB, SUB), :], LANES - STEPS - f * SLOT)
-            out[at, :] = jnp.where(
-                lane < STEPS, west, jnp.where(lane >= LANES - STEPS, east, out[at, :])
-            )
-
-
-def call(kernel, args, outs, scratch=(), flops=1_000_000):
+            out[at, :] = jnp.where(own_edge(lane), turn(edges[e], -f * SLOT - HALO), out[at, :])
+        part = pl.ds(f * eofs * SUB, eofs * SUB)
+        copies.append(pltpu.make_async_copy(out.at[part], result.at[part], sems.at[f]))
+        copies[-1].start()
+    for copy in copies:
+        copy.wait()
+
+
+def call(kernel, args, outs, scratch=(), flops=1_000_000, out_space=pltpu.VMEM):
     whole = pl.BlockSpec(memory_space=pltpu.VMEM)
     moved = sum(a.size * a.dtype.itemsize for a in list(args) + list(outs))
     return pl.pallas_call(
         kernel,
         in_specs=[whole] * len(args),
-        out_specs=[whole] * len(outs),
+        out_specs=[pl.BlockSpec(memory_space=out_space)] * len(outs),
         out_shape=list(outs),
-        scratch_shapes=[pltpu.VMEM(*s) for s in scratch],
+        scratch_shapes=[pltpu.VMEM(*s) if isinstance(s, tuple) else s for s in scratch],
         compiler_params=pltpu.CompilerParams(vmem_limit_bytes=24 * 2**20),
         cost_estimate=pl.CostEstimate(flops=flops, bytes_accessed=moved, transcendentals=0),
     )(*args)
@@ -614,12 +610,19 @@
     sent_a, sent_b = call(start_kernel, [own], [bf16(all_rows, col_count)] * 2)
     from_a, from_b = swap_a(sent_a, "gy"), swap_b(sent_b, "gy", False)
     strip_sent = (eofs // 2 + 1) * row_count
-    west, east, edges, *tiles = call(
+    tiles = call(
+        functools.partial(slice_kernel, members, fields),
+        [panels],
+        [bf16(*panels.shape[:-1], col_count)] * count,
+    )
+    west, east, edges, basis = call(
         functools.partial(own_strips_kernel, fields, eofs, members),
-        [own, panels],
+        [own, eof_basis, *tiles],
         [bf16(strip_sent, col_count)] * 2
-        + [bf16(count, 2, depth * row_count, col_count)]
-        + [bf16(*panels.shape[:-1], col_count)] * count,
+        + [
+            bf16(count, 2, depth * row_count, col_count),
+            bf16(count, fields, eofs * row_count, depth * row_count),
+        ],
     )
     arrived = [
         lax.ppermute(tiles[s], "gz", [(i, (i + s) % count) for i in range(count)])
@@ -638,7 +641,7 @@
     sent_a, sent_b, north, south = call(
         functools.partial(pack_kernel, fields, eofs),
         [from_a, from_b, west, east, *panel_sent],
-        [bf16(3 * strip_sent + len(panel_sent) * depth * row_count, col_count)] * 2
+        [bf16(3 * strip_sent + (count == 2) * depth * row_count, col_count)] * 2
         + [f32(rows + 4 * row_count, col_count)] * 2,
     )
     got_a, got_b = swap_a(sent_a, RING), swap_b(sent_b, RING, True)
@@ -651,20 +654,17 @@
         [own, north, south],
         [
             f32(rows, col_count),
-            f32(3, strip_rows, col_count),
+            f32(3, eofs * row_count, col_count),
             f32(4, 3 * row_count, col_count),
             f32(2, 4, 3 * row_count, col_count),
         ],
         [((4, WINDOW, SUB, LANES), jnp.float32)] + main_scratch,
         flops=20_000_000,
     )
-    basis, proj = call(
+    (proj,) = call(
         functools.partial(project_kernel, fields, eofs, members),
-        [eof_basis, tiles[0], *arrived],
-        [
-            bf16(count, fields, eofs * row_count, depth * row_count),
-            f32(members, rows, col_count),
-        ],
+        [basis, tiles[0], *arrived],
+        [f32(members, rows, col_count)],
         flops=20_000_000,
     )
     packed = 2 * eofs // 4
@@ -701,9 +701,12 @@
         functools.partial(forward_kernel, fields, eofs),
         [combined, from_a, from_b, wide, wide_strip, strip],
         [f32(rows, col_count)],
-        [((sent_a.shape[0], LANES), jnp.float32)] * 2
+        [((rows, LANES), jnp.float32)]
+        + [((sent_a.shape[0], LANES), jnp.float32)] * 2
         + [((3, strip_rows, LANES), jnp.float32), ((strip_rows, LANES), jnp.float32)]
-        + [((WINDOW, total + 3 * SUB, LANES), jnp.float32)] * 2,
+        + [((WINDOW, total + 3 * SUB, LANES), jnp.float32)] * 2
+        + [pltpu.SemaphoreType.DMA((fields,))],
+        out_space=pltpu.HBM,
     )
     return result.reshape(control.shape)
 

time: 28.7 us -> 27.8 us (0.969)
  Pallas kernels: 8.3 us -> 7.58 us
  starting transfers between devices: 11.9 us -> 11.5 us
    pallas_call x8 -> x9, Pallas kernels: 8.3 us -> 7.58 us  [call(): pl.pallas_call(kernel, in_specs=[whole] * len(args), out_specs=[pl.BlockS...]
    ppermute x3, waiting for transfers between devices: 2.32 us -> 2.93 us  [swap_a(): return lax.ppermute(values, axes, [(i, i ^ 1) for i in range(count)])]
    ppermute x3, waiting for transfers between devices: 3.34 us -> 2.84 us  [swap_b(): return lax.ppermute(values, axes, pairs + [(j, i) for i, j in pairs])]
    ppermute x3, starting transfers between devices: 7.46 us -> 7.08 us  [swap_b(): return lax.ppermute(values, axes, pairs + [(j, i) for i, j in pairs])]
  transfers between devices with their start and end apart: 8 -> 8, of which waited for: 4 -> 5; matrix products, arithmetic and copies ran while one was open for 0% -> 0% of each run, Pallas kernels for 12% -> 11%
where the time goes in v5:
time: 27.8 us; the launch traced here: 27.4 us
  starting transfers between devices  11.5 us (41%)
  Pallas kernels  7.58 us (27%)
  waiting for transfers between devices  6.99 us (25%)
  other arithmetic  1.01 us (4%)
    pallas_call x9, Pallas kernels, call(): pl.pallas_call(kernel, in_specs=[whole] * len(args), out_specs=[pl.BlockS...  7.58 us
    ppermute x3, starting transfers between devices, swap_b(): return lax.ppermute(values, axes, pairs + [(j, i) for i, j in pairs])  7.08 us
    ppermute x3, waiting for transfers between devices, swap_a(): return lax.ppermute(values, axes, [(i, i ^ 1) for i in range(count)])  2.93 us
    ppermute x3, waiting for transfers between devices, swap_b(): return lax.ppermute(values, axes, pairs + [(j, i) for i, j in pairs])  2.84 us
    ppermute x1, starting transfers between devices, per_device(): lax.ppermute(jnp.where(me == 1, edges[1, 0], edges[1, 1]), RING, pairs)  2.64 us
    ppermute x1, waiting for transfers between devices, per_device(): lax.ppermute(tiles[s], 'gz', [(i, (i + s) % count) for i in range(count)])  1.23 us
    ppermute x3, starting transfers between devices, swap_a(): return lax.ppermute(values, axes, [(i, i ^ 1) for i in range(count)])  1.22 us
    concatenate x1, other arithmetic, per_device(): jnp.concatenate([control.reshape(rows, col_count), coefficients.reshape(4...  1 us
  transfers between devices with their start and end apart: 8, of which 5 were waited for; matrix products, arithmetic and copies ran while one was open for 0% of the time, Pallas kernels for 11%

profile of v5, /device:TPU:10, one launch (start us, length us, event | category | flops | bytes accessed | tf_op | source)
XLA Modules:
  0.0 27.4 jit_solution(8246742469154622524)
XLA Ops:
  0.0 0.0 copy-start
  0.0 1.0 %pad_maximum_fusion.own = f32[352,128]{1,0:T(8,128)S(1)} fusion(f32[32,128]{1,0:T(8,128)} %bitcast.6, f32[320,128]{1,0:T(8,128)} %bitcast.5), kind=kLoop, calls=%fused_computation | loop fusion | flops 45056 | bytes 360448 | tf_op jit(solution)/shard_map/concatenate | solution.py:607
  1.0 0.1 shard_map.46
  1.1 0.5 %collective-permute-start = (bf16[352,128]{1,0:T(8,128)(2,1)S(1)}, bf16[352,128]{1,0:T(8,128)(2,1)S(1)}, u32[]{:S(2)}, u32[]{:S(2)}) collective-permute-start(bf16[352,128]{1,0:T(8,128)(2,1)S(1)} %get-tuple-element.29), channel_id=1, source_target_pairs={{0,2},{2,0},{4,6},{6,4},{1,3},{3,1},{5,7},{7,5},{8,10},{10,8},{12,... | collective-permute-start | bytes 270344 | tf_op jit(solution)/shard_map/ppermute | solution.py:28
  1.6 4.6 %collective-permute-start.1 = (bf16[352,128]{1,0:T(8,128)(2,1)S(1)}, bf16[352,128]{1,0:T(8,128)(2,1)S(1)}, u32[]{:S(2)}, u32[]{:S(2)}) collective-permute-start(bf16[352,128]{1,0:T(8,128)(2,1)S(1)} %get-tuple-element.30), channel_id=1, source_target_pairs={{2,4},{4,2},{3,5},{5,3},{10,12},{12,10},{11,13},{13,11},{18,20},{2... | collective-permute-start | bytes 270344 | tf_op jit(solution)/shard_map/ppermute | solution.py:36
  6.2 0.0 copy-done
  6.2 0.0 copy-start.1
  6.2 0.1 shard_map.47
  6.3 0.6 %collective-permute-start.5 = (bf16[4,4,8,8,128]{4,3,2,1,0:T(8,128)(2,1)S(1)}, bf16[4,4,8,8,128]{4,3,2,1,0:T(8,128)(2,1)S(1)}, u32[]{:S(2)}, u32[]{:S(2)}) collective-permute-start(bf16[4,4,8,8,128]{4,3,2,1,0:T(8,128)(2,1)S(1)} %get-tuple-element.32.rest_1_), channel_id=1, source_target_pairs={{0,1},{1,0},{2,3},{3,2},{4,5},{5,4},{6,7},{7,6},{8,9},{9,8},{10,11... | collective-permute-start | bytes 786440 | tf_op jit(solution)/shard_map/ppermute | solution.py:628
  6.9 0.0 copy-done.1
  6.9 0.1 copy.5.eof_basis
  7.1 0.7 %shard_map.48 = (bf16[48,128]{1,0:T(8,128)(2,1)S(1)}, bf16[48,128]{1,0:T(8,128)(2,1)S(1)}, bf16[2,2,64,128]{3,2,1,0:T(8,128)(2,1)S(1)}, bf16[2,4,80,64]{3,2,1,0:T(8,128)(2,1)S(1)}) custom-call(f32[352,128]{1,0:T(8,128)S(1)} %pad_maximum_fusion.own, bf16[4,16,10]{2,1,0:T(8,128)(2,1)S(1)} %copy.5.eof_basis, ...), custom_call_target="tpu_custom_call" | custom-call | flops 1000000 | bytes 877824 | tf_op jit(solution)/shard_map/pallas_call | solution.py:566
  7.8 0.0 collective-permute-done.from_a
  7.8 0.9 %collective-permute-done.1.from_b = bf16[352,128]{1,0:T(8,128)(2,1)S(1)} collective-permute-done((bf16[352,128]{1,0:T(8,128)(2,1)S(1)}, bf16[352,128]{1,0:T(8,128)(2,1)S(1)}, u32[]{:S(2)}, u32[]{:S(2)}) %collective-permute-start.1) | collective-permute-done | bytes 90144 | tf_op jit(solution)/shard_map/ppermute | solution.py:36
  8.7 0.3 %shard_map.49 = (bf16[208,128]{1,0:T(8,128)(2,1)S(1)}, bf16[208,128]{1,0:T(8,128)(2,1)S(1)}, f32[352,128]{1,0:T(8,128)S(1)}, f32[352,128]{1,0:T(8,128)S(1)}) custom-call(bf16[352,128]{1,0:T(8,128)(2,1)S(1)} %collective-permute-done.from_a, bf16[352,128]{1,0:T(8,128)(2,1)S(1)} %collective-permute-done.1.from_b, bf16[48,128]{1,0:T(8,128)(2,1)S(1)} %get-tuple-element.33.west, ...), custom_call_target="tpu_custom_call" | custom-call | flops 1000000 | bytes 737280 | tf_op jit(solution)/shard_map/pallas_call | solution.py:566
  9.0 0.6 %collective-permute-start.2 = (bf16[208,128]{1,0:T(8,128)(2,1)S(1)}, bf16[208,128]{1,0:T(8,128)(2,1)S(1)}, u32[]{:S(2)}, u32[]{:S(2)}) collective-permute-start(bf16[208,128]{1,0:T(8,128)(2,1)S(1)} %get-tuple-element.36), channel_id=1, source_target_pairs={{0,1},{1,0},{8,9},{9,8},{16,17},{17,16},{24,25},{25,24},{2,3},{3,2... | collective-permute-start | bytes 159752 | tf_op jit(solution)/shard_map/ppermute | solution.py:28
  9.6 0.0 collective-permute-start.3
  9.6 2.6 %collective-permute-start.4 = (bf16[64,128]{1,0:T(8,128)(2,1)S(1)}, bf16[64,128]{1,0:T(8,128)(2,1)S(1)}, u32[]{:S(2)}, u32[]{:S(2)}) collective-permute-start(bf16[64,128]{1,0:T(8,128)(2,1)S(1)} %select_bitcast_fusion), channel_id=1, source_target_pairs={{0,8},{8,16},{16,24},{24,0},{1,25},{9,1},{17,9},{25,17},{2,10},{10... | collective-permute-start | bytes 49160 | tf_op jit(solution)/shard_map/ppermute | solution.py:636
  12.3 1.5 %shard_map.50 = (f32[320,128]{1,0:T(8,128)S(1)}, f32[3,80,128]{2,1,0:T(8,128)S(1)}, f32[4,24,128]{2,1,0:T(8,128)S(1)}, f32[2,4,24,128]{3,2,1,0:T(8,128)S(1)}) custom-call(f32[352,128]{1,0:T(8,128)S(1)} %pad_maximum_fusion.own, f32[352,128]{1,0:T(8,128)S(1)} %get-tuple-element.39.north, f32[352,128]{1,0:T(8,128)S(1)} %get-tuple-element.40.south), custom_call_target="tpu_custom_call" | custom-call | flops 20000000 | bytes 974848 | tf_op jit(solution)/shard_map/pallas_call | solution.py:566
  13.8 1.2 %collective-permute-done.5.rest_0_ = bf16[4,4,8,8,128]{4,3,2,1,0:T(8,128)(2,1)S(1)} collective-permute-done((bf16[4,4,8,8,128]{4,3,2,1,0:T(8,128)(2,1)S(1)}, bf16[4,4,8,8,128]{4,3,2,1,0:T(8,128)(2,1)S(1)}, u32[]{:S(2)}, u32[]{:S(2)}) %collective-permute-start.5) | collective-permute-done | bytes 262176 | tf_op jit(solution)/shard_map/ppermute | solution.py:628
  15.0 0.3 %shard_map.51.rest_4_ = f32[4,320,128]{2,1,0:T(8,128)S(1)} custom-call(bf16[2,4,80,64]{3,2,1,0:T(8,128)(2,1)S(1)} %get-tuple-element.38.basis.rest_2_, bf16[4,4,8,8,128]{4,3,2,1,0:T(8,128)(2,1)S(1)} %get-tuple-element.31.rest_0_.panel, bf16[4,4,8,8,128]{4,3,2,1,0:T(8,128)(2,1)S(1)} %collective-permute-done.5.rest_0_), custom_call_target="tpu_custom_call" | custom-call | flops 20000000 | bytes 1261568 | tf_op jit(solution)/shard_map/pallas_call | solution.py:566
  15.3 0.0 collective-permute-done.4.rest_1_
  15.3 0.3 collective-permute-done.2.got_a
  15.6 0.0 collective-permute-done.3.got_b
  15.6 1.7 %shard_map.52 = (bf16[368,128]{1,0:T(8,128)(2,1)S(1)}, bf16[368,128]{1,0:T(8,128)(2,1)S(1)}, f32[320,128]{1,0:T(8,128)S(1)}, f32[40,128]{1,0:T(8,128)S(1)}, f32[2,4,24,128]{3,2,1,0:T(8,128)S(1)}) custom-call(bf16[208,128]{1,0:T(8,128)(2,1)S(1)} %collective-permute-done.2.got_a, bf16[208,128]{1,0:T(8,128)(2,1)S(1)} %collective-permute-done.3.got_b, ...), custom_call_target="tpu_custom_call" | custom-call | flops 1000000 | bytes 1781760 | tf_op jit(solution)/shard_map/pallas_call | solution.py:566
  17.4 0.1 collective-permute-start.6
  17.4 2.5 %collective-permute-start.7 = (bf16[368,128]{1,0:T(8,128)(2,1)S(1)}, bf16[368,128]{1,0:T(8,128)(2,1)S(1)}, u32[]{:S(2)}, u32[]{:S(2)}) collective-permute-start(bf16[368,128]{1,0:T(8,128)(2,1)S(1)} %get-tuple-element.46), channel_id=1, source_target_pairs={{2,4},{4,2},{3,5},{5,3},{10,12},{12,10},{11,13},{13,11},{18,20},{2... | collective-permute-start | bytes 282632 | tf_op jit(solution)/shard_map/ppermute | solution.py:36
  19.9 0.1 shard_map.53
  20.1 2.7 %collective-permute-done.6.from_a = bf16[368,128]{1,0:T(8,128)(2,1)S(1)} collective-permute-done((bf16[368,128]{1,0:T(8,128)(2,1)S(1)}, bf16[368,128]{1,0:T(8,128)(2,1)S(1)}, u32[]{:S(2)}, u32[]{:S(2)}) %collective-permute-start.6) | collective-permute-done | bytes 94240 | tf_op jit(solution)/shard_map/ppermute | solution.py:28
  22.7 1.9 %collective-permute-done.7.from_b = bf16[368,128]{1,0:T(8,128)(2,1)S(1)} collective-permute-done((bf16[368,128]{1,0:T(8,128)(2,1)S(1)}, bf16[368,128]{1,0:T(8,128)(2,1)S(1)}, u32[]{:S(2)}, u32[]{:S(2)}) %collective-permute-start.7) | collective-permute-done | bytes 94240 | tf_op jit(solution)/shard_map/ppermute | solution.py:36
  24.6 2.7 %shard_map.54 = f32[320,128]{1,0:T(8,128)} custom-call(f32[320,128]{1,0:T(8,128)S(1)} %get-tuple-element.44.own, bf16[368,128]{1,0:T(8,128)(2,1)S(1)} %collective-permute-done.6.from_a, bf16[368,128]{1,0:T(8,128)(2,1)S(1)} %collective-permute-done.7.from_b, f32[4,20,8,128]{3,2,1,0:T(8,128)S(1)} %get-tuple-element.50.wide, ...), custom_call_target="tpu_custom_call" | custom-call | flops 1000000 | bytes 1925120 | tf_op jit(solution)/shard_map/pallas_call | solution.py:566
  (1 shorter events, 0.0 us)
Async XLA Ops:
  0.0 6.2 %copy-start = (bf16[4,4,8,8,256]{4,3,2,1,0:T(8,128)(2,1)S(1)}, bf16[4,4,8,8,256]{4,3,2,1,0:T(8,128)(2,1)}, u32[]{:S(2)}) copy-start(bf16[4,4,8,8,256]{4,3,2,1,0:T(8,128)(2,1)} %panels.1) | copy-start | bytes 1572868
  1.1 6.7 %collective-permute-start = (bf16[352,128]{1,0:T(8,128)(2,1)S(1)}, bf16[352,128]{1,0:T(8,128)(2,1)S(1)}, u32[]{:S(2)}, u32[]{:S(2)}) collective-permute-start(bf16[352,128]{1,0:T(8,128)(2,1)S(1)} %get-tuple-element.29), channel_id=1, source_target_pairs={{0,2},{2,0},{4,6},{6,4},{1,3},{3,1},{5,7},{7,5},{8,10},{10,8},{12,... | collective-permute-start | bytes 270344 | tf_op jit(solution)/shard_map/ppermute | solution.py:28
  1.6 7.1 %collective-permute-start.1 = (bf16[352,128]{1,0:T(8,128)(2,1)S(1)}, bf16[352,128]{1,0:T(8,128)(2,1)S(1)}, u32[]{:S(2)}, u32[]{:S(2)}) collective-permute-start(bf16[352,128]{1,0:T(8,128)(2,1)S(1)} %get-tuple-element.30), channel_id=1, source_target_pairs={{2,4},{4,2},{3,5},{5,3},{10,12},{12,10},{11,13},{13,11},{18,20},{2... | collective-permute-start | bytes 270344 | tf_op jit(solution)/shard_map/ppermute | solution.py:36
  6.2 0.7 %copy-start.1 = (bf16[4,16,10]{1,0,2:T(4,128)(2,1)S(1)}, bf16[4,16,10]{1,0,2:T(4,128)(2,1)}, u32[]{:S(2)}) copy-start(bf16[4,16,10]{1,0,2:T(4,128)(2,1)} %param.5) | copy-start | bytes 3844
  6.3 8.7 %collective-permute-start.5 = (bf16[4,4,8,8,128]{4,3,2,1,0:T(8,128)(2,1)S(1)}, bf16[4,4,8,8,128]{4,3,2,1,0:T(8,128)(2,1)S(1)}, u32[]{:S(2)}, u32[]{:S(2)}) collective-permute-start(bf16[4,4,8,8,128]{4,3,2,1,0:T(8,128)(2,1)S(1)} %get-tuple-element.32.rest_1_), channel_id=1, source_target_pairs={{0,1},{1,0},{2,3},{3,2},{4,5},{5,4},{6,7},{7,6},{8,9},{9,8},{10,11... | collective-permute-start | bytes 786440 | tf_op jit(solution)/shard_map/ppermute | solution.py:628
  9.0 6.6 %collective-permute-start.2 = (bf16[208,128]{1,0:T(8,128)(2,1)S(1)}, bf16[208,128]{1,0:T(8,128)(2,1)S(1)}, u32[]{:S(2)}, u32[]{:S(2)}) collective-permute-start(bf16[208,128]{1,0:T(8,128)(2,1)S(1)} %get-tuple-element.36), channel_id=1, source_target_pairs={{0,1},{1,0},{8,9},{9,8},{16,17},{17,16},{24,25},{25,24},{2,3},{3,2... | collective-permute-start | bytes 159752 | tf_op jit(solution)/shard_map/ppermute | solution.py:28
  9.6 6.0 %collective-permute-start.3 = (bf16[208,128]{1,0:T(8,128)(2,1)S(1)}, bf16[208,128]{1,0:T(8,128)(2,1)S(1)}, u32[]{:S(2)}, u32[]{:S(2)}) collective-permute-start(bf16[208,128]{1,0:T(8,128)(2,1)S(1)} %get-tuple-element.37), channel_id=1, source_target_pairs={{1,8},{9,16},{17,24},{25,0},{8,1},{16,9},{24,17},{0,25},{3,10},{11... | collective-permute-start | bytes 159752 | tf_op jit(solution)/shard_map/ppermute | solution.py:36
  9.6 5.7 %collective-permute-start.4 = (bf16[64,128]{1,0:T(8,128)(2,1)S(1)}, bf16[64,128]{1,0:T(8,128)(2,1)S(1)}, u32[]{:S(2)}, u32[]{:S(2)}) collective-permute-start(bf16[64,128]{1,0:T(8,128)(2,1)S(1)} %select_bitcast_fusion), channel_id=1, source_target_pairs={{0,8},{8,16},{16,24},{24,0},{1,25},{9,1},{17,9},{25,17},{2,10},{10... | collective-permute-start | bytes 49160 | tf_op jit(solution)/shard_map/ppermute | solution.py:636
  17.4 5.4 %collective-permute-start.6 = (bf16[368,128]{1,0:T(8,128)(2,1)S(1)}, bf16[368,128]{1,0:T(8,128)(2,1)S(1)}, u32[]{:S(2)}, u32[]{:S(2)}) collective-permute-start(bf16[368,128]{1,0:T(8,128)(2,1)S(1)} %get-tuple-element.45), channel_id=1, source_target_pairs={{0,2},{2,0},{4,6},{6,4},{1,3},{3,1},{5,7},{7,5},{8,10},{10,8},{12,... | collective-permute-start | bytes 282632 | tf_op jit(solution)/shard_map/ppermute | solution.py:28
  17.4 7.2 %collective-permute-start.7 = (bf16[368,128]{1,0:T(8,128)(2,1)S(1)}, bf16[368,128]{1,0:T(8,128)(2,1)S(1)}, u32[]{:S(2)}, u32[]{:S(2)}) collective-permute-start(bf16[368,128]{1,0:T(8,128)(2,1)S(1)} %get-tuple-element.46), channel_id=1, source_target_pairs={{2,4},{4,2},{3,5},{5,3},{10,12},{12,10},{11,13},{13,11},{18,20},{2... | collective-permute-start | bytes 282632 | tf_op jit(solution)/shard_map/ppermute | solution.py:36

commit v6 on v5

--- a/solution.py
+++ b/solution.py
@@ -50,18 +50,64 @@
     return lax.broadcasted_iota(jnp.int32, (SUB, LANES), 1)
 
 
-def diffuse(read, write, coeff, groups, first, second, adjoint):
+def early_rows(step):
+    rows = range(STEPS + 1 + step, STEPS + SUB - 1 - step)
+    return rows, sum(len(early_rows(s)[0]) for s in range(step))
+
+
+def diffuse_early(read, coeff, groups, kept, kept_flux):
+    step = 0
+    while len(early_rows(step)[0]):
+        rows, base = early_rows(step)
+        last_rows, last_base = early_rows(step - 1)
+
+        def fetch(w):
+            if step == 0:
+                return [read(w, g) for g in range(groups)]
+            at = last_base + w - last_rows[0]
+            return [kept[at, pl.ds(g * SUB, SUB), :] for g in range(groups)]
+
+        here, south = fetch(rows[0] - 1), None
+        for w in range(rows[0] - 1, rows[-1] + 1):
+            k = [coeff(i, w) for i in range(4)]
+            north = fetch(w + 1)
+            flux = []
+            for g in range(groups):
+                east_diff = turn(here[g], -1) - here[g]
+                north_diff = north[g] - here[g]
+                flux.append(k[1][g] * east_diff + k[2][g] * north_diff)
+                if w in rows:
+                    flux_east = k[0][g] * east_diff + k[1][g] * north_diff
+                    div = (flux[g] - south[g]) + flux_east - turn(flux_east, 1)
+                    kept[base + w - rows[0], pl.ds(g * SUB, SUB), :] = here[g] + k[3][g] * div
+                if w == rows[-1]:
+                    kept_flux[step, pl.ds(g * SUB, SUB), :] = flux[g]
+            here, south = north, flux
+        step += 1
+
+
+def diffuse(read, write, coeff, groups, first, second, adjoint, early=None):
     state, spare = None, first
+    made = range(0)
     for step in range(STEPS):
         low, high = step, WINDOW - 1 - step
+        last, made = made, early_rows(step)[0] if early else range(0)
 
         def fetch(w):
             if state is None:
                 return [read(w, g) for g in range(groups)]
+            if w in last:
+                at = early_rows(step - 1)[1] + w - last[0]
+                return [early[0][at, pl.ds(g * SUB, SUB), :] for g in range(groups)]
             return [state[w, pl.ds(g * SUB, SUB), :] for g in range(groups)]
 
         here, seen, south = fetch(low), None, None
         for w in range(low, high):
+            if w in made:
+                if w == made[-1]:
+                    here = fetch(w + 1)
+                    south = [early[1][step, pl.ds(g * SUB, SUB), :] for g in range(groups)]
+                continue
             k = [coeff(i, w) for i in range(4)]
             north = fetch(w + 1)
             if adjoint:
@@ -504,15 +550,33 @@
     strip[t, pl.ds(2 * eofs * SUB, 4 * SUB), :] = jnp.zeros((4 * SUB, LANES), jnp.float32)
 
 
-def before_forward_kernel(fields, eofs, own, halo, coeff_main, coeff_strip, wide, wide_strip, strip):
+def forward_coefficients(wide, wide_strip, groups):
+    def coeff(k, w):
+        strip = [wide_strip[k, w, pl.ds(g * SUB, SUB), :] for g in range(3)]
+        return strip + [wide[k, w]] * groups
+
+    return coeff
+
+
+def before_forward_kernel(
+    fields, eofs, own, halo, coeff_main, coeff_strip, wide, wide_strip, strip, kept, kept_flux
+):
     lane = lane_grid()
     main_coefficients(coeff_main, wide)
     strip_coefficients(coeff_strip, wide_strip, eofs)
     fill_strip(fields, eofs, lambda i: own[pl.ds(i * SUB, SUB), :], halo, strip, 0, lane)
 
+    def read(w, g):
+        at = pl.ds((g if g < 3 else g - 3) * SUB * SUB + w - STEPS, SUB, stride=SUB)
+        return strip[0, at, :] if g < 3 else own[at, :]
+
+    groups = own.shape[0] // (SUB * SUB)
+    coeff = forward_coefficients(wide, wide_strip, groups)
+    diffuse_early(read, coeff, groups + 3, kept, kept_flux)
+
 
 def forward_kernel(
-    fields, eofs, own, from_a, from_b, wide, wide_strip, strip_own,
+    fields, eofs, own, from_a, from_b, wide, wide_strip, strip_own, kept, kept_flux,
     result, out, north, south, strip, strip_out, first, second, sems,
 ):
     _, odd, _ = position()
@@ -532,7 +596,7 @@
     strip[1] = strip_own[0]
     groups = total // SUB
     read_main, write_main = main_rows(own, north, south, out)
-    read_strip, write_strip, coeff_strip = strip_rows(strip, strip_out, wide_strip)
+    read_strip, write_strip, _ = strip_rows(strip, strip_out, wide_strip)
 
     def read(w, g):
         return read_strip(w, g) if g < 3 else read_main(w, g - 3)
@@ -543,10 +607,9 @@
         else:
             write_main(w, g - 3, cells)
 
-    def coeff(k, w):
-        return coeff_strip(k, w) + [wide[k, w]] * groups
-
-    diffuse(read, write, coeff, groups + 3, first, second, False)
+    coeff = forward_coefficients(wide, wide_strip, groups)
+    early = (kept, kept_flux)
+    diffuse(read, write, coeff, groups + 3, first, second, False, early)
     edges = [both_edges(eofs, strip_out, e, lane & (SLOT - 1)) for e in range(eofs)]
     copies = []
     for f in range(fields):
@@ -687,19 +750,23 @@
         + strip_scratch,
     )
     from_a, from_b = swap_a(sent_a, "gy"), swap_b(sent_b, "gy", False)
-    wide, wide_strip, strip = call(
+    early_steps = (SUB - 1) // 2
+    early_count = sum(len(early_rows(step)[0]) for step in range(early_steps))
+    wide, wide_strip, strip, kept, kept_flux = call(
         functools.partial(before_forward_kernel, fields, eofs),
         [combined, halo, coeff_main, coeff_strip],
         [
             f32(4, WINDOW, SUB, LANES),
             f32(4, WINDOW, 3 * SUB, LANES),
             f32(1, strip_rows, LANES),
+            f32(early_count, total + 3 * SUB, LANES),
+            f32(early_steps, total + 3 * SUB, LANES),
         ],
         flops=20_000_000,
     )
     (result,) = call(
         functools.partial(forward_kernel, fields, eofs),
-        [combined, from_a, from_b, wide, wide_strip, strip],
+        [combined, from_a, from_b, wide, wide_strip, strip, kept, kept_flux],
         [f32(rows, col_count)],
         [((rows, LANES), jnp.float32)]
         + [((sent_a.shape[0], LANES), jnp.float32)] * 2

time: 27.8 us -> 27.6 us (level)
  waiting for transfers between devices: 6.99 us -> 6.51 us
  Pallas kernels: 7.58 us -> 7.86 us
    ppermute x3, waiting for transfers between devices: 2.93 us -> 2.44 us  [swap_a(): return lax.ppermute(values, axes, [(i, i ^ 1) for i in range(count)])]
    pallas_call x9, Pallas kernels: 7.58 us -> 7.86 us  [call(): pl.pallas_call(kernel, in_specs=[whole] * len(args), out_specs=[pl.BlockS...]
  transfers between devices with their start and end apart: 8 -> 8, of which waited for: 5 -> 5; matrix products, arithmetic and copies ran while one was open for 0% -> 0% of each run, Pallas kernels for 11% -> 13%
where the time goes in v6:
time: 27.6 us; the launch traced here: 27.2 us
  starting transfers between devices  11.5 us (42%)
  Pallas kernels  7.86 us (28%)
  waiting for transfers between devices  6.51 us (24%)
  other arithmetic  1.01 us (4%)
    pallas_call x9, Pallas kernels, call(): pl.pallas_call(kernel, in_specs=[whole] * len(args), out_specs=[pl.BlockS...  7.86 us
    ppermute x3, starting transfers between devices, swap_b(): return lax.ppermute(values, axes, pairs + [(j, i) for i, j in pairs])  7.08 us
    ppermute x3, waiting for transfers between devices, swap_b(): return lax.ppermute(values, axes, pairs + [(j, i) for i, j in pairs])  2.84 us
    ppermute x1, starting transfers between devices, per_device(): lax.ppermute(jnp.where(me == 1, edges[1, 0], edges[1, 1]), RING, pairs)  2.64 us
    ppermute x3, waiting for transfers between devices, swap_a(): return lax.ppermute(values, axes, [(i, i ^ 1) for i in range(count)])  2.44 us
    ppermute x1, waiting for transfers between devices, per_device(): lax.ppermute(tiles[s], 'gz', [(i, (i + s) % count) for i in range(count)])  1.23 us
    ppermute x3, starting transfers between devices, swap_a(): return lax.ppermute(values, axes, [(i, i ^ 1) for i in range(count)])  1.22 us
    concatenate x1, other arithmetic, per_device(): jnp.concatenate([control.reshape(rows, col_count), coefficients.reshape(4...  1 us
  transfers between devices with their start and end apart: 8, of which 5 were waited for; matrix products, arithmetic and copies ran while one was open for 0% of the time, Pallas kernels for 13%

profile of v6, /device:TPU:10, one launch (start us, length us, event | category | flops | bytes accessed | tf_op | source)
XLA Modules:
  0.0 27.2 jit_solution(10134216155713873714)
XLA Ops:
  0.0 0.0 copy-start
  0.0 1.0 %pad_maximum_fusion.own = f32[352,128]{1,0:T(8,128)S(1)} fusion(f32[32,128]{1,0:T(8,128)} %bitcast.6, f32[320,128]{1,0:T(8,128)} %bitcast.5), kind=kLoop, calls=%fused_computation | loop fusion | flops 45056 | bytes 360448 | tf_op jit(solution)/shard_map/concatenate | solution.py:670
  1.0 0.1 shard_map.46
  1.1 0.5 %collective-permute-start = (bf16[352,128]{1,0:T(8,128)(2,1)S(1)}, bf16[352,128]{1,0:T(8,128)(2,1)S(1)}, u32[]{:S(2)}, u32[]{:S(2)}) collective-permute-start(bf16[352,128]{1,0:T(8,128)(2,1)S(1)} %get-tuple-element.31), channel_id=1, source_target_pairs={{0,2},{2,0},{4,6},{6,4},{1,3},{3,1},{5,7},{7,5},{8,10},{10,8},{12,... | collective-permute-start | bytes 270344 | tf_op jit(solution)/shard_map/ppermute | solution.py:28
  1.6 4.6 %collective-permute-start.1 = (bf16[352,128]{1,0:T(8,128)(2,1)S(1)}, bf16[352,128]{1,0:T(8,128)(2,1)S(1)}, u32[]{:S(2)}, u32[]{:S(2)}) collective-permute-start(bf16[352,128]{1,0:T(8,128)(2,1)S(1)} %get-tuple-element.32), channel_id=1, source_target_pairs={{2,4},{4,2},{3,5},{5,3},{10,12},{12,10},{11,13},{13,11},{18,20},{2... | collective-permute-start | bytes 270344 | tf_op jit(solution)/shard_map/ppermute | solution.py:36
  6.2 0.0 copy-done
  6.2 0.0 copy-start.1
  6.2 0.1 shard_map.47
  6.3 0.6 %collective-permute-start.5 = (bf16[4,4,8,8,128]{4,3,2,1,0:T(8,128)(2,1)S(1)}, bf16[4,4,8,8,128]{4,3,2,1,0:T(8,128)(2,1)S(1)}, u32[]{:S(2)}, u32[]{:S(2)}) collective-permute-start(bf16[4,4,8,8,128]{4,3,2,1,0:T(8,128)(2,1)S(1)} %get-tuple-element.34.rest_1_), channel_id=1, source_target_pairs={{0,1},{1,0},{2,3},{3,2},{4,5},{5,4},{6,7},{7,6},{8,9},{9,8},{10,11... | collective-permute-start | bytes 786440 | tf_op jit(solution)/shard_map/ppermute | solution.py:691
  6.9 0.0 copy-done.1
  6.9 0.1 copy.5.eof_basis
  7.1 0.7 %shard_map.48 = (bf16[48,128]{1,0:T(8,128)(2,1)S(1)}, bf16[48,128]{1,0:T(8,128)(2,1)S(1)}, bf16[2,2,64,128]{3,2,1,0:T(8,128)(2,1)S(1)}, bf16[2,4,80,64]{3,2,1,0:T(8,128)(2,1)S(1)}) custom-call(f32[352,128]{1,0:T(8,128)S(1)} %pad_maximum_fusion.own, bf16[4,16,10]{2,1,0:T(8,128)(2,1)S(1)} %copy.5.eof_basis, ...), custom_call_target="tpu_custom_call" | custom-call | flops 1000000 | bytes 877824 | tf_op jit(solution)/shard_map/pallas_call | solution.py:629
  7.8 0.0 collective-permute-done.from_a
  7.8 0.9 %collective-permute-done.1.from_b = bf16[352,128]{1,0:T(8,128)(2,1)S(1)} collective-permute-done((bf16[352,128]{1,0:T(8,128)(2,1)S(1)}, bf16[352,128]{1,0:T(8,128)(2,1)S(1)}, u32[]{:S(2)}, u32[]{:S(2)}) %collective-permute-start.1) | collective-permute-done | bytes 90144 | tf_op jit(solution)/shard_map/ppermute | solution.py:36
  8.7 0.3 %shard_map.49 = (bf16[208,128]{1,0:T(8,128)(2,1)S(1)}, bf16[208,128]{1,0:T(8,128)(2,1)S(1)}, f32[352,128]{1,0:T(8,128)S(1)}, f32[352,128]{1,0:T(8,128)S(1)}) custom-call(bf16[352,128]{1,0:T(8,128)(2,1)S(1)} %collective-permute-done.from_a, bf16[352,128]{1,0:T(8,128)(2,1)S(1)} %collective-permute-done.1.from_b, bf16[48,128]{1,0:T(8,128)(2,1)S(1)} %get-tuple-element.35.west, ...), custom_call_target="tpu_custom_call" | custom-call | flops 1000000 | bytes 737280 | tf_op jit(solution)/shard_map/pallas_call | solution.py:629
  9.0 0.6 %collective-permute-start.2 = (bf16[208,128]{1,0:T(8,128)(2,1)S(1)}, bf16[208,128]{1,0:T(8,128)(2,1)S(1)}, u32[]{:S(2)}, u32[]{:S(2)}) collective-permute-start(bf16[208,128]{1,0:T(8,128)(2,1)S(1)} %get-tuple-element.38), channel_id=1, source_target_pairs={{0,1},{1,0},{8,9},{9,8},{16,17},{17,16},{24,25},{25,24},{2,3},{3,2... | collective-permute-start | bytes 159752 | tf_op jit(solution)/shard_map/ppermute | solution.py:28
  9.6 0.0 collective-permute-start.3
  9.6 2.6 %collective-permute-start.4 = (bf16[64,128]{1,0:T(8,128)(2,1)S(1)}, bf16[64,128]{1,0:T(8,128)(2,1)S(1)}, u32[]{:S(2)}, u32[]{:S(2)}) collective-permute-start(bf16[64,128]{1,0:T(8,128)(2,1)S(1)} %select_bitcast_fusion), channel_id=1, source_target_pairs={{0,8},{8,16},{16,24},{24,0},{1,25},{9,1},{17,9},{25,17},{2,10},{10... | collective-permute-start | bytes 49160 | tf_op jit(solution)/shard_map/ppermute | solution.py:699
  12.3 1.5 %shard_map.50 = (f32[320,128]{1,0:T(8,128)S(1)}, f32[3,80,128]{2,1,0:T(8,128)S(1)}, f32[4,24,128]{2,1,0:T(8,128)S(1)}, f32[2,4,24,128]{3,2,1,0:T(8,128)S(1)}) custom-call(f32[352,128]{1,0:T(8,128)S(1)} %pad_maximum_fusion.own, f32[352,128]{1,0:T(8,128)S(1)} %get-tuple-element.41.north, f32[352,128]{1,0:T(8,128)S(1)} %get-tuple-element.42.south), custom_call_target="tpu_custom_call" | custom-call | flops 20000000 | bytes 974848 | tf_op jit(solution)/shard_map/pallas_call | solution.py:629
  13.8 1.2 %collective-permute-done.5.rest_0_ = bf16[4,4,8,8,128]{4,3,2,1,0:T(8,128)(2,1)S(1)} collective-permute-done((bf16[4,4,8,8,128]{4,3,2,1,0:T(8,128)(2,1)S(1)}, bf16[4,4,8,8,128]{4,3,2,1,0:T(8,128)(2,1)S(1)}, u32[]{:S(2)}, u32[]{:S(2)}) %collective-permute-start.5) | collective-permute-done | bytes 262176 | tf_op jit(solution)/shard_map/ppermute | solution.py:691
  15.0 0.3 %shard_map.51.rest_4_ = f32[4,320,128]{2,1,0:T(8,128)S(1)} custom-call(bf16[2,4,80,64]{3,2,1,0:T(8,128)(2,1)S(1)} %get-tuple-element.40.basis.rest_2_, bf16[4,4,8,8,128]{4,3,2,1,0:T(8,128)(2,1)S(1)} %get-tuple-element.33.rest_0_.panel, bf16[4,4,8,8,128]{4,3,2,1,0:T(8,128)(2,1)S(1)} %collective-permute-done.5.rest_0_), custom_call_target="tpu_custom_call" | custom-call | flops 20000000 | bytes 1261568 | tf_op jit(solution)/shard_map/pallas_call | solution.py:629
  15.3 0.0 collective-permute-done.4.rest_1_
  15.3 0.3 collective-permute-done.2.got_a
  15.6 0.0 collective-permute-done.3.got_b
  15.6 1.8 %shard_map.52 = (bf16[368,128]{1,0:T(8,128)(2,1)S(1)}, bf16[368,128]{1,0:T(8,128)(2,1)S(1)}, f32[320,128]{1,0:T(8,128)S(1)}, f32[40,128]{1,0:T(8,128)S(1)}, f32[2,4,24,128]{3,2,1,0:T(8,128)S(1)}) custom-call(bf16[208,128]{1,0:T(8,128)(2,1)S(1)} %collective-permute-done.2.got_a, bf16[208,128]{1,0:T(8,128)(2,1)S(1)} %collective-permute-done.3.got_b, ...), custom_call_target="tpu_custom_call" | custom-call | flops 1000000 | bytes 1781760 | tf_op jit(solution)/shard_map/pallas_call | solution.py:629
  17.4 0.1 collective-permute-start.6
  17.4 2.5 %collective-permute-start.7 = (bf16[368,128]{1,0:T(8,128)(2,1)S(1)}, bf16[368,128]{1,0:T(8,128)(2,1)S(1)}, u32[]{:S(2)}, u32[]{:S(2)}) collective-permute-start(bf16[368,128]{1,0:T(8,128)(2,1)S(1)} %get-tuple-element.48), channel_id=1, source_target_pairs={{2,4},{4,2},{3,5},{5,3},{10,12},{12,10},{11,13},{13,11},{18,20},{2... | collective-permute-start | bytes 282632 | tf_op jit(solution)/shard_map/ppermute | solution.py:36
  19.9 0.6 %shard_map.53 = (f32[4,20,8,128]{3,2,1,0:T(8,128)S(1)}, f32[4,20,24,128]{3,2,1,0:T(8,128)S(1)}, f32[1,192,128]{2,1,0:T(8,128)S(1)}, f32[12,64,128]{2,1,0:T(8,128)S(1)}, f32[3,64,128]{2,1,0:T(8,128)S(1)}) custom-call(f32[320,128]{1,0:T(8,128)S(1)} %get-tuple-element.46.own, f32[40,128]{1,0:T(8,128)S(1)} %get-tuple-element.49.halo, ...), custom_call_target="tpu_custom_call" | custom-call | flops 20000000 | bytes 2232320 | tf_op jit(solution)/shard_map/pallas_call | solution.py:629
  20.6 2.2 %collective-permute-done.6.from_a = bf16[368,128]{1,0:T(8,128)(2,1)S(1)} collective-permute-done((bf16[368,128]{1,0:T(8,128)(2,1)S(1)}, bf16[368,128]{1,0:T(8,128)(2,1)S(1)}, u32[]{:S(2)}, u32[]{:S(2)}) %collective-permute-start.6) | collective-permute-done | bytes 94240 | tf_op jit(solution)/shard_map/ppermute | solution.py:28
  22.7 1.9 %collective-permute-done.7.from_b = bf16[368,128]{1,0:T(8,128)(2,1)S(1)} collective-permute-done((bf16[368,128]{1,0:T(8,128)(2,1)S(1)}, bf16[368,128]{1,0:T(8,128)(2,1)S(1)}, u32[]{:S(2)}, u32[]{:S(2)}) %collective-permute-start.7) | collective-permute-done | bytes 94240 | tf_op jit(solution)/shard_map/ppermute | solution.py:36
  24.6 2.5 %shard_map.54 = f32[320,128]{1,0:T(8,128)} custom-call(f32[320,128]{1,0:T(8,128)S(1)} %get-tuple-element.46.own, bf16[368,128]{1,0:T(8,128)(2,1)S(1)} %collective-permute-done.6.from_a, bf16[368,128]{1,0:T(8,128)(2,1)S(1)} %collective-permute-done.7.from_b, f32[4,20,8,128]{3,2,1,0:T(8,128)S(1)} %get-tuple-element.52.wide, ...), custom_call_target="tpu_custom_call" | custom-call | flops 1000000 | bytes 2416640 | tf_op jit(solution)/shard_map/pallas_call | solution.py:629
  (1 shorter events, 0.0 us)
Async XLA Ops:
  0.0 6.2 %copy-start = (bf16[4,4,8,8,256]{4,3,2,1,0:T(8,128)(2,1)S(1)}, bf16[4,4,8,8,256]{4,3,2,1,0:T(8,128)(2,1)}, u32[]{:S(2)}) copy-start(bf16[4,4,8,8,256]{4,3,2,1,0:T(8,128)(2,1)} %panels.1) | copy-start | bytes 1572868
  1.1 6.7 %collective-permute-start = (bf16[352,128]{1,0:T(8,128)(2,1)S(1)}, bf16[352,128]{1,0:T(8,128)(2,1)S(1)}, u32[]{:S(2)}, u32[]{:S(2)}) collective-permute-start(bf16[352,128]{1,0:T(8,128)(2,1)S(1)} %get-tuple-element.31), channel_id=1, source_target_pairs={{0,2},{2,0},{4,6},{6,4},{1,3},{3,1},{5,7},{7,5},{8,10},{10,8},{12,... | collective-permute-start | bytes 270344 | tf_op jit(solution)/shard_map/ppermute | solution.py:28
  1.6 7.1 %collective-permute-start.1 = (bf16[352,128]{1,0:T(8,128)(2,1)S(1)}, bf16[352,128]{1,0:T(8,128)(2,1)S(1)}, u32[]{:S(2)}, u32[]{:S(2)}) collective-permute-start(bf16[352,128]{1,0:T(8,128)(2,1)S(1)} %get-tuple-element.32), channel_id=1, source_target_pairs={{2,4},{4,2},{3,5},{5,3},{10,12},{12,10},{11,13},{13,11},{18,20},{2... | collective-permute-start | bytes 270344 | tf_op jit(solution)/shard_map/ppermute | solution.py:36
  6.2 0.7 %copy-start.1 = (bf16[4,16,10]{1,0,2:T(4,128)(2,1)S(1)}, bf16[4,16,10]{1,0,2:T(4,128)(2,1)}, u32[]{:S(2)}) copy-start(bf16[4,16,10]{1,0,2:T(4,128)(2,1)} %param.5) | copy-start | bytes 3844
  6.3 8.7 %collective-permute-start.5 = (bf16[4,4,8,8,128]{4,3,2,1,0:T(8,128)(2,1)S(1)}, bf16[4,4,8,8,128]{4,3,2,1,0:T(8,128)(2,1)S(1)}, u32[]{:S(2)}, u32[]{:S(2)}) collective-permute-start(bf16[4,4,8,8,128]{4,3,2,1,0:T(8,128)(2,1)S(1)} %get-tuple-element.34.rest_1_), channel_id=1, source_target_pairs={{0,1},{1,0},{2,3},{3,2},{4,5},{5,4},{6,7},{7,6},{8,9},{9,8},{10,11... | collective-permute-start | bytes 786440 | tf_op jit(solution)/shard_map/ppermute | solution.py:691
  9.0 6.6 %collective-permute-start.2 = (bf16[208,128]{1,0:T(8,128)(2,1)S(1)}, bf16[208,128]{1,0:T(8,128)(2,1)S(1)}, u32[]{:S(2)}, u32[]{:S(2)}) collective-permute-start(bf16[208,128]{1,0:T(8,128)(2,1)S(1)} %get-tuple-element.38), channel_id=1, source_target_pairs={{0,1},{1,0},{8,9},{9,8},{16,17},{17,16},{24,25},{25,24},{2,3},{3,2... | collective-permute-start | bytes 159752 | tf_op jit(solution)/shard_map/ppermute | solution.py:28
  9.6 6.0 %collective-permute-start.3 = (bf16[208,128]{1,0:T(8,128)(2,1)S(1)}, bf16[208,128]{1,0:T(8,128)(2,1)S(1)}, u32[]{:S(2)}, u32[]{:S(2)}) collective-permute-start(bf16[208,128]{1,0:T(8,128)(2,1)S(1)} %get-tuple-element.39), channel_id=1, source_target_pairs={{1,8},{9,16},{17,24},{25,0},{8,1},{16,9},{24,17},{0,25},{3,10},{11... | collective-permute-start | bytes 159752 | tf_op jit(solution)/shard_map/ppermute | solution.py:36
  9.6 5.7 %collective-permute-start.4 = (bf16[64,128]{1,0:T(8,128)(2,1)S(1)}, bf16[64,128]{1,0:T(8,128)(2,1)S(1)}, u32[]{:S(2)}, u32[]{:S(2)}) collective-permute-start(bf16[64,128]{1,0:T(8,128)(2,1)S(1)} %select_bitcast_fusion), channel_id=1, source_target_pairs={{0,8},{8,16},{16,24},{24,0},{1,25},{9,1},{17,9},{25,17},{2,10},{10... | collective-permute-start | bytes 49160 | tf_op jit(solution)/shard_map/ppermute | solution.py:699
  17.4 5.4 %collective-permute-start.6 = (bf16[368,128]{1,0:T(8,128)(2,1)S(1)}, bf16[368,128]{1,0:T(8,128)(2,1)S(1)}, u32[]{:S(2)}, u32[]{:S(2)}) collective-permute-start(bf16[368,128]{1,0:T(8,128)(2,1)S(1)} %get-tuple-element.47), channel_id=1, source_target_pairs={{0,2},{2,0},{4,6},{6,4},{1,3},{3,1},{5,7},{7,5},{8,10},{10,8},{12,... | collective-permute-start | bytes 282632 | tf_op jit(solution)/shard_map/ppermute | solution.py:28
  17.4 7.2 %collective-permute-start.7 = (bf16[368,128]{1,0:T(8,128)(2,1)S(1)}, bf16[368,128]{1,0:T(8,128)(2,1)S(1)}, u32[]{:S(2)}, u32[]{:S(2)}) collective-permute-start(bf16[368,128]{1,0:T(8,128)(2,1)S(1)} %get-tuple-element.48), channel_id=1, source_target_pairs={{2,4},{4,2},{3,5},{5,3},{10,12},{12,10},{11,13},{13,11},{18,20},{2... | collective-permute-start | bytes 282632 | tf_op jit(solution)/shard_map/ppermute | solution.py:36

commit v7 on v6

--- a/solution.py
+++ b/solution.py
@@ -398,7 +398,7 @@
     return read, write, coeff
 
 
-def combine_kernel(fields, eofs, members, got_a, got_b, *rest):
+def combine_kernel(fields, eofs, members, got_b, got_a, *rest):
     (
         basis, adj, proj, strip_own, coeff_own,
         out_a, out_b, combined, halo_out, coeff_strip,
@@ -707,7 +707,8 @@
         [bf16(3 * strip_sent + (count == 2) * depth * row_count, col_count)] * 2
         + [f32(rows + 4 * row_count, col_count)] * 2,
     )
-    got_a, got_b = swap_a(sent_a, RING), swap_b(sent_b, RING, True)
+    got_b = swap_b(sent_b, RING, True)
+    got_a = swap_a(sent_a, RING)
 
     strip_rows = (2 * eofs + 4) * row_count
     main_scratch = [((WINDOW, total, LANES), jnp.float32)] * 2
@@ -733,7 +734,7 @@
     packed = 2 * eofs // 4
     sent_a, sent_b, combined, halo, coeff_strip = call(
         functools.partial(combine_kernel, fields, eofs, members),
-        [got_a, got_b, *panel_parts, basis, adj, proj, strip, coeff_strip],
+        [got_b, got_a, *panel_parts, basis, adj, proj, strip, coeff_strip],
         [bf16((total + packed + 1) // 2 * 2 * row_count, col_count)] * 2
         + [
             f32(rows, col_count),

time: 27.6 us -> 27.4 us (level); the launches traced: 27.2 us -> 27.2 us
  waiting for transfers between devices: 6.51 us -> 7.1 us
  starting transfers between devices: 11.5 us -> 11 us
    ppermute x1, starting transfers between devices: 2.64 us -> 1.71 us  [per_device(): lax.ppermute(jnp.where(me == 1, edges[1, 0], edges[1, 1]), RING, pairs)]
    ppermute x3, starting transfers between devices: 1.22 us -> 1.84 us  [swap_a(): return lax.ppermute(values, axes, [(i, i ^ 1) for i in range(count)])]
    ppermute x3, waiting for transfers between devices: 2.44 us -> 2.81 us  [swap_a(): return lax.ppermute(values, axes, [(i, i ^ 1) for i in range(count)])]
where the time goes in v7:
time: 27.4 us; the launch traced here: 27.2 us
  starting transfers between devices  11 us (40%)
  Pallas kernels  7.85 us (29%)
  waiting for transfers between devices  7.1 us (26%)
  other arithmetic  1.01 us (4%)
    pallas_call x9, Pallas kernels, call(): pl.pallas_call(kernel, in_specs=[whole] * len(args), out_specs=[pl.BlockS...  7.85 us
    ppermute x3, starting transfers between devices, swap_b(): return lax.ppermute(values, axes, pairs + [(j, i) for i, j in pairs])  6.87 us
    ppermute x3, waiting for transfers between devices, swap_b(): return lax.ppermute(values, axes, pairs + [(j, i) for i, j in pairs])  2.84 us
    ppermute x3, waiting for transfers between devices, swap_a(): return lax.ppermute(values, axes, [(i, i ^ 1) for i in range(count)])  2.81 us
    ppermute x3, starting transfers between devices, swap_a(): return lax.ppermute(values, axes, [(i, i ^ 1) for i in range(count)])  1.84 us
    ppermute x1, starting transfers between devices, per_device(): lax.ppermute(jnp.where(me == 1, edges[1, 0], edges[1, 1]), RING, pairs)  1.71 us
    ppermute x1, waiting for transfers between devices, per_device(): lax.ppermute(tiles[s], 'gz', [(i, (i + s) % count) for i in range(count)])  1.45 us
    concatenate x1, other arithmetic, per_device(): jnp.concatenate([control.reshape(rows, col_count), coefficients.reshape(4...  1 us
  transfers between devices with their start and end apart: 8, of which 5 were waited for; matrix products, arithmetic and copies ran while one was open for 0% of the time, Pallas kernels for 13%

profile of v7, /device:TPU:10, one launch (start us, length us, event | category | flops | bytes accessed | tf_op | source)
XLA Modules:
  0.0 27.2 jit_solution(8431143514613398971)
XLA Ops:
  0.0 0.0 copy-start
  0.0 1.0 %pad_maximum_fusion.own = f32[352,128]{1,0:T(8,128)S(1)} fusion(f32[32,128]{1,0:T(8,128)} %bitcast.6, f32[320,128]{1,0:T(8,128)} %bitcast.5), kind=kLoop, calls=%fused_computation | loop fusion | flops 45056 | bytes 360448 | tf_op jit(solution)/shard_map/concatenate | solution.py:670
  1.0 0.1 shard_map.46
  1.1 0.5 %collective-permute-start = (bf16[352,128]{1,0:T(8,128)(2,1)S(1)}, bf16[352,128]{1,0:T(8,128)(2,1)S(1)}, u32[]{:S(2)}, u32[]{:S(2)}) collective-permute-start(bf16[352,128]{1,0:T(8,128)(2,1)S(1)} %get-tuple-element.31), channel_id=1, source_target_pairs={{0,2},{2,0},{4,6},{6,4},{1,3},{3,1},{5,7},{7,5},{8,10},{10,8},{12,... | collective-permute-start | bytes 270344 | tf_op jit(solution)/shard_map/ppermute | solution.py:28
  1.6 4.6 %collective-permute-start.1 = (bf16[352,128]{1,0:T(8,128)(2,1)S(1)}, bf16[352,128]{1,0:T(8,128)(2,1)S(1)}, u32[]{:S(2)}, u32[]{:S(2)}) collective-permute-start(bf16[352,128]{1,0:T(8,128)(2,1)S(1)} %get-tuple-element.32), channel_id=1, source_target_pairs={{2,4},{4,2},{3,5},{5,3},{10,12},{12,10},{11,13},{13,11},{18,20},{2... | collective-permute-start | bytes 270344 | tf_op jit(solution)/shard_map/ppermute | solution.py:36
  6.2 0.0 copy-done
  6.2 0.0 copy-start.1
  6.2 0.1 shard_map.47
  6.3 0.6 %collective-permute-start.5 = (bf16[4,4,8,8,128]{4,3,2,1,0:T(8,128)(2,1)S(1)}, bf16[4,4,8,8,128]{4,3,2,1,0:T(8,128)(2,1)S(1)}, u32[]{:S(2)}, u32[]{:S(2)}) collective-permute-start(bf16[4,4,8,8,128]{4,3,2,1,0:T(8,128)(2,1)S(1)} %get-tuple-element.34.rest_1_), channel_id=1, source_target_pairs={{0,1},{1,0},{2,3},{3,2},{4,5},{5,4},{6,7},{7,6},{8,9},{9,8},{10,11... | collective-permute-start | bytes 786440 | tf_op jit(solution)/shard_map/ppermute | solution.py:691
  6.9 0.0 copy-done.1
  6.9 0.1 copy.5.eof_basis
  7.1 0.7 %shard_map.48 = (bf16[48,128]{1,0:T(8,128)(2,1)S(1)}, bf16[48,128]{1,0:T(8,128)(2,1)S(1)}, bf16[2,2,64,128]{3,2,1,0:T(8,128)(2,1)S(1)}, bf16[2,4,80,64]{3,2,1,0:T(8,128)(2,1)S(1)}) custom-call(f32[352,128]{1,0:T(8,128)S(1)} %pad_maximum_fusion.own, bf16[4,16,10]{2,1,0:T(8,128)(2,1)S(1)} %copy.5.eof_basis, ...), custom_call_target="tpu_custom_call" | custom-call | flops 1000000 | bytes 877824 | tf_op jit(solution)/shard_map/pallas_call | solution.py:629
  7.8 0.0 collective-permute-done.from_a
  7.8 0.9 %collective-permute-done.1.from_b = bf16[352,128]{1,0:T(8,128)(2,1)S(1)} collective-permute-done((bf16[352,128]{1,0:T(8,128)(2,1)S(1)}, bf16[352,128]{1,0:T(8,128)(2,1)S(1)}, u32[]{:S(2)}, u32[]{:S(2)}) %collective-permute-start.1) | collective-permute-done | bytes 90144 | tf_op jit(solution)/shard_map/ppermute | solution.py:36
  8.7 0.3 %shard_map.49 = (bf16[208,128]{1,0:T(8,128)(2,1)S(1)}, bf16[208,128]{1,0:T(8,128)(2,1)S(1)}, f32[352,128]{1,0:T(8,128)S(1)}, f32[352,128]{1,0:T(8,128)S(1)}) custom-call(bf16[352,128]{1,0:T(8,128)(2,1)S(1)} %collective-permute-done.from_a, bf16[352,128]{1,0:T(8,128)(2,1)S(1)} %collective-permute-done.1.from_b, bf16[48,128]{1,0:T(8,128)(2,1)S(1)} %get-tuple-element.35.west, ...), custom_call_target="tpu_custom_call" | custom-call | flops 1000000 | bytes 737280 | tf_op jit(solution)/shard_map/pallas_call | solution.py:629
  9.0 0.1 collective-permute-start.2
  9.1 1.3 %collective-permute-start.3 = (bf16[208,128]{1,0:T(8,128)(2,1)S(1)}, bf16[208,128]{1,0:T(8,128)(2,1)S(1)}, u32[]{:S(2)}, u32[]{:S(2)}) collective-permute-start(bf16[208,128]{1,0:T(8,128)(2,1)S(1)} %get-tuple-element.39), channel_id=1, source_target_pairs={{0,1},{1,0},{8,9},{9,8},{16,17},{17,16},{24,25},{25,24},{2,3},{3,2... | collective-permute-start | bytes 159752 | tf_op jit(solution)/shard_map/ppermute | solution.py:28
  10.3 1.7 %collective-permute-start.4 = (bf16[64,128]{1,0:T(8,128)(2,1)S(1)}, bf16[64,128]{1,0:T(8,128)(2,1)S(1)}, u32[]{:S(2)}, u32[]{:S(2)}) collective-permute-start(bf16[64,128]{1,0:T(8,128)(2,1)S(1)} %select_bitcast_fusion), channel_id=1, source_target_pairs={{0,8},{8,16},{16,24},{24,0},{1,25},{9,1},{17,9},{25,17},{2,10},{10... | collective-permute-start | bytes 49160 | tf_op jit(solution)/shard_map/ppermute | solution.py:699
  12.0 1.5 %shard_map.50 = (f32[320,128]{1,0:T(8,128)S(1)}, f32[3,80,128]{2,1,0:T(8,128)S(1)}, f32[4,24,128]{2,1,0:T(8,128)S(1)}, f32[2,4,24,128]{3,2,1,0:T(8,128)S(1)}) custom-call(f32[352,128]{1,0:T(8,128)S(1)} %pad_maximum_fusion.own, f32[352,128]{1,0:T(8,128)S(1)} %get-tuple-element.41.north, f32[352,128]{1,0:T(8,128)S(1)} %get-tuple-element.42.south), custom_call_target="tpu_custom_call" | custom-call | flops 20000000 | bytes 974848 | tf_op jit(solution)/shard_map/pallas_call | solution.py:629
  13.6 1.4 %collective-permute-done.5.rest_0_ = bf16[4,4,8,8,128]{4,3,2,1,0:T(8,128)(2,1)S(1)} collective-permute-done((bf16[4,4,8,8,128]{4,3,2,1,0:T(8,128)(2,1)S(1)}, bf16[4,4,8,8,128]{4,3,2,1,0:T(8,128)(2,1)S(1)}, u32[]{:S(2)}, u32[]{:S(2)}) %collective-permute-start.5) | collective-permute-done | bytes 262176 | tf_op jit(solution)/shard_map/ppermute | solution.py:691
  15.0 0.3 %shard_map.51.rest_4_ = f32[4,320,128]{2,1,0:T(8,128)S(1)} custom-call(bf16[2,4,80,64]{3,2,1,0:T(8,128)(2,1)S(1)} %get-tuple-element.40.basis.rest_2_, bf16[4,4,8,8,128]{4,3,2,1,0:T(8,128)(2,1)S(1)} %get-tuple-element.33.rest_0_.panel, bf16[4,4,8,8,128]{4,3,2,1,0:T(8,128)(2,1)S(1)} %collective-permute-done.5.rest_0_), custom_call_target="tpu_custom_call" | custom-call | flops 20000000 | bytes 1261568 | tf_op jit(solution)/shard_map/pallas_call | solution.py:629
  15.3 0.0 collective-permute-done.4.rest_1_
  15.3 0.0 collective-permute-done.2.got_b
  15.4 0.8 %collective-permute-done.3.got_a = bf16[208,128]{1,0:T(8,128)(2,1)S(1)} collective-permute-done((bf16[208,128]{1,0:T(8,128)(2,1)S(1)}, bf16[208,128]{1,0:T(8,128)(2,1)S(1)}, u32[]{:S(2)}, u32[]{:S(2)}) %collective-permute-start.3) | collective-permute-done | bytes 53280 | tf_op jit(solution)/shard_map/ppermute | solution.py:28
  16.2 1.8 %shard_map.52 = (bf16[368,128]{1,0:T(8,128)(2,1)S(1)}, bf16[368,128]{1,0:T(8,128)(2,1)S(1)}, f32[320,128]{1,0:T(8,128)S(1)}, f32[40,128]{1,0:T(8,128)S(1)}, f32[2,4,24,128]{3,2,1,0:T(8,128)S(1)}) custom-call(bf16[208,128]{1,0:T(8,128)(2,1)S(1)} %collective-permute-done.2.got_b, bf16[208,128]{1,0:T(8,128)(2,1)S(1)} %collective-permute-done.3.got_a, ...), custom_call_target="tpu_custom_call" | custom-call | flops 1000000 | bytes 1781760 | tf_op jit(solution)/shard_map/pallas_call | solution.py:629
  17.9 0.1 collective-permute-start.6
  18.0 2.2 %collective-permute-start.7 = (bf16[368,128]{1,0:T(8,128)(2,1)S(1)}, bf16[368,128]{1,0:T(8,128)(2,1)S(1)}, u32[]{:S(2)}, u32[]{:S(2)}) collective-permute-start(bf16[368,128]{1,0:T(8,128)(2,1)S(1)} %get-tuple-element.48), channel_id=1, source_target_pairs={{2,4},{4,2},{3,5},{5,3},{10,12},{12,10},{11,13},{13,11},{18,20},{2... | collective-permute-start | bytes 282632 | tf_op jit(solution)/shard_map/ppermute | solution.py:36
  20.2 0.6 %shard_map.53 = (f32[4,20,8,128]{3,2,1,0:T(8,128)S(1)}, f32[4,20,24,128]{3,2,1,0:T(8,128)S(1)}, f32[1,192,128]{2,1,0:T(8,128)S(1)}, f32[12,64,128]{2,1,0:T(8,128)S(1)}, f32[3,64,128]{2,1,0:T(8,128)S(1)}) custom-call(f32[320,128]{1,0:T(8,128)S(1)} %get-tuple-element.46.own, f32[40,128]{1,0:T(8,128)S(1)} %get-tuple-element.49.halo, ...), custom_call_target="tpu_custom_call" | custom-call | flops 20000000 | bytes 2232320 | tf_op jit(solution)/shard_map/pallas_call | solution.py:629
  20.8 2.0 %collective-permute-done.6.from_a = bf16[368,128]{1,0:T(8,128)(2,1)S(1)} collective-permute-done((bf16[368,128]{1,0:T(8,128)(2,1)S(1)}, bf16[368,128]{1,0:T(8,128)(2,1)S(1)}, u32[]{:S(2)}, u32[]{:S(2)}) %collective-permute-start.6) | collective-permute-done | bytes 94240 | tf_op jit(solution)/shard_map/ppermute | solution.py:28
  22.8 1.9 %collective-permute-done.7.from_b = bf16[368,128]{1,0:T(8,128)(2,1)S(1)} collective-permute-done((bf16[368,128]{1,0:T(8,128)(2,1)S(1)}, bf16[368,128]{1,0:T(8,128)(2,1)S(1)}, u32[]{:S(2)}, u32[]{:S(2)}) %collective-permute-start.7) | collective-permute-done | bytes 94240 | tf_op jit(solution)/shard_map/ppermute | solution.py:36
  24.7 2.5 %shard_map.54 = f32[320,128]{1,0:T(8,128)} custom-call(f32[320,128]{1,0:T(8,128)S(1)} %get-tuple-element.46.own, bf16[368,128]{1,0:T(8,128)(2,1)S(1)} %collective-permute-done.6.from_a, bf16[368,128]{1,0:T(8,128)(2,1)S(1)} %collective-permute-done.7.from_b, f32[4,20,8,128]{3,2,1,0:T(8,128)S(1)} %get-tuple-element.52.wide, ...), custom_call_target="tpu_custom_call" | custom-call | flops 1000000 | bytes 2416640 | tf_op jit(solution)/shard_map/pallas_call | solution.py:629
  (1 shorter events, 0.0 us)
Async XLA Ops:
  0.0 6.2 %copy-start = (bf16[4,4,8,8,256]{4,3,2,1,0:T(8,128)(2,1)S(1)}, bf16[4,4,8,8,256]{4,3,2,1,0:T(8,128)(2,1)}, u32[]{:S(2)}) copy-start(bf16[4,4,8,8,256]{4,3,2,1,0:T(8,128)(2,1)} %panels.1) | copy-start | bytes 1572868
  1.1 6.7 %collective-permute-start = (bf16[352,128]{1,0:T(8,128)(2,1)S(1)}, bf16[352,128]{1,0:T(8,128)(2,1)S(1)}, u32[]{:S(2)}, u32[]{:S(2)}) collective-permute-start(bf16[352,128]{1,0:T(8,128)(2,1)S(1)} %get-tuple-element.31), channel_id=1, source_target_pairs={{0,2},{2,0},{4,6},{6,4},{1,3},{3,1},{5,7},{7,5},{8,10},{10,8},{12,... | collective-permute-start | bytes 270344 | tf_op jit(solution)/shard_map/ppermute | solution.py:28
  1.6 7.1 %collective-permute-start.1 = (bf16[352,128]{1,0:T(8,128)(2,1)S(1)}, bf16[352,128]{1,0:T(8,128)(2,1)S(1)}, u32[]{:S(2)}, u32[]{:S(2)}) collective-permute-start(bf16[352,128]{1,0:T(8,128)(2,1)S(1)} %get-tuple-element.32), channel_id=1, source_target_pairs={{2,4},{4,2},{3,5},{5,3},{10,12},{12,10},{11,13},{13,11},{18,20},{2... | collective-permute-start | bytes 270344 | tf_op jit(solution)/shard_map/ppermute | solution.py:36
  6.2 0.7 %copy-start.1 = (bf16[4,16,10]{1,0,2:T(4,128)(2,1)S(1)}, bf16[4,16,10]{1,0,2:T(4,128)(2,1)}, u32[]{:S(2)}) copy-start(bf16[4,16,10]{1,0,2:T(4,128)(2,1)} %param.5) | copy-start | bytes 3844
  6.3 8.7 %collective-permute-start.5 = (bf16[4,4,8,8,128]{4,3,2,1,0:T(8,128)(2,1)S(1)}, bf16[4,4,8,8,128]{4,3,2,1,0:T(8,128)(2,1)S(1)}, u32[]{:S(2)}, u32[]{:S(2)}) collective-permute-start(bf16[4,4,8,8,128]{4,3,2,1,0:T(8,128)(2,1)S(1)} %get-tuple-element.34.rest_1_), channel_id=1, source_target_pairs={{0,1},{1,0},{2,3},{3,2},{4,5},{5,4},{6,7},{7,6},{8,9},{9,8},{10,11... | collective-permute-start | bytes 786440 | tf_op jit(solution)/shard_map/ppermute | solution.py:691
  9.0 6.4 %collective-permute-start.2 = (bf16[208,128]{1,0:T(8,128)(2,1)S(1)}, bf16[208,128]{1,0:T(8,128)(2,1)S(1)}, u32[]{:S(2)}, u32[]{:S(2)}) collective-permute-start(bf16[208,128]{1,0:T(8,128)(2,1)S(1)} %get-tuple-element.38), channel_id=1, source_target_pairs={{1,8},{9,16},{17,24},{25,0},{8,1},{16,9},{24,17},{0,25},{3,10},{11... | collective-permute-start | bytes 159752 | tf_op jit(solution)/shard_map/ppermute | solution.py:36
  9.1 7.1 %collective-permute-start.3 = (bf16[208,128]{1,0:T(8,128)(2,1)S(1)}, bf16[208,128]{1,0:T(8,128)(2,1)S(1)}, u32[]{:S(2)}, u32[]{:S(2)}) collective-permute-start(bf16[208,128]{1,0:T(8,128)(2,1)S(1)} %get-tuple-element.39), channel_id=1, source_target_pairs={{0,1},{1,0},{8,9},{9,8},{16,17},{17,16},{24,25},{25,24},{2,3},{3,2... | collective-permute-start | bytes 159752 | tf_op jit(solution)/shard_map/ppermute | solution.py:28
  10.3 5.0 %collective-permute-start.4 = (bf16[64,128]{1,0:T(8,128)(2,1)S(1)}, bf16[64,128]{1,0:T(8,128)(2,1)S(1)}, u32[]{:S(2)}, u32[]{:S(2)}) collective-permute-start(bf16[64,128]{1,0:T(8,128)(2,1)S(1)} %select_bitcast_fusion), channel_id=1, source_target_pairs={{0,8},{8,16},{16,24},{24,0},{1,25},{9,1},{17,9},{25,17},{2,10},{10... | collective-permute-start | bytes 49160 | tf_op jit(solution)/shard_map/ppermute | solution.py:699
  17.9 4.9 %collective-permute-start.6 = (bf16[368,128]{1,0:T(8,128)(2,1)S(1)}, bf16[368,128]{1,0:T(8,128)(2,1)S(1)}, u32[]{:S(2)}, u32[]{:S(2)}) collective-permute-start(bf16[368,128]{1,0:T(8,128)(2,1)S(1)} %get-tuple-element.47), channel_id=1, source_target_pairs={{0,2},{2,0},{4,6},{6,4},{1,3},{3,1},{5,7},{7,5},{8,10},{10,8},{12,... | collective-permute-start | bytes 282632 | tf_op jit(solution)/shard_map/ppermute | solution.py:28
  18.0 6.7 %collective-permute-start.7 = (bf16[368,128]{1,0:T(8,128)(2,1)S(1)}, bf16[368,128]{1,0:T(8,128)(2,1)S(1)}, u32[]{:S(2)}, u32[]{:S(2)}) collective-permute-start(bf16[368,128]{1,0:T(8,128)(2,1)S(1)} %get-tuple-element.48), channel_id=1, source_target_pairs={{2,4},{4,2},{3,5},{5,3},{10,12},{12,10},{11,13},{13,11},{18,20},{2... | collective-permute-start | bytes 282632 | tf_op jit(solution)/shard_map/ppermute | solution.py:36

commit v8 on v7

--- a/solution.py
+++ b/solution.py
@@ -451,10 +451,6 @@
                 if k < 3:
                     mine = time_step * mine
                 coeff_strip[side, k, at, :] = jnp.where(mask, mine, coeff_own[side, k, at, :])
-    strip_coefficients(coeff_strip, wide_strip, eofs)
-    read, write, coeff = strip_rows(strip, adj_strip, wide_strip)
-    diffuse(read, write, coeff, 3, first, second, True)
-
     count, depth = basis.shape[0], basis.shape[3]
     if len(panel_parts) == 2:
         edges, far = panel_parts
@@ -480,6 +476,10 @@
         halo = jnp.where(wide_lane // SLOT == f, total, halo)
     proj_strip[pl.ds(0, eofs * SUB), :] = halo[:, :LANES]
     proj_strip[pl.ds(eofs * SUB, eofs * SUB), :] = halo[:, LANES:]
+
+    strip_coefficients(coeff_strip, wide_strip, eofs)
+    read, write, coeff = strip_rows(strip, adj_strip, wide_strip)
+    diffuse(read, write, coeff, 3, first, second, True)
 
     scores = [jnp.zeros((SUB, LANES), jnp.float32) for _ in range(members)]
     for e in range(eofs):

time: 27.4 us -> 27.4 us (level)
  no operation moved by 1% of the time
where the time goes in v8:
time: 27.4 us; the launch traced here: 27.2 us
  starting transfers between devices  11 us (40%)
  Pallas kernels  7.85 us (29%)
  waiting for transfers between devices  7.1 us (26%)
  other arithmetic  1.01 us (4%)
    pallas_call x9, Pallas kernels, call(): pl.pallas_call(kernel, in_specs=[whole] * len(args), out_specs=[pl.BlockS...  7.85 us
    ppermute x3, starting transfers between devices, swap_b(): return lax.ppermute(values, axes, pairs + [(j, i) for i, j in pairs])  6.87 us
    ppermute x3, waiting for transfers between devices, swap_b(): return lax.ppermute(values, axes, pairs + [(j, i) for i, j in pairs])  2.84 us
    ppermute x3, waiting for transfers between devices, swap_a(): return lax.ppermute(values, axes, [(i, i ^ 1) for i in range(count)])  2.81 us
    ppermute x3, starting transfers between devices, swap_a(): return lax.ppermute(values, axes, [(i, i ^ 1) for i in range(count)])  1.84 us
    ppermute x1, starting transfers between devices, per_device(): lax.ppermute(jnp.where(me == 1, edges[1, 0], edges[1, 1]), RING, pairs)  1.71 us
    ppermute x1, waiting for transfers between devices, per_device(): lax.ppermute(tiles[s], 'gz', [(i, (i + s) % count) for i in range(count)])  1.45 us
    concatenate x1, other arithmetic, per_device(): jnp.concatenate([control.reshape(rows, col_count), coefficients.reshape(4...  1 us
  transfers between devices with their start and end apart: 8, of which 5 were waited for; matrix products, arithmetic and copies ran while one was open for 0% of the time, Pallas kernels for 13%

profile of v8, /device:TPU:10, one launch (start us, length us, event | category | flops | bytes accessed | tf_op | source)
XLA Modules:
  0.0 27.2 jit_solution(8431143514613398971)
XLA Ops:
  0.0 0.0 copy-start
  0.0 1.0 %pad_maximum_fusion.own = f32[352,128]{1,0:T(8,128)S(1)} fusion(f32[32,128]{1,0:T(8,128)} %bitcast.6, f32[320,128]{1,0:T(8,128)} %bitcast.5), kind=kLoop, calls=%fused_computation | loop fusion | flops 45056 | bytes 360448 | tf_op jit(solution)/shard_map/concatenate | solution.py:670
  1.0 0.1 shard_map.46
  1.1 0.5 %collective-permute-start = (bf16[352,128]{1,0:T(8,128)(2,1)S(1)}, bf16[352,128]{1,0:T(8,128)(2,1)S(1)}, u32[]{:S(2)}, u32[]{:S(2)}) collective-permute-start(bf16[352,128]{1,0:T(8,128)(2,1)S(1)} %get-tuple-element.31), channel_id=1, source_target_pairs={{0,2},{2,0},{4,6},{6,4},{1,3},{3,1},{5,7},{7,5},{8,10},{10,8},{12,... | collective-permute-start | bytes 270344 | tf_op jit(solution)/shard_map/ppermute | solution.py:28
  1.6 4.6 %collective-permute-start.1 = (bf16[352,128]{1,0:T(8,128)(2,1)S(1)}, bf16[352,128]{1,0:T(8,128)(2,1)S(1)}, u32[]{:S(2)}, u32[]{:S(2)}) collective-permute-start(bf16[352,128]{1,0:T(8,128)(2,1)S(1)} %get-tuple-element.32), channel_id=1, source_target_pairs={{2,4},{4,2},{3,5},{5,3},{10,12},{12,10},{11,13},{13,11},{18,20},{2... | collective-permute-start | bytes 270344 | tf_op jit(solution)/shard_map/ppermute | solution.py:36
  6.2 0.0 copy-done
  6.2 0.0 copy-start.1
  6.2 0.1 shard_map.47
  6.3 0.6 %collective-permute-start.5 = (bf16[4,4,8,8,128]{4,3,2,1,0:T(8,128)(2,1)S(1)}, bf16[4,4,8,8,128]{4,3,2,1,0:T(8,128)(2,1)S(1)}, u32[]{:S(2)}, u32[]{:S(2)}) collective-permute-start(bf16[4,4,8,8,128]{4,3,2,1,0:T(8,128)(2,1)S(1)} %get-tuple-element.34.rest_1_), channel_id=1, source_target_pairs={{0,1},{1,0},{2,3},{3,2},{4,5},{5,4},{6,7},{7,6},{8,9},{9,8},{10,11... | collective-permute-start | bytes 786440 | tf_op jit(solution)/shard_map/ppermute | solution.py:691
  6.9 0.0 copy-done.1
  6.9 0.1 copy.5.eof_basis
  7.1 0.7 %shard_map.48 = (bf16[48,128]{1,0:T(8,128)(2,1)S(1)}, bf16[48,128]{1,0:T(8,128)(2,1)S(1)}, bf16[2,2,64,128]{3,2,1,0:T(8,128)(2,1)S(1)}, bf16[2,4,80,64]{3,2,1,0:T(8,128)(2,1)S(1)}) custom-call(f32[352,128]{1,0:T(8,128)S(1)} %pad_maximum_fusion.own, bf16[4,16,10]{2,1,0:T(8,128)(2,1)S(1)} %copy.5.eof_basis, ...), custom_call_target="tpu_custom_call" | custom-call | flops 1000000 | bytes 877824 | tf_op jit(solution)/shard_map/pallas_call | solution.py:629
  7.8 0.0 collective-permute-done.from_a
  7.8 0.9 %collective-permute-done.1.from_b = bf16[352,128]{1,0:T(8,128)(2,1)S(1)} collective-permute-done((bf16[352,128]{1,0:T(8,128)(2,1)S(1)}, bf16[352,128]{1,0:T(8,128)(2,1)S(1)}, u32[]{:S(2)}, u32[]{:S(2)}) %collective-permute-start.1) | collective-permute-done | bytes 90144 | tf_op jit(solution)/shard_map/ppermute | solution.py:36
  8.7 0.3 %shard_map.49 = (bf16[208,128]{1,0:T(8,128)(2,1)S(1)}, bf16[208,128]{1,0:T(8,128)(2,1)S(1)}, f32[352,128]{1,0:T(8,128)S(1)}, f32[352,128]{1,0:T(8,128)S(1)}) custom-call(bf16[352,128]{1,0:T(8,128)(2,1)S(1)} %collective-permute-done.from_a, bf16[352,128]{1,0:T(8,128)(2,1)S(1)} %collective-permute-done.1.from_b, bf16[48,128]{1,0:T(8,128)(2,1)S(1)} %get-tuple-element.35.west, ...), custom_call_target="tpu_custom_call" | custom-call | flops 1000000 | bytes 737280 | tf_op jit(solution)/shard_map/pallas_call | solution.py:629
  9.0 0.1 collective-permute-start.2
  9.1 1.3 %collective-permute-start.3 = (bf16[208,128]{1,0:T(8,128)(2,1)S(1)}, bf16[208,128]{1,0:T(8,128)(2,1)S(1)}, u32[]{:S(2)}, u32[]{:S(2)}) collective-permute-start(bf16[208,128]{1,0:T(8,128)(2,1)S(1)} %get-tuple-element.39), channel_id=1, source_target_pairs={{0,1},{1,0},{8,9},{9,8},{16,17},{17,16},{24,25},{25,24},{2,3},{3,2... | collective-permute-start | bytes 159752 | tf_op jit(solution)/shard_map/ppermute | solution.py:28
  10.3 1.7 %collective-permute-start.4 = (bf16[64,128]{1,0:T(8,128)(2,1)S(1)}, bf16[64,128]{1,0:T(8,128)(2,1)S(1)}, u32[]{:S(2)}, u32[]{:S(2)}) collective-permute-start(bf16[64,128]{1,0:T(8,128)(2,1)S(1)} %select_bitcast_fusion), channel_id=1, source_target_pairs={{0,8},{8,16},{16,24},{24,0},{1,25},{9,1},{17,9},{25,17},{2,10},{10... | collective-permute-start | bytes 49160 | tf_op jit(solution)/shard_map/ppermute | solution.py:699
  12.0 1.5 %shard_map.50 = (f32[320,128]{1,0:T(8,128)S(1)}, f32[3,80,128]{2,1,0:T(8,128)S(1)}, f32[4,24,128]{2,1,0:T(8,128)S(1)}, f32[2,4,24,128]{3,2,1,0:T(8,128)S(1)}) custom-call(f32[352,128]{1,0:T(8,128)S(1)} %pad_maximum_fusion.own, f32[352,128]{1,0:T(8,128)S(1)} %get-tuple-element.41.north, f32[352,128]{1,0:T(8,128)S(1)} %get-tuple-element.42.south), custom_call_target="tpu_custom_call" | custom-call | flops 20000000 | bytes 974848 | tf_op jit(solution)/shard_map/pallas_call | solution.py:629
  13.6 1.4 %collective-permute-done.5.rest_0_ = bf16[4,4,8,8,128]{4,3,2,1,0:T(8,128)(2,1)S(1)} collective-permute-done((bf16[4,4,8,8,128]{4,3,2,1,0:T(8,128)(2,1)S(1)}, bf16[4,4,8,8,128]{4,3,2,1,0:T(8,128)(2,1)S(1)}, u32[]{:S(2)}, u32[]{:S(2)}) %collective-permute-start.5) | collective-permute-done | bytes 262176 | tf_op jit(solution)/shard_map/ppermute | solution.py:691
  15.0 0.3 %shard_map.51.rest_4_ = f32[4,320,128]{2,1,0:T(8,128)S(1)} custom-call(bf16[2,4,80,64]{3,2,1,0:T(8,128)(2,1)S(1)} %get-tuple-element.40.basis.rest_2_, bf16[4,4,8,8,128]{4,3,2,1,0:T(8,128)(2,1)S(1)} %get-tuple-element.33.rest_0_.panel, bf16[4,4,8,8,128]{4,3,2,1,0:T(8,128)(2,1)S(1)} %collective-permute-done.5.rest_0_), custom_call_target="tpu_custom_call" | custom-call | flops 20000000 | bytes 1261568 | tf_op jit(solution)/shard_map/pallas_call | solution.py:629
  15.3 0.0 collective-permute-done.4.rest_1_
  15.3 0.0 collective-permute-done.2.got_b
  15.4 0.8 %collective-permute-done.3.got_a = bf16[208,128]{1,0:T(8,128)(2,1)S(1)} collective-permute-done((bf16[208,128]{1,0:T(8,128)(2,1)S(1)}, bf16[208,128]{1,0:T(8,128)(2,1)S(1)}, u32[]{:S(2)}, u32[]{:S(2)}) %collective-permute-start.3) | collective-permute-done | bytes 53280 | tf_op jit(solution)/shard_map/ppermute | solution.py:28
  16.2 1.8 %shard_map.52 = (bf16[368,128]{1,0:T(8,128)(2,1)S(1)}, bf16[368,128]{1,0:T(8,128)(2,1)S(1)}, f32[320,128]{1,0:T(8,128)S(1)}, f32[40,128]{1,0:T(8,128)S(1)}, f32[2,4,24,128]{3,2,1,0:T(8,128)S(1)}) custom-call(bf16[208,128]{1,0:T(8,128)(2,1)S(1)} %collective-permute-done.2.got_b, bf16[208,128]{1,0:T(8,128)(2,1)S(1)} %collective-permute-done.3.got_a, ...), custom_call_target="tpu_custom_call" | custom-call | flops 1000000 | bytes 1781760 | tf_op jit(solution)/shard_map/pallas_call | solution.py:629
  17.9 0.1 collective-permute-start.6
  18.0 2.2 %collective-permute-start.7 = (bf16[368,128]{1,0:T(8,128)(2,1)S(1)}, bf16[368,128]{1,0:T(8,128)(2,1)S(1)}, u32[]{:S(2)}, u32[]{:S(2)}) collective-permute-start(bf16[368,128]{1,0:T(8,128)(2,1)S(1)} %get-tuple-element.48), channel_id=1, source_target_pairs={{2,4},{4,2},{3,5},{5,3},{10,12},{12,10},{11,13},{13,11},{18,20},{2... | collective-permute-start | bytes 282632 | tf_op jit(solution)/shard_map/ppermute | solution.py:36
  20.2 0.6 %shard_map.53 = (f32[4,20,8,128]{3,2,1,0:T(8,128)S(1)}, f32[4,20,24,128]{3,2,1,0:T(8,128)S(1)}, f32[1,192,128]{2,1,0:T(8,128)S(1)}, f32[12,64,128]{2,1,0:T(8,128)S(1)}, f32[3,64,128]{2,1,0:T(8,128)S(1)}) custom-call(f32[320,128]{1,0:T(8,128)S(1)} %get-tuple-element.46.own, f32[40,128]{1,0:T(8,128)S(1)} %get-tuple-element.49.halo, ...), custom_call_target="tpu_custom_call" | custom-call | flops 20000000 | bytes 2232320 | tf_op jit(solution)/shard_map/pallas_call | solution.py:629
  20.8 2.0 %collective-permute-done.6.from_a = bf16[368,128]{1,0:T(8,128)(2,1)S(1)} collective-permute-done((bf16[368,128]{1,0:T(8,128)(2,1)S(1)}, bf16[368,128]{1,0:T(8,128)(2,1)S(1)}, u32[]{:S(2)}, u32[]{:S(2)}) %collective-permute-start.6) | collective-permute-done | bytes 94240 | tf_op jit(solution)/shard_map/ppermute | solution.py:28
  22.8 1.9 %collective-permute-done.7.from_b = bf16[368,128]{1,0:T(8,128)(2,1)S(1)} collective-permute-done((bf16[368,128]{1,0:T(8,128)(2,1)S(1)}, bf16[368,128]{1,0:T(8,128)(2,1)S(1)}, u32[]{:S(2)}, u32[]{:S(2)}) %collective-permute-start.7) | collective-permute-done | bytes 94240 | tf_op jit(solution)/shard_map/ppermute | solution.py:36
  24.7 2.5 %shard_map.54 = f32[320,128]{1,0:T(8,128)} custom-call(f32[320,128]{1,0:T(8,128)S(1)} %get-tuple-element.46.own, bf16[368,128]{1,0:T(8,128)(2,1)S(1)} %collective-permute-done.6.from_a, bf16[368,128]{1,0:T(8,128)(2,1)S(1)} %collective-permute-done.7.from_b, f32[4,20,8,128]{3,2,1,0:T(8,128)S(1)} %get-tuple-element.52.wide, ...), custom_call_target="tpu_custom_call" | custom-call | flops 1000000 | bytes 2416640 | tf_op jit(solution)/shard_map/pallas_call | solution.py:629
  (1 shorter events, 0.0 us)
Async XLA Ops:
  0.0 6.2 %copy-start = (bf16[4,4,8,8,256]{4,3,2,1,0:T(8,128)(2,1)S(1)}, bf16[4,4,8,8,256]{4,3,2,1,0:T(8,128)(2,1)}, u32[]{:S(2)}) copy-start(bf16[4,4,8,8,256]{4,3,2,1,0:T(8,128)(2,1)} %panels.1) | copy-start | bytes 1572868
  1.1 6.7 %collective-permute-start = (bf16[352,128]{1,0:T(8,128)(2,1)S(1)}, bf16[352,128]{1,0:T(8,128)(2,1)S(1)}, u32[]{:S(2)}, u32[]{:S(2)}) collective-permute-start(bf16[352,128]{1,0:T(8,128)(2,1)S(1)} %get-tuple-element.31), channel_id=1, source_target_pairs={{0,2},{2,0},{4,6},{6,4},{1,3},{3,1},{5,7},{7,5},{8,10},{10,8},{12,... | collective-permute-start | bytes 270344 | tf_op jit(solution)/shard_map/ppermute | solution.py:28
  1.6 7.1 %collective-permute-start.1 = (bf16[352,128]{1,0:T(8,128)(2,1)S(1)}, bf16[352,128]{1,0:T(8,128)(2,1)S(1)}, u32[]{:S(2)}, u32[]{:S(2)}) collective-permute-start(bf16[352,128]{1,0:T(8,128)(2,1)S(1)} %get-tuple-element.32), channel_id=1, source_target_pairs={{2,4},{4,2},{3,5},{5,3},{10,12},{12,10},{11,13},{13,11},{18,20},{2... | collective-permute-start | bytes 270344 | tf_op jit(solution)/shard_map/ppermute | solution.py:36
  6.2 0.7 %copy-start.1 = (bf16[4,16,10]{1,0,2:T(4,128)(2,1)S(1)}, bf16[4,16,10]{1,0,2:T(4,128)(2,1)}, u32[]{:S(2)}) copy-start(bf16[4,16,10]{1,0,2:T(4,128)(2,1)} %param.5) | copy-start | bytes 3844
  6.3 8.7 %collective-permute-start.5 = (bf16[4,4,8,8,128]{4,3,2,1,0:T(8,128)(2,1)S(1)}, bf16[4,4,8,8,128]{4,3,2,1,0:T(8,128)(2,1)S(1)}, u32[]{:S(2)}, u32[]{:S(2)}) collective-permute-start(bf16[4,4,8,8,128]{4,3,2,1,0:T(8,128)(2,1)S(1)} %get-tuple-element.34.rest_1_), channel_id=1, source_target_pairs={{0,1},{1,0},{2,3},{3,2},{4,5},{5,4},{6,7},{7,6},{8,9},{9,8},{10,11... | collective-permute-start | bytes 786440 | tf_op jit(solution)/shard_map/ppermute | solution.py:691
  9.0 6.4 %collective-permute-start.2 = (bf16[208,128]{1,0:T(8,128)(2,1)S(1)}, bf16[208,128]{1,0:T(8,128)(2,1)S(1)}, u32[]{:S(2)}, u32[]{:S(2)}) collective-permute-start(bf16[208,128]{1,0:T(8,128)(2,1)S(1)} %get-tuple-element.38), channel_id=1, source_target_pairs={{1,8},{9,16},{17,24},{25,0},{8,1},{16,9},{24,17},{0,25},{3,10},{11... | collective-permute-start | bytes 159752 | tf_op jit(solution)/shard_map/ppermute | solution.py:36
  9.1 7.1 %collective-permute-start.3 = (bf16[208,128]{1,0:T(8,128)(2,1)S(1)}, bf16[208,128]{1,0:T(8,128)(2,1)S(1)}, u32[]{:S(2)}, u32[]{:S(2)}) collective-permute-start(bf16[208,128]{1,0:T(8,128)(2,1)S(1)} %get-tuple-element.39), channel_id=1, source_target_pairs={{0,1},{1,0},{8,9},{9,8},{16,17},{17,16},{24,25},{25,24},{2,3},{3,2... | collective-permute-start | bytes 159752 | tf_op jit(solution)/shard_map/ppermute | solution.py:28
  10.3 5.0 %collective-permute-start.4 = (bf16[64,128]{1,0:T(8,128)(2,1)S(1)}, bf16[64,128]{1,0:T(8,128)(2,1)S(1)}, u32[]{:S(2)}, u32[]{:S(2)}) collective-permute-start(bf16[64,128]{1,0:T(8,128)(2,1)S(1)} %select_bitcast_fusion), channel_id=1, source_target_pairs={{0,8},{8,16},{16,24},{24,0},{1,25},{9,1},{17,9},{25,17},{2,10},{10... | collective-permute-start | bytes 49160 | tf_op jit(solution)/shard_map/ppermute | solution.py:699
  17.9 4.9 %collective-permute-start.6 = (bf16[368,128]{1,0:T(8,128)(2,1)S(1)}, bf16[368,128]{1,0:T(8,128)(2,1)S(1)}, u32[]{:S(2)}, u32[]{:S(2)}) collective-permute-start(bf16[368,128]{1,0:T(8,128)(2,1)S(1)} %get-tuple-element.47), channel_id=1, source_target_pairs={{0,2},{2,0},{4,6},{6,4},{1,3},{3,1},{5,7},{7,5},{8,10},{10,8},{12,... | collective-permute-start | bytes 282632 | tf_op jit(solution)/shard_map/ppermute | solution.py:28
  18.0 6.7 %collective-permute-start.7 = (bf16[368,128]{1,0:T(8,128)(2,1)S(1)}, bf16[368,128]{1,0:T(8,128)(2,1)S(1)}, u32[]{:S(2)}, u32[]{:S(2)}) collective-permute-start(bf16[368,128]{1,0:T(8,128)(2,1)S(1)} %get-tuple-element.48), channel_id=1, source_target_pairs={{2,4},{4,2},{3,5},{5,3},{10,12},{12,10},{11,13},{13,11},{18,20},{2... | collective-permute-start | bytes 282632 | tf_op jit(solution)/shard_map/ppermute | solution.py:36

commit v9 on v8

--- a/solution.py
+++ b/solution.py
@@ -481,15 +481,15 @@
     read, write, coeff = strip_rows(strip, adj_strip, wide_strip)
     diffuse(read, write, coeff, 3, first, second, True)
 
-    scores = [jnp.zeros((SUB, LANES), jnp.float32) for _ in range(members)]
+    scores = [[jnp.zeros((SUB, LANES), jnp.float32)] * 2 for _ in range(members)]
     for e in range(eofs):
         edges = both_edges(eofs, adj_strip, e, inner)
         for f in range(fields):
             at = pl.ds((f * eofs + e) * SUB, SUB)
             cells = jnp.where(own_edge(lane), turn(edges, -f * SLOT - HALO), adj[at, :])
             for m in range(members):
-                scores[m] = scores[m] + proj[m, at, :] * cells
-    scores = [s / (members - 1) for s in scores]
+                scores[m][f % 2] = scores[m][f % 2] + proj[m, at, :] * cells
+    scores = [(even + odd_sum) / (members - 1) for even, odd_sum in scores]
     tiles = []
     for i in range(fields * eofs):
         at = pl.ds(i * SUB, SUB)

time: 27.4 us -> 27.4 us (level)
  no operation moved by 1% of the time
where the time goes in v9:
time: 27.4 us; the launch traced here: 27.2 us
  starting transfers between devices  11 us (40%)
  Pallas kernels  7.85 us (29%)
  waiting for transfers between devices  7.1 us (26%)
  other arithmetic  1.01 us (4%)
    pallas_call x9, Pallas kernels, call(): pl.pallas_call(kernel, in_specs=[whole] * len(args), out_specs=[pl.BlockS...  7.85 us
    ppermute x3, starting transfers between devices, swap_b(): return lax.ppermute(values, axes, pairs + [(j, i) for i, j in pairs])  6.87 us
    ppermute x3, waiting for transfers between devices, swap_b(): return lax.ppermute(values, axes, pairs + [(j, i) for i, j in pairs])  2.84 us
    ppermute x3, waiting for transfers between devices, swap_a(): return lax.ppermute(values, axes, [(i, i ^ 1) for i in range(count)])  2.81 us
    ppermute x3, starting transfers between devices, swap_a(): return lax.ppermute(values, axes, [(i, i ^ 1) for i in range(count)])  1.84 us
    ppermute x1, starting transfers between devices, per_device(): lax.ppermute(jnp.where(me == 1, edges[1, 0], edges[1, 1]), RING, pairs)  1.71 us
    ppermute x1, waiting for transfers between devices, per_device(): lax.ppermute(tiles[s], 'gz', [(i, (i + s) % count) for i in range(count)])  1.45 us
    concatenate x1, other arithmetic, per_device(): jnp.concatenate([control.reshape(rows, col_count), coefficients.reshape(4...  1 us
  transfers between devices with their start and end apart: 8, of which 5 were waited for; matrix products, arithmetic and copies ran while one was open for 0% of the time, Pallas kernels for 13%

profile of v9, /device:TPU:10, one launch (start us, length us, event | category | flops | bytes accessed | tf_op | source)
XLA Modules:
  0.0 27.2 jit_solution(3529379668942156849)
XLA Ops:
  0.0 0.0 copy-start
  0.0 1.0 %pad_maximum_fusion.own = f32[352,128]{1,0:T(8,128)S(1)} fusion(f32[32,128]{1,0:T(8,128)} %bitcast.6, f32[320,128]{1,0:T(8,128)} %bitcast.5), kind=kLoop, calls=%fused_computation | loop fusion | flops 45056 | bytes 360448 | tf_op jit(solution)/shard_map/concatenate | solution.py:670
  1.0 0.1 shard_map.46
  1.1 0.5 %collective-permute-start = (bf16[352,128]{1,0:T(8,128)(2,1)S(1)}, bf16[352,128]{1,0:T(8,128)(2,1)S(1)}, u32[]{:S(2)}, u32[]{:S(2)}) collective-permute-start(bf16[352,128]{1,0:T(8,128)(2,1)S(1)} %get-tuple-element.31), channel_id=1, source_target_pairs={{0,2},{2,0},{4,6},{6,4},{1,3},{3,1},{5,7},{7,5},{8,10},{10,8},{12,... | collective-permute-start | bytes 270344 | tf_op jit(solution)/shard_map/ppermute | solution.py:28
  1.6 4.6 %collective-permute-start.1 = (bf16[352,128]{1,0:T(8,128)(2,1)S(1)}, bf16[352,128]{1,0:T(8,128)(2,1)S(1)}, u32[]{:S(2)}, u32[]{:S(2)}) collective-permute-start(bf16[352,128]{1,0:T(8,128)(2,1)S(1)} %get-tuple-element.32), channel_id=1, source_target_pairs={{2,4},{4,2},{3,5},{5,3},{10,12},{12,10},{11,13},{13,11},{18,20},{2... | collective-permute-start | bytes 270344 | tf_op jit(solution)/shard_map/ppermute | solution.py:36
  6.2 0.0 copy-done
  6.2 0.0 copy-start.1
  6.2 0.1 shard_map.47
  6.3 0.6 %collective-permute-start.5 = (bf16[4,4,8,8,128]{4,3,2,1,0:T(8,128)(2,1)S(1)}, bf16[4,4,8,8,128]{4,3,2,1,0:T(8,128)(2,1)S(1)}, u32[]{:S(2)}, u32[]{:S(2)}) collective-permute-start(bf16[4,4,8,8,128]{4,3,2,1,0:T(8,128)(2,1)S(1)} %get-tuple-element.34.rest_1_), channel_id=1, source_target_pairs={{0,1},{1,0},{2,3},{3,2},{4,5},{5,4},{6,7},{7,6},{8,9},{9,8},{10,11... | collective-permute-start | bytes 786440 | tf_op jit(solution)/shard_map/ppermute | solution.py:691
  6.9 0.0 copy-done.1
  6.9 0.1 copy.5.eof_basis
  7.1 0.7 %shard_map.48 = (bf16[48,128]{1,0:T(8,128)(2,1)S(1)}, bf16[48,128]{1,0:T(8,128)(2,1)S(1)}, bf16[2,2,64,128]{3,2,1,0:T(8,128)(2,1)S(1)}, bf16[2,4,80,64]{3,2,1,0:T(8,128)(2,1)S(1)}) custom-call(f32[352,128]{1,0:T(8,128)S(1)} %pad_maximum_fusion.own, bf16[4,16,10]{2,1,0:T(8,128)(2,1)S(1)} %copy.5.eof_basis, ...), custom_call_target="tpu_custom_call" | custom-call | flops 1000000 | bytes 877824 | tf_op jit(solution)/shard_map/pallas_call | solution.py:629
  7.8 0.0 collective-permute-done.from_a
  7.8 0.9 %collective-permute-done.1.from_b = bf16[352,128]{1,0:T(8,128)(2,1)S(1)} collective-permute-done((bf16[352,128]{1,0:T(8,128)(2,1)S(1)}, bf16[352,128]{1,0:T(8,128)(2,1)S(1)}, u32[]{:S(2)}, u32[]{:S(2)}) %collective-permute-start.1) | collective-permute-done | bytes 90144 | tf_op jit(solution)/shard_map/ppermute | solution.py:36
  8.7 0.3 %shard_map.49 = (bf16[208,128]{1,0:T(8,128)(2,1)S(1)}, bf16[208,128]{1,0:T(8,128)(2,1)S(1)}, f32[352,128]{1,0:T(8,128)S(1)}, f32[352,128]{1,0:T(8,128)S(1)}) custom-call(bf16[352,128]{1,0:T(8,128)(2,1)S(1)} %collective-permute-done.from_a, bf16[352,128]{1,0:T(8,128)(2,1)S(1)} %collective-permute-done.1.from_b, bf16[48,128]{1,0:T(8,128)(2,1)S(1)} %get-tuple-element.35.west, ...), custom_call_target="tpu_custom_call" | custom-call | flops 1000000 | bytes 737280 | tf_op jit(solution)/shard_map/pallas_call | solution.py:629
  9.0 0.1 collective-permute-start.2
  9.1 1.3 %collective-permute-start.3 = (bf16[208,128]{1,0:T(8,128)(2,1)S(1)}, bf16[208,128]{1,0:T(8,128)(2,1)S(1)}, u32[]{:S(2)}, u32[]{:S(2)}) collective-permute-start(bf16[208,128]{1,0:T(8,128)(2,1)S(1)} %get-tuple-element.39), channel_id=1, source_target_pairs={{0,1},{1,0},{8,9},{9,8},{16,17},{17,16},{24,25},{25,24},{2,3},{3,2... | collective-permute-start | bytes 159752 | tf_op jit(solution)/shard_map/ppermute | solution.py:28
  10.3 1.7 %collective-permute-start.4 = (bf16[64,128]{1,0:T(8,128)(2,1)S(1)}, bf16[64,128]{1,0:T(8,128)(2,1)S(1)}, u32[]{:S(2)}, u32[]{:S(2)}) collective-permute-start(bf16[64,128]{1,0:T(8,128)(2,1)S(1)} %select_bitcast_fusion), channel_id=1, source_target_pairs={{0,8},{8,16},{16,24},{24,0},{1,25},{9,1},{17,9},{25,17},{2,10},{10... | collective-permute-start | bytes 49160 | tf_op jit(solution)/shard_map/ppermute | solution.py:699
  12.0 1.5 %shard_map.50 = (f32[320,128]{1,0:T(8,128)S(1)}, f32[3,80,128]{2,1,0:T(8,128)S(1)}, f32[4,24,128]{2,1,0:T(8,128)S(1)}, f32[2,4,24,128]{3,2,1,0:T(8,128)S(1)}) custom-call(f32[352,128]{1,0:T(8,128)S(1)} %pad_maximum_fusion.own, f32[352,128]{1,0:T(8,128)S(1)} %get-tuple-element.41.north, f32[352,128]{1,0:T(8,128)S(1)} %get-tuple-element.42.south), custom_call_target="tpu_custom_call" | custom-call | flops 20000000 | bytes 974848 | tf_op jit(solution)/shard_map/pallas_call | solution.py:629
  13.6 1.4 %collective-permute-done.5.rest_0_ = bf16[4,4,8,8,128]{4,3,2,1,0:T(8,128)(2,1)S(1)} collective-permute-done((bf16[4,4,8,8,128]{4,3,2,1,0:T(8,128)(2,1)S(1)}, bf16[4,4,8,8,128]{4,3,2,1,0:T(8,128)(2,1)S(1)}, u32[]{:S(2)}, u32[]{:S(2)}) %collective-permute-start.5) | collective-permute-done | bytes 262176 | tf_op jit(solution)/shard_map/ppermute | solution.py:691
  15.0 0.3 %shard_map.51.rest_4_ = f32[4,320,128]{2,1,0:T(8,128)S(1)} custom-call(bf16[2,4,80,64]{3,2,1,0:T(8,128)(2,1)S(1)} %get-tuple-element.40.basis.rest_2_, bf16[4,4,8,8,128]{4,3,2,1,0:T(8,128)(2,1)S(1)} %get-tuple-element.33.rest_0_.panel, bf16[4,4,8,8,128]{4,3,2,1,0:T(8,128)(2,1)S(1)} %collective-permute-done.5.rest_0_), custom_call_target="tpu_custom_call" | custom-call | flops 20000000 | bytes 1261568 | tf_op jit(solution)/shard_map/pallas_call | solution.py:629
  15.3 0.0 collective-permute-done.4.rest_1_
  15.3 0.0 collective-permute-done.2.got_b
  15.4 0.8 %collective-permute-done.3.got_a = bf16[208,128]{1,0:T(8,128)(2,1)S(1)} collective-permute-done((bf16[208,128]{1,0:T(8,128)(2,1)S(1)}, bf16[208,128]{1,0:T(8,128)(2,1)S(1)}, u32[]{:S(2)}, u32[]{:S(2)}) %collective-permute-start.3) | collective-permute-done | bytes 53280 | tf_op jit(solution)/shard_map/ppermute | solution.py:28
  16.2 1.8 %shard_map.52 = (bf16[368,128]{1,0:T(8,128)(2,1)S(1)}, bf16[368,128]{1,0:T(8,128)(2,1)S(1)}, f32[320,128]{1,0:T(8,128)S(1)}, f32[40,128]{1,0:T(8,128)S(1)}, f32[2,4,24,128]{3,2,1,0:T(8,128)S(1)}) custom-call(bf16[208,128]{1,0:T(8,128)(2,1)S(1)} %collective-permute-done.2.got_b, bf16[208,128]{1,0:T(8,128)(2,1)S(1)} %collective-permute-done.3.got_a, ...), custom_call_target="tpu_custom_call" | custom-call | flops 1000000 | bytes 1781760 | tf_op jit(solution)/shard_map/pallas_call | solution.py:629
  17.9 0.1 collective-permute-start.6
  18.0 2.2 %collective-permute-start.7 = (bf16[368,128]{1,0:T(8,128)(2,1)S(1)}, bf16[368,128]{1,0:T(8,128)(2,1)S(1)}, u32[]{:S(2)}, u32[]{:S(2)}) collective-permute-start(bf16[368,128]{1,0:T(8,128)(2,1)S(1)} %get-tuple-element.48), channel_id=1, source_target_pairs={{2,4},{4,2},{3,5},{5,3},{10,12},{12,10},{11,13},{13,11},{18,20},{2... | collective-permute-start | bytes 282632 | tf_op jit(solution)/shard_map/ppermute | solution.py:36
  20.2 0.6 %shard_map.53 = (f32[4,20,8,128]{3,2,1,0:T(8,128)S(1)}, f32[4,20,24,128]{3,2,1,0:T(8,128)S(1)}, f32[1,192,128]{2,1,0:T(8,128)S(1)}, f32[12,64,128]{2,1,0:T(8,128)S(1)}, f32[3,64,128]{2,1,0:T(8,128)S(1)}) custom-call(f32[320,128]{1,0:T(8,128)S(1)} %get-tuple-element.46.own, f32[40,128]{1,0:T(8,128)S(1)} %get-tuple-element.49.halo, ...), custom_call_target="tpu_custom_call" | custom-call | flops 20000000 | bytes 2232320 | tf_op jit(solution)/shard_map/pallas_call | solution.py:629
  20.8 2.0 %collective-permute-done.6.from_a = bf16[368,128]{1,0:T(8,128)(2,1)S(1)} collective-permute-done((bf16[368,128]{1,0:T(8,128)(2,1)S(1)}, bf16[368,128]{1,0:T(8,128)(2,1)S(1)}, u32[]{:S(2)}, u32[]{:S(2)}) %collective-permute-start.6) | collective-permute-done | bytes 94240 | tf_op jit(solution)/shard_map/ppermute | solution.py:28
  22.8 1.9 %collective-permute-done.7.from_b = bf16[368,128]{1,0:T(8,128)(2,1)S(1)} collective-permute-done((bf16[368,128]{1,0:T(8,128)(2,1)S(1)}, bf16[368,128]{1,0:T(8,128)(2,1)S(1)}, u32[]{:S(2)}, u32[]{:S(2)}) %collective-permute-start.7) | collective-permute-done | bytes 94240 | tf_op jit(solution)/shard_map/ppermute | solution.py:36
  24.7 2.5 %shard_map.54 = f32[320,128]{1,0:T(8,128)} custom-call(f32[320,128]{1,0:T(8,128)S(1)} %get-tuple-element.46.own, bf16[368,128]{1,0:T(8,128)(2,1)S(1)} %collective-permute-done.6.from_a, bf16[368,128]{1,0:T(8,128)(2,1)S(1)} %collective-permute-done.7.from_b, f32[4,20,8,128]{3,2,1,0:T(8,128)S(1)} %get-tuple-element.52.wide, ...), custom_call_target="tpu_custom_call" | custom-call | flops 1000000 | bytes 2416640 | tf_op jit(solution)/shard_map/pallas_call | solution.py:629
  (1 shorter events, 0.0 us)
Async XLA Ops:
  0.0 6.2 %copy-start = (bf16[4,4,8,8,256]{4,3,2,1,0:T(8,128)(2,1)S(1)}, bf16[4,4,8,8,256]{4,3,2,1,0:T(8,128)(2,1)}, u32[]{:S(2)}) copy-start(bf16[4,4,8,8,256]{4,3,2,1,0:T(8,128)(2,1)} %panels.1) | copy-start | bytes 1572868
  1.1 6.7 %collective-permute-start = (bf16[352,128]{1,0:T(8,128)(2,1)S(1)}, bf16[352,128]{1,0:T(8,128)(2,1)S(1)}, u32[]{:S(2)}, u32[]{:S(2)}) collective-permute-start(bf16[352,128]{1,0:T(8,128)(2,1)S(1)} %get-tuple-element.31), channel_id=1, source_target_pairs={{0,2},{2,0},{4,6},{6,4},{1,3},{3,1},{5,7},{7,5},{8,10},{10,8},{12,... | collective-permute-start | bytes 270344 | tf_op jit(solution)/shard_map/ppermute | solution.py:28
  1.6 7.1 %collective-permute-start.1 = (bf16[352,128]{1,0:T(8,128)(2,1)S(1)}, bf16[352,128]{1,0:T(8,128)(2,1)S(1)}, u32[]{:S(2)}, u32[]{:S(2)}) collective-permute-start(bf16[352,128]{1,0:T(8,128)(2,1)S(1)} %get-tuple-element.32), channel_id=1, source_target_pairs={{2,4},{4,2},{3,5},{5,3},{10,12},{12,10},{11,13},{13,11},{18,20},{2... | collective-permute-start | bytes 270344 | tf_op jit(solution)/shard_map/ppermute | solution.py:36
  6.2 0.7 %copy-start.1 = (bf16[4,16,10]{1,0,2:T(4,128)(2,1)S(1)}, bf16[4,16,10]{1,0,2:T(4,128)(2,1)}, u32[]{:S(2)}) copy-start(bf16[4,16,10]{1,0,2:T(4,128)(2,1)} %param.5) | copy-start | bytes 3844
  6.3 8.7 %collective-permute-start.5 = (bf16[4,4,8,8,128]{4,3,2,1,0:T(8,128)(2,1)S(1)}, bf16[4,4,8,8,128]{4,3,2,1,0:T(8,128)(2,1)S(1)}, u32[]{:S(2)}, u32[]{:S(2)}) collective-permute-start(bf16[4,4,8,8,128]{4,3,2,1,0:T(8,128)(2,1)S(1)} %get-tuple-element.34.rest_1_), channel_id=1, source_target_pairs={{0,1},{1,0},{2,3},{3,2},{4,5},{5,4},{6,7},{7,6},{8,9},{9,8},{10,11... | collective-permute-start | bytes 786440 | tf_op jit(solution)/shard_map/ppermute | solution.py:691
  9.0 6.4 %collective-permute-start.2 = (bf16[208,128]{1,0:T(8,128)(2,1)S(1)}, bf16[208,128]{1,0:T(8,128)(2,1)S(1)}, u32[]{:S(2)}, u32[]{:S(2)}) collective-permute-start(bf16[208,128]{1,0:T(8,128)(2,1)S(1)} %get-tuple-element.38), channel_id=1, source_target_pairs={{1,8},{9,16},{17,24},{25,0},{8,1},{16,9},{24,17},{0,25},{3,10},{11... | collective-permute-start | bytes 159752 | tf_op jit(solution)/shard_map/ppermute | solution.py:36
  9.1 7.1 %collective-permute-start.3 = (bf16[208,128]{1,0:T(8,128)(2,1)S(1)}, bf16[208,128]{1,0:T(8,128)(2,1)S(1)}, u32[]{:S(2)}, u32[]{:S(2)}) collective-permute-start(bf16[208,128]{1,0:T(8,128)(2,1)S(1)} %get-tuple-element.39), channel_id=1, source_target_pairs={{0,1},{1,0},{8,9},{9,8},{16,17},{17,16},{24,25},{25,24},{2,3},{3,2... | collective-permute-start | bytes 159752 | tf_op jit(solution)/shard_map/ppermute | solution.py:28
  10.3 5.0 %collective-permute-start.4 = (bf16[64,128]{1,0:T(8,128)(2,1)S(1)}, bf16[64,128]{1,0:T(8,128)(2,1)S(1)}, u32[]{:S(2)}, u32[]{:S(2)}) collective-permute-start(bf16[64,128]{1,0:T(8,128)(2,1)S(1)} %select_bitcast_fusion), channel_id=1, source_target_pairs={{0,8},{8,16},{16,24},{24,0},{1,25},{9,1},{17,9},{25,17},{2,10},{10... | collective-permute-start | bytes 49160 | tf_op jit(solution)/shard_map/ppermute | solution.py:699
  17.9 4.9 %collective-permute-start.6 = (bf16[368,128]{1,0:T(8,128)(2,1)S(1)}, bf16[368,128]{1,0:T(8,128)(2,1)S(1)}, u32[]{:S(2)}, u32[]{:S(2)}) collective-permute-start(bf16[368,128]{1,0:T(8,128)(2,1)S(1)} %get-tuple-element.47), channel_id=1, source_target_pairs={{0,2},{2,0},{4,6},{6,4},{1,3},{3,1},{5,7},{7,5},{8,10},{10,8},{12,... | collective-permute-start | bytes 282632 | tf_op jit(solution)/shard_map/ppermute | solution.py:28
  18.0 6.7 %collective-permute-start.7 = (bf16[368,128]{1,0:T(8,128)(2,1)S(1)}, bf16[368,128]{1,0:T(8,128)(2,1)S(1)}, u32[]{:S(2)}, u32[]{:S(2)}) collective-permute-start(bf16[368,128]{1,0:T(8,128)(2,1)S(1)} %get-tuple-element.48), channel_id=1, source_target_pairs={{2,4},{4,2},{3,5},{5,3},{10,12},{12,10},{11,13},{13,11},{18,20},{2... | collective-permute-start | bytes 282632 | tf_op jit(solution)/shard_map/ppermute | solution.py:36
